TPU v7x, 256 devices: a whole 4x4x8 slice. The times are simulated.
256 devices in a mesh: sec: 4 (over z_lo), head: 8 (over x, z_hi), req: 8 (over y, core).
Axes of the slice: x: 4, y: 4, z: 8 (z_hi: 2, z_lo: 4; z = z_hi * 4 + z_lo), core: 2. Of those that a mesh axis runs over, the one named last changes fastest.
Arguments:
- prompt_x: bfloat16 [4096, 16384], P('req', 'sec'), may hold values from -6 to 6
- w_kv: bfloat16 [16384, 2048], P('sec', 'head'), may hold values from -0.046875 to 0.046875
- queries: bfloat16 [16, 16384], P('req', 'head'), may hold values from -120 to 120
- cache: bfloat16 [16, 4096, 8, 256], P('req', 'sec', 'head'), may hold values from -5 to 5
- w_out: bfloat16 [16384, 16384], P('head', ('sec', 'req')), may hold values from -0.046875 to 0.046875
- blk_owner: int32 [256, 1], replicated, may hold values from 0 to 7; in each aligned block of 8 rows (0 to 7, 8 to 15, ...) at most 2 rows name the same one
- blk_slot: int32 [256], replicated, may hold values from 0 to 1
- blk_len: int32 [256], replicated, may hold values from 1 to 16
- ctx_len: int32 [16], P('req'), may hold values from 2 to 4096
Outputs:
- projected: bfloat16 [16, 16384], P('head', ('sec', 'req'))
Inputs may be any that keep to these rules, and one draw needn't show every extreme that they name: `blk_owner`: in each aligned run of 8 blocks (the blocks of one device) no owner is named more than 2 times, a bound that some block reaches.
All inputs are finite; a program needn't handle non-finite values.
Results may differ from a plain program's by a relative error of at most 0.013.
Values may be sent and summed in bfloat16 or wider, within the bound.
No kernel may reach another device: no remote copies, remote signals or barrier semaphores. Data moves between devices by JAX's collectives and lax.ppermute only.
A program may use at most 64 MiB of HBM per device.

v0:
```python
import math

import jax
import jax.numpy as jnp
from jax import lax
from jax.sharding import PartitionSpec as P

HD = 128
BLK = 16
CAP = 2


masked_score = -1e30


def combined_all(value, axis, join):
    pieces = jax.tree.map(lambda part: lax.all_gather(part, axis), value)
    head = jax.tree.map(lambda part: part[0], pieces)
    tail = jax.tree.map(lambda part: part[1:], pieces)
    so_far, _ = lax.scan(lambda so_far, share: (join(so_far, share), None), head, tail)
    return so_far


def pick_entry(table, first, second):
    inner = lax.dynamic_index_in_dim(table, first, 0, False)
    return lax.dynamic_index_in_dim(inner, second, 0, False)


def earlier_same(owners):
    count = owners.shape[-1]
    same = owners[..., :, None] == owners[..., None, :]
    before = jnp.arange(count)[None, :] < jnp.arange(count)[:, None]
    return jnp.sum((same & before).astype(jnp.int32), axis=-1)


def combine_parts(left, right):
    peak = jnp.maximum(left[0], right[0])
    scale_left = jnp.exp(left[0] - peak)
    scale_right = jnp.exp(right[0] - peak)
    total = left[1] * scale_left + right[1] * scale_right
    summed = left[2] * scale_left[..., None] + right[2] * scale_right[..., None]
    return (peak, total, summed)


def on_device(prompt_x, w_kv, queries, cache, w_out, blk_owner, blk_slot, blk_len, ctx_len):
    sec_count = lax.axis_size("sec")
    req_count = lax.axis_size("req")
    sec_id = lax.axis_index("sec")
    req_id = lax.axis_index("req")
    prompt_rows = prompt_x.shape[0]
    kept_rows = prompt_rows // sec_count
    width = w_kv.shape[1]
    summed = lax.psum_scatter(
        jnp.dot(prompt_x, w_kv, preferred_element_type=jnp.float32),
        "sec",
        scatter_dimension=0,
        tiled=True,
    )
    new_kv = summed.astype(jnp.bfloat16)
    blocks_dev = kept_rows // BLK
    owners = blk_owner[:, 0].reshape(req_count, sec_count, blocks_dev)
    slots = blk_slot.reshape(req_count, sec_count, blocks_dev)
    lengths = blk_len.reshape(req_count, sec_count, blocks_dev)
    my_owner = pick_entry(owners, req_id, sec_id)
    target = my_owner * CAP + earlier_same(my_owner)
    placing = (target[None, :] == jnp.arange(req_count * CAP)[:, None]).astype(jnp.bfloat16)
    outgoing = jnp.dot(
        placing, new_kv.reshape(blocks_dev, BLK * width), preferred_element_type=jnp.float32
    )
    outgoing = outgoing.astype(jnp.bfloat16).reshape(req_count, CAP * BLK, width)
    arrived = lax.all_to_all(outgoing, "req", split_axis=0, concat_axis=0, tiled=True)
    source_owner = lax.dynamic_index_in_dim(owners, sec_id, 1, False)
    source_slot = lax.dynamic_index_in_dim(slots, sec_id, 1, False)
    source_len = lax.dynamic_index_in_dim(lengths, sec_id, 1, False)
    source_rank = earlier_same(source_owner)
    matched = (source_owner == req_id)[:, None, :] & (
        source_rank[:, None, :] == jnp.arange(CAP)[None, :, None]
    )
    present = jnp.any(matched, axis=-1)
    slot_taken = jnp.sum(jnp.where(matched, source_slot[:, None, :], 0), axis=-1)
    len_taken = jnp.sum(jnp.where(matched, source_len[:, None, :], 0), axis=-1)
    token_live = present[:, :, None] & (jnp.arange(BLK)[None, None, :] < len_taken[:, :, None])
    token_owner = jnp.broadcast_to(slot_taken[:, :, None], token_live.shape)
    token_live = token_live.reshape(-1)
    token_owner = token_owner.reshape(-1)
    req_dev = queries.shape[0]
    kv_local = width // (2 * HD)
    group = queries.shape[1] // (kv_local * HD)
    factor = 1.0 / math.sqrt(HD)
    query_heads = queries.reshape(req_dev, kv_local, group, HD)
    arrived = arrived.reshape(-1, kv_local, 2 * HD)
    cached_scores = (
        jnp.einsum(
            "rkgd,rpkd->rkgp", query_heads, cache[..., :HD], preferred_element_type=jnp.float32
        )
        * factor
    )
    prompt_scores = (
        jnp.einsum(
            "rkgd,tkd->rkgt", query_heads, arrived[..., :HD], preferred_element_type=jnp.float32
        )
        * factor
    )
    ctx_dev = cache.shape[1]
    positions = sec_id * ctx_dev + jnp.arange(ctx_dev)
    cached_mask = (positions[None, :] < ctx_len[:, None])[:, None, None, :]
    prompt_mask = (token_live[None, :] & (token_owner[None, :] == jnp.arange(req_dev)[:, None]))[
        :, None, None, :
    ]
    cached_scores = jnp.where(cached_mask, cached_scores, masked_score)
    prompt_scores = jnp.where(prompt_mask, prompt_scores, masked_score)
    peak = jnp.maximum(jnp.max(cached_scores, axis=-1), jnp.max(prompt_scores, axis=-1))
    cached_weights = jnp.where(cached_mask, jnp.exp(cached_scores - peak[..., None]), 0.0)
    prompt_weights = jnp.where(prompt_mask, jnp.exp(prompt_scores - peak[..., None]), 0.0)
    total = jnp.sum(cached_weights, axis=-1) + jnp.sum(prompt_weights, axis=-1)
    weighted = jnp.einsum("rkgp,rpkd->rkgd", cached_weights, cache[..., HD:].astype(jnp.float32))
    weighted = weighted + jnp.einsum(
        "rkgt,tkd->rkgd", prompt_weights, arrived[..., HD:].astype(jnp.float32)
    )
    peak, total, weighted = combined_all((peak, total, weighted), "sec", combine_parts)
    attended = (
        (weighted / total[..., None]).reshape(req_dev, kv_local * group * HD).astype(jnp.bfloat16)
    )
    partial_out = jnp.dot(
        lax.all_gather(attended, "req", axis=0, tiled=True),
        w_out,
        preferred_element_type=jnp.float32,
    )
    return lax.psum_scatter(partial_out, "head", scatter_dimension=0, tiled=True).astype(
        jnp.bfloat16
    )


def solution(mesh):
    return jax.shard_map(
        on_device,
        mesh=mesh,
        in_specs=(
            P("req", "sec"),
            P("sec", "head"),
            P("req", "head"),
            P("req", "sec", "head", None),
            P("head", ("sec", "req")),
            P(),
            P(),
            P(),
            P("req"),
        ),
        out_specs=P("head", ("sec", "req")),
        check_vma=False,
    )
```

profile of v0, /device:TPU:2, one launch (start us, length us, event | category | flops | bytes accessed | tf_op | source)
XLA Modules:
  0.0 159.0 jit_solution(13552078268879430379)
XLA Ops:
  6.5 0.0 copy-start
  6.5 0.0 copy-start.7
  6.5 0.0 copy-start.5
  6.5 0.0 copy-start.3
  6.5 0.0 copy-start.4
  6.5 0.0 copy-start.6
  6.6 0.0 copy-start.2
  6.6 0.0 copy-start.1
  6.6 0.0 reduce-scatter.2.cloned.1.call-start
  6.6 1.5 copy-done
  8.2 4.2 %fusion.31 = f32[512,256]{1,0:T(8,128)} fusion(bf16[512,4096]{1,0:T(8,128)(2,1)} %param.11, bf16[4096,256]{1,0:T(8,128)(2,1)S(1)} %copy-done), kind=kOutput, calls=%fused_computation.73 | convolution fusion | flops 1073741824 | bytes 6815744 | tf_op jit(solution)/shard_map/dot_general | solution.py:54
  12.4 0.0 reduce-scatter.2.cloned.1.call-update
  12.4 0.5 broadcast.88
  13.0 0.0 copy-done.5
  13.0 0.6 reduce.9
  13.6 0.1 reshape_squeeze.3
  13.8 0.0 copy-done.3
  13.8 0.1 reshape.240
  13.9 0.0 copy-done.4
  13.9 0.1 reshape.241
  14.0 0.3 convert_reduce_fusion
  14.3 0.1 fusion.22
  14.4 0.2 select_reduce_fusion
  14.6 0.1 copy.36
  14.7 0.1 copy.35
  14.8 0.1 compare_and_fusion
  14.9 0.1 and.57
  14.9 0.1 copy.37
  15.0 0.1 broadcast_in_dim.100
  15.1 0.1 eq.89
  15.2 0.0 copy-done.7
  15.2 0.6 dynamic-slice.2
  16.5 0.2 convert_reduce_fusion.1
  16.7 0.0 copy-done.6
  16.7 0.1 broadcast_compare_fusion
  16.7 0.0 copy-done.2
  16.7 0.0 copy-done.1
  16.8 0.3 fusion.29
  17.1 25.2 %reduce-scatter.2.cloned.1.call-done = f32[128,256]{1,0:T(8,128)} async-done(((f32[512,256]{1,0:T(8,128)}), f32[128,256]{1,0:T(8,128)}) %reduce-scatter.2.cloned.1.call-update) | async-done | bytes 131088 | tf_op jit(solution)/shard_map/reduce_scatter | solution.py:53
  42.3 0.9 convert_element_type.26
  43.2 0.2 convolution_convert_fusion
  43.4 0.7 reshape.243
  44.1 4.3 %all-to-all-start = ((bf16[8,32,256]{2,1,0:T(8,128)(2,1)}), bf16[8,32,256]{2,1,0:T(8,128)(2,1)S(1)}, u32[]{:S(2)}, u32[]{:S(2)}) async-start(bf16[8,32,256]{2,1,0:T(8,128)(2,1)} %reshape.243), calls=%async_computation.1 | async-start | bytes 262144 | tf_op jit(solution)/shard_map/all_to_all | solution.py:71
  48.4 6.1 %all-to-all-done = bf16[8,32,256]{2,1,0:T(8,128)(2,1)S(1)} async-done(((bf16[8,32,256]{2,1,0:T(8,128)(2,1)}), bf16[8,32,256]{2,1,0:T(8,128)(2,1)S(1)}, u32[]{:S(2)}, u32[]{:S(2)}) %all-to-all-start) | async-done | bytes 131104 | tf_op jit(solution)/shard_map/all_to_all | solution.py:71
  54.6 0.2 fusion.30
  54.8 0.3 convolution_bitcast_fusion.1
  55.0 0.2 fusion.9
  55.2 13.2 %all-gather.2 = f32[8,1,16,128]{3,2,1,0:T(8,128)S(1)} all-gather(f32[2,1,16,128]{3,2,1,0:T(8,128)S(1)} %fusion.9), channel_id=4, replica_groups=mesh['sec'=4,'head'=8,'req'=8] {'sec'}, dimensions={0}, use_global_device_ids=true | all-gather | bytes 81920 | tf_op jit(solution)/shard_map/all_gather | solution.py:17
  68.5 0.2 fusion.15
  68.6 0.2 fusion.10
  68.8 8.0 %all-gather.4 = f32[4,2,16]{2,1,0:T(2,128)S(1)} all-gather(f32[1,2,16]{2,1,0:T(2,128)S(1)} %add_bitcast_fusion), channel_id=3, replica_groups=mesh['sec'=4,'head'=8,'req'=8] {'sec'}, dimensions={0}, use_global_device_ids=true | all-gather | bytes 640 | tf_op jit(solution)/shard_map/all_gather | solution.py:17
  76.8 9.2 %all-gather.3 = f32[4,2,16]{2,1,0:T(2,128)S(1)} all-gather(f32[1,2,16]{2,1,0:T(2,128)S(1)} %bitcast.127), channel_id=2, replica_groups=mesh['sec'=4,'head'=8,'req'=8] {'sec'}, dimensions={0}, use_global_device_ids=true | all-gather | bytes 640 | tf_op jit(solution)/shard_map/all_gather | solution.py:17
  86.0 0.4 while.14
  86.0 0.1 fusion.43
  86.1 0.1 fusion.43
  86.2 0.1 fusion.43
  86.3 0.1 divide_convert_fusion
  86.4 12.7 %all-gather.5 = bf16[8,2,2048]{2,1,0:T(2,128)(2,1)S(1)} all-gather(bf16[1,2,2048]{2,1,0:T(2,128)(2,1)S(1)} %reshape.265), channel_id=1, replica_groups=mesh['sec'=4,'head'=8,'req'=8] {'req'}, dimensions={0}, use_global_device_ids=true | all-gather | bytes 73728 | tf_op jit(solution)/shard_map/all_gather | solution.py:125
  99.2 2.0 %fusion.32 = f32[16,512]{1,0:T(8,128)S(1)} fusion(bf16[16,2048]{1,0:T(8,128)(2,1)S(1)} %reshape.266, bf16[2048,512]{1,0:T(8,128)(2,1)} %param.15), kind=kOutput, calls=%fused_computation.74 | convolution fusion | flops 33554432 | bytes 2195456 | tf_op jit(solution)/shard_map/dot_general | solution.py:124
  101.2 50.4 %all-reduce = bf16[16,512]{1,0:T(8,128)(2,1)S(1)} all-reduce(f32[16,512]{1,0:T(8,128)S(1)} %fusion.32), channel_id=6, replica_groups=mesh['sec'=4,'head'=8,'req'=8] {'head'}, use_global_device_ids=true, to_apply=%region_12.13.clone | all-reduce | flops 8192 | bytes 49152
  151.5 0.6 dynamic-slice_convert_fusion
  (28 shorter events, 0.3 us)
Async XLA Ops:
  6.5 1.6 %copy-start = (bf16[4096,256]{1,0:T(8,128)(2,1)S(1)}, bf16[4096,256]{1,0:T(8,128)(2,1)}, u32[]{:S(2)}) copy-start(bf16[4096,256]{1,0:T(8,128)(2,1)} %param.12) | copy-start | bytes 6291460
  6.5 8.7 %copy-start.7 = (u32[256]{0:T(256)S(1)}, u32[256]{0:T(256)}, u32[]{:S(2)}) copy-start(u32[256]{0:T(256)} %constant.78) | copy-start | bytes 3076
  6.5 6.4 %copy-start.5 = (s32[256,1]{0,1:T(1,128)S(1)}, s32[256,1]{0,1:T(1,128)}, u32[]{:S(2)}) copy-start(s32[256,1]{0,1:T(1,128)} %param.16) | copy-start | bytes 3076
  6.5 7.2 %copy-start.3 = (s32[256]{0:T(256)S(1)}, s32[256]{0:T(256)}, u32[]{:S(2)}) copy-start(s32[256]{0:T(256)} %param.18) | copy-start | bytes 3076
  6.5 7.3 %copy-start.4 = (s32[256]{0:T(256)S(1)}, s32[256]{0:T(256)}, u32[]{:S(2)}) copy-start(s32[256]{0:T(256)} %param.17) | copy-start | bytes 3076
  6.5 10.1 %copy-start.6 = (s32[2]{0:T(128)S(1)}, s32[2]{0:T(128)}, u32[]{:S(2)}) copy-start(s32[2]{0:T(128)} %param.19) | copy-start | bytes 28
  6.6 10.2 %copy-start.2 = (bf16[2,2048]{1,0:T(2,128)(2,1)S(1)}, bf16[2,2048]{1,0:T(2,128)(2,1)}, u32[]{:S(2)}) copy-start(bf16[2,2048]{1,0:T(2,128)(2,1)} %param.13) | copy-start | bytes 24580
  6.6 10.2 %copy-start.1 = (bf16[2,1024,1,256]{3,1,2,0:T(8,128)(2,1)S(1)}, bf16[2,1024,1,256]{3,1,2,0:T(8,128)(2,1)}, u32[]{:S(2)}) copy-start(bf16[2,1024,1,256]{3,1,2,0:T(8,128)(2,1)} %param.14) | copy-start | bytes 3145732
  6.6 35.7 %reduce-scatter.2.cloned.1.call-start = ((), (), s32[]{:S(2)}) async-start(), calls=%async_computation.2 | async-start | bytes 655360 | tf_op jit(solution)/shard_map/reduce_scatter | solution.py:53
  44.1 10.4 %all-to-all-start = ((bf16[8,32,256]{2,1,0:T(8,128)(2,1)}), bf16[8,32,256]{2,1,0:T(8,128)(2,1)S(1)}, u32[]{:S(2)}, u32[]{:S(2)}) async-start(bf16[8,32,256]{2,1,0:T(8,128)(2,1)} %reshape.243), calls=%async_computation.1 | async-start | bytes 262144 | tf_op jit(solution)/shard_map/all_to_all | solution.py:71
Sparse Core Ops, SparseCore 0:
  12.5 29.7 reduce-scatter.1
where the time goes:
time: 162 us; the launch traced here: 159 us
  blocking collectives  93.5 us (58%)
  waiting for transfers between devices  31.4 us (19%)
  between operations  14.2 us (9%)
  matrix products  7.36 us (5%)
  local copies, waits for them, and re-layouts  4.91 us (3%)
  starting transfers between devices  4.34 us (3%)
  other arithmetic  3.3 us (2%)
    unnamed x1, blocking collectives  50.4 us
    all_gather x3, blocking collectives, combined_all(): pieces = jax.tree.map(lambda part: lax.all_gather(part, axis), value)  30.3 us
    reduce_scatter x1, waiting for transfers between devices, on_device(): lax.psum_scatter(jnp.dot(prompt_x, w_kv, preferred_element_type=jnp.float...  25.2 us
    all_gather x1, blocking collectives, on_device(): lax.all_gather(attended, 'req', axis=0, tiled=True)  12.7 us
    all_to_all x1, waiting for transfers between devices, on_device(): lax.all_to_all(outgoing, 'req', split_axis=0, concat_axis=0, tiled=True)  6.13 us
    all_to_all x1, starting transfers between devices, on_device(): lax.all_to_all(outgoing, 'req', split_axis=0, concat_axis=0, tiled=True)  4.3 us
    dot_general x1, matrix products, on_device(): jnp.dot(prompt_x, w_kv, preferred_element_type=jnp.float32)  4.23 us
  transfers between devices with their start and end apart: 2, of which 2 were waited for; matrix products, arithmetic and copies ran while one was open for 2% of the time, Pallas kernels for 0%

commit v1 on v0

v1 whole, which is shorter than its diff:
```python
import math

import jax
import jax.numpy as jnp
from jax import lax
from jax.experimental import pallas as pl
from jax.experimental.pallas import tpu as pltpu
from jax.sharding import PartitionSpec as P

HD = 128
BLK = 16
GROUP = 16
NREQ = 16
LANES = GROUP * NREQ
HALF = LANES // 2
STAT = 16
LOW = -1e30
FACTOR = 1.0 / math.sqrt(HD)
BF = jnp.bfloat16
F32 = jnp.float32


def vmem():
    return pl.BlockSpec(memory_space=pltpu.VMEM)


def smem():
    return pl.BlockSpec(memory_space=pltpu.SMEM)


def dot(a, b, dims):
    return lax.dot_general(a, b, (dims, ((), ())), preferred_element_type=F32)


def rows_of(queries):
    return jnp.concatenate([queries[:, h * HD : (h + 1) * HD] for h in range(GROUP)], axis=0)


def stat_rows(peak, total, rows):
    place = lax.broadcasted_iota(jnp.int32, (rows, peak.shape[1]), 0)
    return jnp.where(place == 0, peak, jnp.where(place == 1, total, 0.0))


def packed_stats(peak, total):
    hi = peak.astype(BF).astype(F32)
    rest = peak - hi
    mid = rest.astype(BF).astype(F32)
    low = rest - mid
    total_hi = total.astype(BF).astype(F32)
    total_low = total - total_hi
    place = lax.broadcasted_iota(jnp.int32, (STAT, peak.shape[1]), 0)
    packed = jnp.zeros((STAT, peak.shape[1]), F32)
    for row, part in enumerate((hi, mid, low, total_hi, total_low)):
        packed = jnp.where(place == row, part, packed)
    return packed.astype(BF)


def unpacked_stats(packed):
    rows = packed.astype(F32)
    peak = rows[0:1] + (rows[1:2] + rows[2:3])
    total = rows[3:4] + rows[4:5]
    return peak, total


def store_packed(ref, weighted, peak, total):
    ref[0:HD, :] = weighted.astype(BF)
    ref[HD : HD + STAT, :] = packed_stats(peak, total)


def cached_kernel(meta, q_ref, cache_ref, weighted_ref, stats_ref):
    queries = rows_of(q_ref[...])
    count = cache_ref.shape[1]
    lane = lax.broadcasted_iota(jnp.int32, (count, LANES), 1) % NREQ
    position = lax.broadcasted_iota(jnp.int32, (count, LANES), 0) + meta[18]
    first = meta[16] * 2
    live0 = (lane == first) & (position < meta[19])
    live1 = (lane == first + 1) & (position < meta[20])
    live = live0 | live1
    scores0 = dot(cache_ref[0, :, 0:HD], queries, ((1,), (1,)))
    scores1 = dot(cache_ref[1, :, 0:HD], queries, ((1,), (1,)))
    scores = jnp.where(live, jnp.where(lane == first, scores0, scores1) * FACTOR, LOW)
    peak = jnp.max(scores, axis=0, keepdims=True)
    weights = jnp.where(live, jnp.exp(scores - peak), 0.0)
    total = jnp.sum(weights, axis=0, keepdims=True)
    weights = weights.astype(BF)
    zero = jnp.zeros_like(weights)
    weighted_ref[...] = dot(
        cache_ref[0, :, HD : 2 * HD], jnp.where(live0, weights, zero), ((0,), (0,))
    ) + dot(cache_ref[1, :, HD : 2 * HD], jnp.where(live1, weights, zero), ((0,), (0,)))
    stats_ref[...] = stat_rows(peak, total, 8)


def prompt_kernel(
    meta, q_ref, perm_ref, own_ref, a_ref, b_ref, c_ref, cw_ref, cs_ref, kw_ref, ks_ref, send_ref
):
    summed = (own_ref[...].astype(F32) + a_ref[...].astype(F32)) + (
        b_ref[...].astype(F32) + c_ref[...].astype(F32)
    )
    new_kv = summed.astype(BF)
    ordered = dot(perm_ref[...], q_ref[...], ((1,), (0,))).astype(BF)
    queries = rows_of(ordered)
    scores = dot(new_kv[:, 0:HD], queries, ((1,), (1,))) * FACTOR
    tokens = new_kv.shape[0]
    lane = lax.broadcasted_iota(jnp.int32, (BLK, LANES), 1) % NREQ
    place = lax.broadcasted_iota(jnp.int32, (BLK, LANES), 0)
    pieces = []
    for block in range(tokens // BLK):
        live = (lane == meta[block]) & (place < meta[8 + block])
        pieces.append(jnp.where(live, scores[block * BLK : (block + 1) * BLK], LOW))
    scores = jnp.concatenate(pieces, axis=0)
    peak = jnp.max(scores, axis=0, keepdims=True)
    weights = jnp.where(scores > 0.5 * LOW, jnp.exp(scores - peak), 0.0)
    total = jnp.sum(weights, axis=0, keepdims=True)
    weighted = dot(new_kv[:, HD : 2 * HD], weights.astype(BF), ((0,), (0,)))
    cached_peak, cached_total = cs_ref[0:1, :], cs_ref[1:2, :]
    joint = jnp.maximum(peak, cached_peak)
    scale, cached_scale = jnp.exp(peak - joint), jnp.exp(cached_peak - joint)
    weighted = weighted * scale + cw_ref[...] * cached_scale
    total = total * scale + cached_total * cached_scale
    core = meta[17]

    @pl.when(core == 0)
    def _():
        kw_ref[...] = weighted[:, :HALF]
        ks_ref[...] = stat_rows(joint[:, :HALF], total[:, :HALF], 8)
        store_packed(send_ref, weighted[:, HALF:], joint[:, HALF:], total[:, HALF:])

    @pl.when(core == 1)
    def _():
        kw_ref[...] = weighted[:, HALF:]
        ks_ref[...] = stat_rows(joint[:, HALF:], total[:, HALF:], 8)
        store_packed(send_ref, weighted[:, :HALF], joint[:, :HALF], total[:, :HALF])


def joined(w_ref, s_ref, got_ref):
    peak, total = s_ref[0:1, :], s_ref[1:2, :]
    got_peak, got_total = unpacked_stats(got_ref[HD : HD + STAT, :])
    joint = jnp.maximum(peak, got_peak)
    scale, got_scale = jnp.exp(peak - joint), jnp.exp(got_peak - joint)
    weighted = w_ref[...] * scale + got_ref[0:HD, :].astype(F32) * got_scale
    return weighted, joint, total * scale + got_total * got_scale


def join_kernel(w_ref, s_ref, got_ref, kw_ref, ks_ref, send_ref):
    weighted, peak, total = joined(w_ref, s_ref, got_ref)
    kw_ref[...] = weighted
    ks_ref[...] = stat_rows(peak, total, 8)
    store_packed(send_ref, weighted, peak, total)


def last_kernel(w_ref, s_ref, got_ref, out_ref):
    weighted, peak, total = joined(w_ref, s_ref, got_ref)
    rows = (weighted / total).T
    for h in range(GROUP // 2):
        out_ref[:, h * HD : (h + 1) * HD] = rows[h * NREQ : (h + 1) * NREQ, :].astype(BF)


def shape(dims, dtype):
    return jax.ShapeDtypeStruct(dims, dtype)


def call(kernel, ins, outs, name, flops=0):
    moved = 0
    for _, value in ins:
        moved += value.size * value.dtype.itemsize
    return pl.pallas_call(
        kernel,
        out_shape=outs,
        in_specs=[spec for spec, _ in ins],
        out_specs=jax.tree.map(lambda _: vmem(), outs),
        compiler_params=pltpu.CompilerParams(vmem_limit_bytes=32 * 1024 * 1024),
        cost_estimate=pl.CostEstimate(flops=flops, bytes_accessed=moved, transcendentals=0),
        name=name,
    )(*[value for _, value in ins])


def joined_call(state, got, name):
    return call(
        join_kernel,
        [(vmem(), state[0]), (vmem(), state[1]), (vmem(), got)],
        (shape((HD, HALF), F32), shape((8, HALF), F32), shape((HD + STAT, HALF), BF)),
        name,
    )


def on_device(prompt_x, w_kv, queries, cache, w_out, blk_owner, blk_slot, blk_len, ctx_len):
    sec_count = lax.axis_size("sec")
    req_count = lax.axis_size("req")
    sec_id = lax.axis_index("sec")
    req_id = lax.axis_index("req")
    core = req_id % 2
    y_id = req_id // 2
    rows = prompt_x.shape[0] // sec_count

    def over_sec(value, flip):
        return lax.ppermute(value, "sec", [(i, i ^ flip) for i in range(sec_count)])

    def over_req(value, flip):
        return lax.ppermute(value, "req", [(i, i ^ flip) for i in range(req_count)])

    base = (req_id * sec_count + sec_id) * (rows // BLK)
    count = rows // BLK
    owner = lax.dynamic_slice(blk_owner, (base, 0), (count, 1))[:, 0]
    slot = lax.dynamic_slice(blk_slot, (base,), (count,))
    length = lax.dynamic_slice(blk_len, (base,), (count,))
    ids = jnp.stack([req_id, core, sec_id * cache.shape[1]]).astype(jnp.int32)
    meta = jnp.concatenate([owner * 2 + slot, length, ids, ctx_len]).astype(jnp.int32)

    gathered = queries
    for flip in (1, 2, 6):
        gathered = jnp.concatenate([gathered, over_req(gathered, flip)], axis=0)
    place = jnp.arange(NREQ, dtype=jnp.int32)
    member = place // 2
    holder = req_id ^ (member % 2) ^ ((member // 2) % 2 * 2) ^ (member // 4 * 6)
    perm = (holder[None, :] * 2 + place[None, :] % 2 == place[:, None]).astype(BF)

    part = jnp.dot(prompt_x, w_kv, preferred_element_type=F32).astype(BF)
    chunks = part.reshape(sec_count, rows, part.shape[1])

    def chunk(index):
        return lax.dynamic_index_in_dim(chunks, index, 0, False)

    arrived = [over_sec(chunk(sec_id ^ flip), flip) for flip in (3, 2, 1)]

    cached = call(
        cached_kernel,
        [
            (smem(), meta),
            (vmem(), jnp.tile(queries, (NREQ // 2, 1))),
            (vmem(), cache[:, :, 0, :]),
        ],
        (shape((HD, LANES), F32), shape((8, LANES), F32)),
        "cached",
        flops=2 * 4 * cache.shape[1] * HD * LANES,
    )
    state = call(
        prompt_kernel,
        [
            (smem(), meta),
            (vmem(), gathered),
            (vmem(), perm),
            (vmem(), chunk(sec_id)),
            (vmem(), arrived[0]),
            (vmem(), arrived[1]),
            (vmem(), arrived[2]),
            (vmem(), cached[0]),
            (vmem(), cached[1]),
        ],
        (shape((HD, HALF), F32), shape((8, HALF), F32), shape((HD + STAT, HALF), BF)),
        "prompt",
        flops=2 * 2 * rows * HD * LANES,
    )
    state = joined_call(state, over_req(state[2], 1), "join_core")
    state = joined_call(state, over_sec(state[2], 1), "join_sec1")
    state = joined_call(state, over_sec(state[2], 2), "join_sec2")
    state = joined_call(state, over_req(state[2], 2), "join_y1")
    got = over_req(state[2], 6)
    mine = call(
        last_kernel,
        [(vmem(), state[0]), (vmem(), state[1]), (vmem(), got)],
        shape((NREQ, HALF // NREQ * HD), BF),
        "join_y2",
    )
    other = over_req(mine, 1)
    attended = jnp.concatenate(
        [jnp.where(core == 0, mine, other), jnp.where(core == 0, other, mine)], axis=1
    )
    partial_out = jnp.dot(attended, w_out, preferred_element_type=F32).astype(BF)
    head_count = lax.axis_size("head")
    pieces = partial_out.reshape(head_count, NREQ // head_count, partial_out.shape[1])
    pieces = lax.all_to_all(pieces, "head", 0, 0, tiled=True)
    return jnp.sum(pieces.astype(F32), axis=0).astype(BF)


def solution(mesh):
    return jax.shard_map(
        on_device,
        mesh=mesh,
        in_specs=(
            P("req", "sec"),
            P("sec", "head"),
            P("req", "head"),
            P("req", "sec", "head", None),
            P("head", ("sec", "req")),
            P(),
            P(),
            P(),
            P("req"),
        ),
        out_specs=P("head", ("sec", "req")),
        check_vma=False,
    )
```

time: 162 us -> 69.9 us (0.43); the launches traced: 159 us -> 68.9 us
  blocking collectives: 93.5 us -> 19.1 us
  between operations: 14.2 us -> 0.21 us
  waiting for transfers between devices: 31.4 us -> 18.3 us
  starting transfers between devices: 4.34 us -> 14.6 us
  Pallas kernels: 0 us -> 3.37 us
  matrix products: 7.36 us -> 5.49 us
    unnamed x1 -> x0, blocking collectives: 50.4 us -> none
    all_gather x4 -> x0, blocking collectives: 43.1 us -> none  [the longest x3 30.3 us: combined_all(): pieces = jax.tree.map(lambda part: lax.all_gather(part, axis), value)]
    reduce_scatter x1 -> x0, waiting for transfers between devices: 25.2 us -> none  [on_device(): lax.psum_scatter(jnp.dot(prompt_x, w_kv, preferred_element_type=jnp.float...]
    all_to_all x0 -> x1, blocking collectives: none -> 19.1 us  [on_device(): pieces = lax.all_to_all(pieces, 'head', 0, 0, tiled=True)]
    ppermute x0 -> x12, waiting for transfers between devices: none -> 18.3 us  [the longest x7 13.3 us: over_req(): return lax.ppermute(value, 'req', [(i, i ^ flip) for i in range(req_count)])]
    ppermute x0 -> x12, starting transfers between devices: none -> 14.6 us  [the longest x5 9.2 us: over_sec(): return lax.ppermute(value, 'sec', [(i, i ^ flip) for i in range(sec_count)])]
    all_to_all x1 -> x0, waiting for transfers between devices: 6.13 us -> none  [on_device(): lax.all_to_all(outgoing, 'req', split_axis=0, concat_axis=0, tiled=True)]
    all_to_all x1 -> x0, starting transfers between devices: 4.3 us -> none  [on_device(): lax.all_to_all(outgoing, 'req', split_axis=0, concat_axis=0, tiled=True)]
  transfers between devices with their start and end apart: 2 -> 12, of which waited for: 2 -> 7; matrix products, arithmetic and copies ran while one was open for 2% -> 13% of each run, Pallas kernels for 0% -> 3%
where the time goes in v1:
time: 69.9 us; the launch traced here: 68.9 us
  blocking collectives  19.1 us (27%)
  waiting for transfers between devices  18.3 us (26%)
  starting transfers between devices  14.6 us (21%)
  matrix products  5.49 us (8%)
  local copies, waits for them, and re-layouts  4.38 us (6%)
  other arithmetic  3.45 us (5%)
  Pallas kernels  3.37 us (5%)
    all_to_all x1, blocking collectives, on_device(): pieces = lax.all_to_all(pieces, 'head', 0, 0, tiled=True)  19.1 us
    ppermute x7, waiting for transfers between devices, over_req(): return lax.ppermute(value, 'req', [(i, i ^ flip) for i in range(req_count)])  13.3 us
    ppermute x5, starting transfers between devices, over_sec(): return lax.ppermute(value, 'sec', [(i, i ^ flip) for i in range(sec_count)])  9.2 us
    ppermute x7, starting transfers between devices, over_req(): return lax.ppermute(value, 'req', [(i, i ^ flip) for i in range(req_count)])  5.4 us
    ppermute x5, waiting for transfers between devices, over_sec(): return lax.ppermute(value, 'sec', [(i, i ^ flip) for i in range(sec_count)])  4.99 us
    dot_general x1, matrix products, on_device(): part = jnp.dot(prompt_x, w_kv, preferred_element_type=F32).astype(BF)  3.52 us
    pallas_call x7, Pallas kernels, call(): pl.pallas_call(kernel, out_shape=outs, in_specs=[spec for spec, _ in ins]...  3.37 us
    dot_general x1, matrix products, on_device(): jnp.dot(attended, w_out, preferred_element_type=F32).astype(BF)  1.96 us
  transfers between devices with their start and end apart: 12, of which 7 were waited for; matrix products, arithmetic and copies ran while one was open for 13% of the time, Pallas kernels for 3%

profile of v1, /device:TPU:2, one launch (start us, length us, event | category | flops | bytes accessed | tf_op | source)
XLA Modules:
  0.0 68.9 jit_solution(9951529274415796225)
XLA Ops:
  0.0 0.0 copy-start
  0.0 0.0 collective-permute-start
  0.0 1.6 %copy-done = bf16[4096,256]{1,0:T(8,128)(2,1)S(1)} copy-done((bf16[4096,256]{1,0:T(8,128)(2,1)S(1)}, bf16[4096,256]{1,0:T(8,128)(2,1)}, u32[]{:S(2)}) %copy-start) | copy-done | bytes 2097176
  1.6 0.0 copy-start.2
  1.6 0.0 copy-start.1
  1.6 3.5 %convolution_convert_fusion = bf16[512,256]{1,0:T(8,128)(2,1)S(1)} fusion(bf16[512,4096]{1,0:T(8,128)(2,1)} %param.9, bf16[4096,256]{1,0:T(8,128)(2,1)S(1)} %copy-done), kind=kOutput, calls=%fused_computation | convolution fusion | flops 1073872896 | bytes 6553600 | tf_op jit(solution)/shard_map/dot_general | solution.py:217
  5.1 0.7 dynamic-slice_bitcast_fusion
  5.8 4.6 %collective-permute-start.3 = (bf16[128,256]{1,0:T(8,128)(2,1)}, bf16[128,256]{1,0:T(8,128)(2,1)S(1)}, u32[]{:S(2)}, u32[]{:S(2)}) collective-permute-start(bf16[128,256]{1,0:T(8,128)(2,1)} %get-tuple-element.41), channel_id=1, source_target_pairs={{0,192},{64,128},{128,64},{192,0},{1,193},{65,129},{129,65},{193,1... | collective-permute-start | bytes 196616 | tf_op jit(solution)/shard_map/ppermute | solution.py:196
  10.5 0.0 collective-permute-start.4
  10.5 0.6 collective-permute-start.5
  11.0 0.0 collective-permute-done
  11.0 0.0 copy-done.2
  11.1 0.0 copy-start.3
  11.1 1.7 %collective-permute-start.1 = (bf16[4,2048]{1,0:T(4,128)(2,1)S(1)}, bf16[4,2048]{1,0:T(4,128)(2,1)S(1)}, u32[]{:S(2)}, u32[]{:S(2)}) collective-permute-start(bf16[4,2048]{1,0:T(4,128)(2,1)S(1)} %pad_maximum_fusion.2), channel_id=1, source_target_pairs={{0,2},{1,3},{2,0},{3,1},{4,6},{5,7},{6,4},{7,5},{8,10},{9,11},{10,... | collective-permute-start | bytes 49160 | tf_op jit(solution)/shard_map/ppermute | solution.py:199
  12.8 2.2 %collective-permute-done.1 = bf16[4,2048]{1,0:T(4,128)(2,1)S(1)} collective-permute-done((bf16[4,2048]{1,0:T(4,128)(2,1)S(1)}, bf16[4,2048]{1,0:T(4,128)(2,1)S(1)}, u32[]{:S(2)}, u32[]{:S(2)}) %collective-permute-start.1) | collective-permute-done | bytes 16416 | tf_op jit(solution)/shard_map/ppermute | solution.py:199
  14.9 0.0 copy-start.4
  14.9 0.6 pad_maximum_fusion.1
  15.6 3.0 %collective-permute-start.2 = (bf16[8,2048]{1,0:T(8,128)(2,1)}, bf16[8,2048]{1,0:T(8,128)(2,1)}, u32[]{:S(2)}, u32[]{:S(2)}) collective-permute-start(bf16[8,2048]{1,0:T(8,128)(2,1)} %pad_maximum_fusion.1), channel_id=1, source_target_pairs={{0,6},{1,7},{2,4},{3,5},{4,2},{5,3},{6,0},{7,1},{8,14},{9,15},{10,... | collective-permute-start | bytes 98312 | tf_op jit(solution)/shard_map/ppermute | solution.py:199
  18.6 1.3 %fusion.7 = s32[8]{0:T(128)} fusion(s32[256,1]{0,1:T(1,128)} %param.14, s32[]{:T(128)S(6)} %select_n.95, s32[256]{0:T(256)} %param.15), kind=kLoop, calls=%fused_computation.36 | loop fusion | flops 16 | bytes 100 | tf_op jit(solution)/shard_map/add | solution.py:207
  19.9 1.3 %dynamic_slice.24 = s32[8]{0:T(128)} dynamic-slice(s32[256]{0:T(256)} %param.16, s32[]{:T(128)S(6)} %select_n.95), dynamic_slice_sizes={8} | dynamic-slice | bytes 68 | tf_op jit(solution)/shard_map/dynamic_slice | solution.py:205
  21.2 0.0 copy-done.3
  21.2 0.0 copy-done.4
  21.3 0.7 %concatenate.17.meta = s32[21]{0:T(128)S(1)} concatenate(s32[8]{0:T(128)} %fusion.7, s32[8]{0:T(128)} %dynamic_slice.24, s32[1]{0:T(128)} %bitcast.1, s32[1]{0:T(128)} %bitcast.2, s32[1]{0:T(128)} %bitcast.3, s32[2]{0:T(128)} %param.17), dimensions={0} | concatenate | bytes 168 | tf_op jit(solution)/shard_map/concatenate | solution.py:207
  22.0 0.0 copy-done.1
  22.0 2.1 %cached.1 = (f32[128,256]{1,0:T(8,128)S(1)}, f32[8,256]{1,0:T(8,128)S(1)}) custom-call(s32[21]{0:T(128)S(1)} %concatenate.17.meta, bf16[16,2048]{1,0:T(8,128)(2,1)S(1)} %tile.10.q_ref, bf16[2,1024,256]{2,1,0:T(8,128)(2,1)S(1)} %bitcast.20), custom_call_target="tpu_custom_call" | custom-call | flops 268435456 | bytes 1114196 | tf_op jit(solution)/shard_map/cached/pallas_call | solution.py:166
  24.1 0.0 collective-permute-done.2
  24.1 0.8 %pad_maximum_fusion.q_ref = bf16[16,2048]{1,0:T(8,128)(2,1)S(1)} fusion(bf16[8,2048]{1,0:T(8,128)(2,1)} %collective-permute-done.2, bf16[4,2048]{1,0:T(4,128)(2,1)} %copy-done.4, bf16[2,2048]{1,0:T(2,128)(2,1)} %copy-done.3, bf16[2,2048]{1,0:T(2,128)(2,1)S(1)} %copy-done.2), kind=kLoop, calls=%fused_computation.2 | loop fusion | flops 262144 | bytes 131072 | tf_op jit(solution)/shard_map/concatenate | solution.py:211
  24.9 0.0 collective-permute-done.3.a_ref
  24.9 0.0 collective-permute-done.4.b_ref
  24.9 0.0 collective-permute-done.5.c_ref
  25.0 1.1 %prompt.1 = (f32[128,128]{1,0:T(8,128)S(1)}, f32[8,128]{1,0:T(8,128)S(1)}, bf16[144,128]{1,0:T(8,128)(2,1)S(1)}) custom-call(s32[21]{0:T(128)S(1)} %concatenate.17.meta, bf16[16,2048]{1,0:T(8,128)(2,1)S(1)} %pad_maximum_fusion.q_ref, bf16[16,16]{1,0:T(8,128)(2,1)S(1)} %fusion.3.perm_ref, bf16[128,256]{1,0:T(8,128)(2,1)S(1)} %get-tuple-element.42.own_ref, ...), custom_call_target="tpu_custom_call" | custom-call | flops 16777216 | bytes 467540 | tf_op jit(solution)/shard_map/prompt/pallas_call | solution.py:166
  26.0 0.1 collective-permute-start.6
  26.1 1.2 %collective-permute-done.6.got_ref = bf16[144,128]{1,0:T(8,128)(2,1)S(1)} collective-permute-done((bf16[144,128]{1,0:T(8,128)(2,1)S(1)}, bf16[144,128]{1,0:T(8,128)(2,1)S(1)}, u32[]{:S(2)}, u32[]{:S(2)}) %collective-permute-start.6) | collective-permute-done | bytes 36896 | tf_op jit(solution)/shard_map/ppermute | solution.py:199
  27.4 1.6 %collective-permute-start.7 = (bf16[144,128]{1,0:T(8,128)(2,1)S(1)}, bf16[144,128]{1,0:T(8,128)(2,1)S(1)}, u32[]{:S(2)}, u32[]{:S(2)}) collective-permute-start(bf16[144,128]{1,0:T(8,128)(2,1)S(1)} %get-tuple-element.29), channel_id=1, source_target_pairs={{0,64},{64,0},{128,192},{192,128},{1,65},{65,1},{129,193},{193,129... | collective-permute-start | bytes 110600 | tf_op jit(solution)/shard_map/ppermute | solution.py:196
  28.9 2.5 %collective-permute-done.7.got_ref = bf16[144,128]{1,0:T(8,128)(2,1)S(1)} collective-permute-done((bf16[144,128]{1,0:T(8,128)(2,1)S(1)}, bf16[144,128]{1,0:T(8,128)(2,1)S(1)}, u32[]{:S(2)}, u32[]{:S(2)}) %collective-permute-start.7) | collective-permute-done | bytes 36896 | tf_op jit(solution)/shard_map/ppermute | solution.py:196
  31.4 2.5 %collective-permute-start.8 = (bf16[144,128]{1,0:T(8,128)(2,1)S(1)}, bf16[144,128]{1,0:T(8,128)(2,1)S(1)}, u32[]{:S(2)}, u32[]{:S(2)}) collective-permute-start(bf16[144,128]{1,0:T(8,128)(2,1)S(1)} %get-tuple-element.32), channel_id=1, source_target_pairs={{0,128},{64,192},{128,0},{192,64},{1,129},{65,193},{129,1},{193,65... | collective-permute-start | bytes 110600 | tf_op jit(solution)/shard_map/ppermute | solution.py:196
  33.9 2.5 %collective-permute-done.8.got_ref = bf16[144,128]{1,0:T(8,128)(2,1)S(1)} collective-permute-done((bf16[144,128]{1,0:T(8,128)(2,1)S(1)}, bf16[144,128]{1,0:T(8,128)(2,1)S(1)}, u32[]{:S(2)}, u32[]{:S(2)}) %collective-permute-start.8) | collective-permute-done | bytes 36896 | tf_op jit(solution)/shard_map/ppermute | solution.py:196
  36.4 0.2 collective-permute-start.9
  36.7 3.8 %collective-permute-done.9.got_ref = bf16[144,128]{1,0:T(8,128)(2,1)S(1)} collective-permute-done((bf16[144,128]{1,0:T(8,128)(2,1)S(1)}, bf16[144,128]{1,0:T(8,128)(2,1)S(1)}, u32[]{:S(2)}, u32[]{:S(2)}) %collective-permute-start.9) | collective-permute-done | bytes 36896 | tf_op jit(solution)/shard_map/ppermute | solution.py:199
  40.5 0.3 collective-permute-start.10
  40.8 4.9 %collective-permute-done.10.got_ref = bf16[144,128]{1,0:T(8,128)(2,1)S(1)} collective-permute-done((bf16[144,128]{1,0:T(8,128)(2,1)S(1)}, bf16[144,128]{1,0:T(8,128)(2,1)S(1)}, u32[]{:S(2)}, u32[]{:S(2)}) %collective-permute-start.10) | collective-permute-done | bytes 36896 | tf_op jit(solution)/shard_map/ppermute | solution.py:199
  45.8 0.1 join_y2.1
  45.9 0.1 collective-permute-start.11
  46.0 1.2 %collective-permute-done.11 = bf16[16,1024]{1,0:T(8,128)(2,1)S(1)} collective-permute-done((bf16[16,1024]{1,0:T(8,128)(2,1)S(1)}, bf16[16,1024]{1,0:T(8,128)(2,1)S(1)}, u32[]{:S(2)}, u32[]{:S(2)}) %collective-permute-start.11) | collective-permute-done | bytes 32800 | tf_op jit(solution)/shard_map/ppermute | solution.py:199
  47.2 2.0 %convolution_convert_fusion.1 = bf16[16,512]{1,0:T(8,128)(2,1)S(1)} fusion(bf16[2048,512]{1,0:T(8,128)(2,1)} %param.13, bf16[16,1024]{1,0:T(8,128)(2,1)S(1)} %get-tuple-element.44, bf16[16,1024]{1,0:T(8,128)(2,1)S(1)} %get-tuple-element.43), kind=kOutput, calls=%fused_computation.1 | convolution fusion | flops 33693696 | bytes 2179072 | tf_op jit(solution)/shard_map/dot_general | solution.py:268
  49.2 19.1 %all_to_all.5 = bf16[8,2,512]{2,1,0:T(2,128)(2,1)S(1)} all-to-all(bf16[8,2,512]{2,1,0:T(2,128)(2,1)S(1)} %reshape.97), channel_id=1, replica_groups=mesh['sec'=4,'head'=8,'req'=8] {'head'}, dimensions={0} | all-to-all | bytes 32768 | tf_op jit(solution)/shard_map/all_to_all | solution.py:271
  68.3 0.6 reduce_sum.12
  (11 shorter events, 0.3 us)
Async XLA Ops:
  0.0 1.6 %copy-start = (bf16[4096,256]{1,0:T(8,128)(2,1)S(1)}, bf16[4096,256]{1,0:T(8,128)(2,1)}, u32[]{:S(2)}) copy-start(bf16[4096,256]{1,0:T(8,128)(2,1)} %param.10) | copy-start | bytes 6291460
  0.0 11.0 %collective-permute-start = (bf16[2,2048]{1,0:T(2,128)(2,1)}, bf16[2,2048]{1,0:T(2,128)(2,1)S(1)}, u32[]{:S(2)}, u32[]{:S(2)}) collective-permute-start(bf16[2,2048]{1,0:T(2,128)(2,1)} %param.11), channel_id=1, source_target_pairs={{0,1},{1,0},{2,3},{3,2},{4,5},{5,4},{6,7},{7,6},{8,9},{9,8},{10,11... | collective-permute-start | bytes 24584 | tf_op jit(solution)/shard_map/ppermute | solution.py:199
  1.6 9.5 %copy-start.2 = (bf16[2,2048]{1,0:T(2,128)(2,1)S(1)}, bf16[2,2048]{1,0:T(2,128)(2,1)}, u32[]{:S(2)}) copy-start(bf16[2,2048]{1,0:T(2,128)(2,1)} %param.11) | copy-start | bytes 24580
  1.6 20.4 %copy-start.1 = (bf16[2,1024,1,256]{3,1,2,0:T(8,128)(2,1)S(1)}, bf16[2,1024,1,256]{3,1,2,0:T(8,128)(2,1)}, u32[]{:S(2)}) copy-start(bf16[2,1024,1,256]{3,1,2,0:T(8,128)(2,1)} %param.12) | copy-start | bytes 3145732
  5.8 19.1 %collective-permute-start.3 = (bf16[128,256]{1,0:T(8,128)(2,1)}, bf16[128,256]{1,0:T(8,128)(2,1)S(1)}, u32[]{:S(2)}, u32[]{:S(2)}) collective-permute-start(bf16[128,256]{1,0:T(8,128)(2,1)} %get-tuple-element.41), channel_id=1, source_target_pairs={{0,192},{64,128},{128,64},{192,0},{1,193},{65,129},{129,65},{193,1... | collective-permute-start | bytes 196616 | tf_op jit(solution)/shard_map/ppermute | solution.py:196
  10.5 14.5 %collective-permute-start.4 = (bf16[128,256]{1,0:T(8,128)(2,1)}, bf16[128,256]{1,0:T(8,128)(2,1)S(1)}, u32[]{:S(2)}, u32[]{:S(2)}) collective-permute-start(bf16[128,256]{1,0:T(8,128)(2,1)} %get-tuple-element.40), channel_id=1, source_target_pairs={{0,128},{64,192},{128,0},{192,64},{1,129},{65,193},{129,1},{193,65... | collective-permute-start | bytes 196616 | tf_op jit(solution)/shard_map/ppermute | solution.py:196
  10.5 14.5 %collective-permute-start.5 = (bf16[128,256]{1,0:T(8,128)(2,1)}, bf16[128,256]{1,0:T(8,128)(2,1)S(1)}, u32[]{:S(2)}, u32[]{:S(2)}) collective-permute-start(bf16[128,256]{1,0:T(8,128)(2,1)} %get-tuple-element.39), channel_id=1, source_target_pairs={{0,64},{64,0},{128,192},{192,128},{1,65},{65,1},{129,193},{193,129... | collective-permute-start | bytes 196616 | tf_op jit(solution)/shard_map/ppermute | solution.py:196
  11.1 10.1 %copy-start.3 = (bf16[2,2048]{1,0:T(2,128)(2,1)}, bf16[2,2048]{1,0:T(2,128)(2,1)S(1)}, u32[]{:S(2)}) copy-start(bf16[2,2048]{1,0:T(2,128)(2,1)S(1)} %collective-permute-done) | copy-start | bytes 24580
  11.1 3.8 %collective-permute-start.1 = (bf16[4,2048]{1,0:T(4,128)(2,1)S(1)}, bf16[4,2048]{1,0:T(4,128)(2,1)S(1)}, u32[]{:S(2)}, u32[]{:S(2)}) collective-permute-start(bf16[4,2048]{1,0:T(4,128)(2,1)S(1)} %pad_maximum_fusion.2), channel_id=1, source_target_pairs={{0,2},{1,3},{2,0},{3,1},{4,6},{5,7},{6,4},{7,5},{8,10},{9,11},{10,... | collective-permute-start | bytes 49160 | tf_op jit(solution)/shard_map/ppermute | solution.py:199
  14.9 6.2 %copy-start.4 = (bf16[4,2048]{1,0:T(4,128)(2,1)}, bf16[4,2048]{1,0:T(4,128)(2,1)S(1)}, u32[]{:S(2)}) copy-start(bf16[4,2048]{1,0:T(4,128)(2,1)S(1)} %collective-permute-done.1) | copy-start | bytes 49156
  15.6 8.5 %collective-permute-start.2 = (bf16[8,2048]{1,0:T(8,128)(2,1)}, bf16[8,2048]{1,0:T(8,128)(2,1)}, u32[]{:S(2)}, u32[]{:S(2)}) collective-permute-start(bf16[8,2048]{1,0:T(8,128)(2,1)} %pad_maximum_fusion.1), channel_id=1, source_target_pairs={{0,6},{1,7},{2,4},{3,5},{4,2},{5,3},{6,0},{7,1},{8,14},{9,15},{10,... | collective-permute-start | bytes 98312 | tf_op jit(solution)/shard_map/ppermute | solution.py:199
  26.0 1.3 %collective-permute-start.6 = (bf16[144,128]{1,0:T(8,128)(2,1)S(1)}, bf16[144,128]{1,0:T(8,128)(2,1)S(1)}, u32[]{:S(2)}, u32[]{:S(2)}) collective-permute-start(bf16[144,128]{1,0:T(8,128)(2,1)S(1)} %get-tuple-element.26), channel_id=1, source_target_pairs={{0,1},{1,0},{2,3},{3,2},{4,5},{5,4},{6,7},{7,6},{8,9},{9,8},{10,11... | collective-permute-start | bytes 110600 | tf_op jit(solution)/shard_map/ppermute | solution.py:199
  27.4 4.0 %collective-permute-start.7 = (bf16[144,128]{1,0:T(8,128)(2,1)S(1)}, bf16[144,128]{1,0:T(8,128)(2,1)S(1)}, u32[]{:S(2)}, u32[]{:S(2)}) collective-permute-start(bf16[144,128]{1,0:T(8,128)(2,1)S(1)} %get-tuple-element.29), channel_id=1, source_target_pairs={{0,64},{64,0},{128,192},{192,128},{1,65},{65,1},{129,193},{193,129... | collective-permute-start | bytes 110600 | tf_op jit(solution)/shard_map/ppermute | solution.py:196
  31.4 4.9 %collective-permute-start.8 = (bf16[144,128]{1,0:T(8,128)(2,1)S(1)}, bf16[144,128]{1,0:T(8,128)(2,1)S(1)}, u32[]{:S(2)}, u32[]{:S(2)}) collective-permute-start(bf16[144,128]{1,0:T(8,128)(2,1)S(1)} %get-tuple-element.32), channel_id=1, source_target_pairs={{0,128},{64,192},{128,0},{192,64},{1,129},{65,193},{129,1},{193,65... | collective-permute-start | bytes 110600 | tf_op jit(solution)/shard_map/ppermute | solution.py:196
  36.4 4.0 %collective-permute-start.9 = (bf16[144,128]{1,0:T(8,128)(2,1)S(1)}, bf16[144,128]{1,0:T(8,128)(2,1)S(1)}, u32[]{:S(2)}, u32[]{:S(2)}) collective-permute-start(bf16[144,128]{1,0:T(8,128)(2,1)S(1)} %get-tuple-element.35), channel_id=1, source_target_pairs={{0,2},{1,3},{2,0},{3,1},{4,6},{5,7},{6,4},{7,5},{8,10},{9,11},{10,... | collective-permute-start | bytes 110600 | tf_op jit(solution)/shard_map/ppermute | solution.py:199
  40.5 5.3 %collective-permute-start.10 = (bf16[144,128]{1,0:T(8,128)(2,1)S(1)}, bf16[144,128]{1,0:T(8,128)(2,1)S(1)}, u32[]{:S(2)}, u32[]{:S(2)}) collective-permute-start(bf16[144,128]{1,0:T(8,128)(2,1)S(1)} %get-tuple-element.38), channel_id=1, source_target_pairs={{0,6},{1,7},{2,4},{3,5},{4,2},{5,3},{6,0},{7,1},{8,14},{9,15},{10,... | collective-permute-start | bytes 110600 | tf_op jit(solution)/shard_map/ppermute | solution.py:199
  45.9 1.3 %collective-permute-start.11 = (bf16[16,1024]{1,0:T(8,128)(2,1)S(1)}, bf16[16,1024]{1,0:T(8,128)(2,1)S(1)}, u32[]{:S(2)}, u32[]{:S(2)}) collective-permute-start(bf16[16,1024]{1,0:T(8,128)(2,1)S(1)} %join_y2.1), channel_id=1, source_target_pairs={{0,1},{1,0},{2,3},{3,2},{4,5},{5,4},{6,7},{7,6},{8,9},{9,8},{10,11... | collective-permute-start | bytes 98312 | tf_op jit(solution)/shard_map/ppermute | solution.py:199

commit v2 on v1

v2 whole, which is shorter than its diff:
```python
import math

import jax
import jax.numpy as jnp
from jax import lax
from jax.experimental import pallas as pl
from jax.experimental.pallas import tpu as pltpu
from jax.sharding import PartitionSpec as P

HD = 128
BLK = 16
GROUP = 16
NREQ = 16
LANES = GROUP * NREQ
HALF = LANES // 2
STAT = 16
LOW = -1e30
FACTOR = 1.0 / math.sqrt(HD)
BF = jnp.bfloat16
F32 = jnp.float32


def vmem():
    return pl.BlockSpec(memory_space=pltpu.VMEM)


def smem():
    return pl.BlockSpec(memory_space=pltpu.SMEM)


def dot(a, b, dims):
    return lax.dot_general(a, b, (dims, ((), ())), preferred_element_type=F32)


def rows_of(queries):
    return jnp.concatenate([queries[:, h * HD : (h + 1) * HD] for h in range(GROUP)], axis=0)


def stat_rows(peak, total, rows):
    place = lax.broadcasted_iota(jnp.int32, (rows, peak.shape[1]), 0)
    return jnp.where(place == 0, peak, jnp.where(place == 1, total, 0.0))


def packed_stats(peak, total):
    hi = peak.astype(BF).astype(F32)
    rest = peak - hi
    mid = rest.astype(BF).astype(F32)
    low = rest - mid
    total_hi = total.astype(BF).astype(F32)
    total_low = total - total_hi
    place = lax.broadcasted_iota(jnp.int32, (STAT, peak.shape[1]), 0)
    packed = jnp.zeros((STAT, peak.shape[1]), F32)
    for row, part in enumerate((hi, mid, low, total_hi, total_low)):
        packed = jnp.where(place == row, part, packed)
    return packed.astype(BF)


def unpacked_stats(packed):
    rows = packed.astype(F32)
    peak = rows[0:1] + (rows[1:2] + rows[2:3])
    total = rows[3:4] + rows[4:5]
    return peak, total


def store_packed(ref, weighted, peak, total):
    ref[0:HD, :] = weighted.astype(BF)
    ref[HD : HD + STAT, :] = packed_stats(peak, total)


def kv_kernel(x_ref, w_ref, out0, out1, out2, out3, x_buf, w_buf, x_sem, w_sem):
    me = lax.axis_index("sec")
    rows = out0.shape[0]
    parts = w_sem.shape[0]
    depth = w_ref.shape[0] // parts
    flips = (3, 2, 1, 0)
    outs = (out0, out1, out2, out3)

    def x_copy(turn):
        start = pl.multiple_of((me ^ flips[turn]) * rows, rows)
        return pltpu.make_async_copy(
            x_ref.at[pl.ds(start, rows), :],
            x_buf.at[pl.ds(turn * rows, rows), :],
            x_sem.at[turn],
        )

    def w_copy(part):
        span = pl.ds(part * depth, depth)
        return pltpu.make_async_copy(w_ref.at[span, :], w_buf.at[span, :], w_sem.at[part])

    x_copy(0).start()
    for part in range(parts):
        w_copy(part).start()
    for turn in range(1, 4):
        x_copy(turn).start()
    for turn in range(4):
        x_copy(turn).wait()
        mine = x_buf[turn * rows : (turn + 1) * rows, :]
        if turn == 0:
            total = jnp.zeros(out0.shape, F32)
            for part in range(parts):
                w_copy(part).wait()
                span = slice(part * depth, (part + 1) * depth)
                total = total + dot(mine[:, span], w_buf[span, :], ((1,), (0,)))
        else:
            total = dot(mine, w_buf[...], ((1,), (0,)))
        outs[flips[turn]][...] = total.astype(BF)


def cached_kernel(
    owner_ref, slot_ref, len_ref, ctx_ref, q_ref, cache_ref, weighted_ref, stats_ref, live_ref
):
    sec_id, req_id = lax.axis_index("sec"), lax.axis_index("req")
    queries = rows_of(q_ref[...])
    count = cache_ref.shape[1]
    lane = lax.broadcasted_iota(jnp.int32, (count, LANES), 1) % NREQ
    position = lax.broadcasted_iota(jnp.int32, (count, LANES), 0) + sec_id * count
    first = req_id * 2
    live0 = (lane == first) & (position < ctx_ref[0])
    live1 = (lane == first + 1) & (position < ctx_ref[1])
    live = live0 | live1
    scores0 = dot(cache_ref[0, :, 0:HD], queries, ((1,), (1,)))
    scores1 = dot(cache_ref[1, :, 0:HD], queries, ((1,), (1,)))
    scores = jnp.where(live, jnp.where(lane == first, scores0, scores1) * FACTOR, LOW)
    peak = jnp.max(scores, axis=0, keepdims=True)
    weights = jnp.where(live, jnp.exp(scores - peak), 0.0)
    total = jnp.sum(weights, axis=0, keepdims=True)
    weights = weights.astype(BF)
    zero = jnp.zeros_like(weights)
    weighted_ref[...] = dot(
        cache_ref[0, :, HD : 2 * HD], jnp.where(live0, weights, zero), ((0,), (0,))
    ) + dot(cache_ref[1, :, HD : 2 * HD], jnp.where(live1, weights, zero), ((0,), (0,)))
    stats_ref[...] = stat_rows(peak, total, 8)
    blocks = live_ref.shape[0] // BLK
    base = (req_id * lax.axis_size("sec") + sec_id) * blocks
    lane = lax.broadcasted_iota(jnp.int32, (BLK, LANES), 1) % NREQ
    place = lax.broadcasted_iota(jnp.int32, (BLK, LANES), 0)
    for block in range(blocks):
        holder = owner_ref[base + block] * 2 + slot_ref[base + block]
        live_block = (lane == holder) & (place < len_ref[base + block])
        live_ref[block * BLK : (block + 1) * BLK, :] = live_block.astype(F32)


def prompt_kernel(
    q_ref, live_ref, own_ref, a_ref, b_ref, c_ref, cw_ref, cs_ref, kw_ref, ks_ref, send_ref
):
    summed = (own_ref[...].astype(F32) + a_ref[...].astype(F32)) + (
        b_ref[...].astype(F32) + c_ref[...].astype(F32)
    )
    new_kv = summed.astype(BF)
    queries = rows_of(q_ref[...])
    live = live_ref[...] > 0.5
    scores = dot(new_kv[:, 0:HD], queries, ((1,), (1,))) * FACTOR
    scores = jnp.where(live, scores, LOW)
    peak = jnp.max(scores, axis=0, keepdims=True)
    weights = jnp.where(live, jnp.exp(scores - peak), 0.0)
    total = jnp.sum(weights, axis=0, keepdims=True)
    weighted = dot(new_kv[:, HD : 2 * HD], weights.astype(BF), ((0,), (0,)))
    cached_peak, cached_total = cs_ref[0:1, :], cs_ref[1:2, :]
    joint = jnp.maximum(peak, cached_peak)
    scale, cached_scale = jnp.exp(peak - joint), jnp.exp(cached_peak - joint)
    weighted = weighted * scale + cw_ref[...] * cached_scale
    total = total * scale + cached_total * cached_scale
    core = lax.axis_index("req") % 2

    @pl.when(core == 0)
    def _():
        kw_ref[...] = weighted[:, :HALF]
        ks_ref[...] = stat_rows(joint[:, :HALF], total[:, :HALF], 8)
        store_packed(send_ref, weighted[:, HALF:], joint[:, HALF:], total[:, HALF:])

    @pl.when(core == 1)
    def _():
        kw_ref[...] = weighted[:, HALF:]
        ks_ref[...] = stat_rows(joint[:, HALF:], total[:, HALF:], 8)
        store_packed(send_ref, weighted[:, :HALF], joint[:, :HALF], total[:, :HALF])


def joined(w_ref, s_ref, got_refs):
    peaks, totals = [s_ref[0:1, :]], [s_ref[1:2, :]]
    for got_ref in got_refs:
        peak, total = unpacked_stats(got_ref[HD : HD + STAT, :])
        peaks.append(peak)
        totals.append(total)
    joint = peaks[0]
    for peak in peaks[1:]:
        joint = jnp.maximum(joint, peak)
    scales = [jnp.exp(peak - joint) for peak in peaks]
    weighted, total = w_ref[...] * scales[0], totals[0] * scales[0]
    for got_ref, part, scale in zip(got_refs, totals[1:], scales[1:]):
        weighted = weighted + got_ref[0:HD, :].astype(F32) * scale
        total = total + part * scale
    return weighted, joint, total


def join_kernel(w_ref, s_ref, *refs):
    got_refs, (kw_ref, ks_ref, send_ref) = refs[:-3], refs[-3:]
    weighted, peak, total = joined(w_ref, s_ref, got_refs)
    kw_ref[...] = weighted
    ks_ref[...] = stat_rows(peak, total, 8)
    store_packed(send_ref, weighted, peak, total)


def last_kernel(w_ref, s_ref, *refs):
    weighted, _, total = joined(w_ref, s_ref, refs[:-1])
    rows = (weighted / total).T
    for h in range(GROUP // 2):
        refs[-1][:, h * HD : (h + 1) * HD] = rows[h * NREQ : (h + 1) * NREQ, :].astype(BF)


def half_rows(w_ref, core):
    half = w_ref.shape[0] // 2
    return w_ref[pl.ds(pl.multiple_of(core * half, half), half), :]


def first_half_kernel(mine_ref, w_ref, out_ref):
    core = lax.axis_index("req") % 2
    out_ref[...] = dot(mine_ref[...], half_rows(w_ref, core), ((1,), (0,)))


def second_half_kernel(other_ref, w_ref, so_far_ref, out_ref):
    core = lax.axis_index("req") % 2
    more = dot(other_ref[...], half_rows(w_ref, 1 - core), ((1,), (0,)))
    out_ref[...] = (so_far_ref[...] + more).astype(BF)


def shape(dims, dtype):
    return jax.ShapeDtypeStruct(dims, dtype)


def call(kernel, ins, outs, name, flops=0, scratch=()):
    moved = 0
    for _, value in ins:
        moved += value.size * value.dtype.itemsize
    return pl.pallas_call(
        kernel,
        out_shape=outs,
        in_specs=[spec for spec, _ in ins],
        out_specs=jax.tree.map(lambda _: vmem(), outs),
        scratch_shapes=scratch,
        compiler_params=pltpu.CompilerParams(vmem_limit_bytes=32 * 1024 * 1024),
        cost_estimate=pl.CostEstimate(flops=flops, bytes_accessed=moved, transcendentals=0),
        name=name,
    )(*[value for _, value in ins])


STATE = (shape((HD, HALF), F32), shape((8, HALF), F32), shape((HD + STAT, HALF), BF))


def on_device(prompt_x, w_kv, queries, cache, w_out, blk_owner, blk_slot, blk_len, ctx_len):
    sec_count = lax.axis_size("sec")
    req_count = lax.axis_size("req")
    req_id = lax.axis_index("req")
    rows = prompt_x.shape[0] // sec_count
    width = w_kv.shape[1]

    def over(value, sec_flip, req_flip):
        if req_flip == 0:
            return lax.ppermute(value, "sec", [(i, i ^ sec_flip) for i in range(sec_count)])
        if sec_flip == 0:
            return lax.ppermute(value, "req", [(i, i ^ req_flip) for i in range(req_count)])
        pairs = []
        for i in range(sec_count):
            for j in range(req_count):
                pairs.append((i * req_count + j, (i ^ sec_flip) * req_count + (j ^ req_flip)))
        return lax.ppermute(value, ("sec", "req"), pairs)

    tiled = jnp.tile(queries, (NREQ // 2, 1))
    holder = lax.broadcasted_iota(jnp.int32, tiled.shape, 0) // 2
    gathered = jnp.where(holder == req_id, tiled, jnp.zeros_like(tiled))
    for flip in (1, 2, 6):
        gathered = gathered + over(gathered, 0, flip)

    chunk = shape((rows, width), BF)
    chunks = call(
        kv_kernel,
        [(pl.BlockSpec(memory_space=pltpu.HBM), prompt_x), (pl.BlockSpec(memory_space=pltpu.HBM), w_kv)],
        (chunk, chunk, chunk, chunk),
        "new_kv",
        flops=2 * prompt_x.size * width,
        scratch=(
            pltpu.VMEM(prompt_x.shape, BF),
            pltpu.VMEM(w_kv.shape, BF),
            pltpu.SemaphoreType.DMA((4,)),
            pltpu.SemaphoreType.DMA((4,)),
        ),
    )
    arrived = [over(chunks[flip], flip, 0) for flip in (3, 2, 1)]

    cached = call(
        cached_kernel,
        [
            (smem(), blk_owner[:, 0]),
            (smem(), blk_slot),
            (smem(), blk_len),
            (smem(), ctx_len),
            (vmem(), tiled),
            (vmem(), cache[:, :, 0, :]),
        ],
        (shape((HD, LANES), F32), shape((8, LANES), F32), shape((rows, LANES), F32)),
        "cached",
        flops=2 * 4 * cache.shape[1] * HD * LANES,
    )
    kept = call(
        prompt_kernel,
        [
            (vmem(), value)
            for value in (gathered, cached[2], chunks[0], *arrived, cached[0], cached[1])
        ],
        STATE,
        "prompt",
        flops=2 * 2 * rows * HD * LANES,
    )
    kept = call(
        join_kernel,
        [(vmem(), value) for value in (kept[0], kept[1], over(kept[2], 0, 1))],
        STATE,
        "join_core",
    )
    got = [over(kept[2], *flips) for flips in ((1, 2), (1, 0), (0, 2))]
    kept = call(
        join_kernel, [(vmem(), value) for value in (kept[0], kept[1], *got)], STATE, "join_near"
    )
    got = [over(kept[2], *flips) for flips in ((2, 6), (2, 0), (0, 6))]
    mine = call(
        last_kernel,
        [(vmem(), value) for value in (kept[0], kept[1], *got)],
        shape((NREQ, HALF // NREQ * HD), BF),
        "join_far",
    )
    other = over(mine, 0, 1)
    columns = w_out.shape[1]
    flops = w_out.size * NREQ
    so_far = call(
        first_half_kernel,
        [(vmem(), mine), (vmem(), w_out)],
        shape((NREQ, columns), F32),
        "project_mine",
        flops=flops,
    )
    partial_out = call(
        second_half_kernel,
        [(vmem(), other), (vmem(), w_out), (vmem(), so_far)],
        shape((NREQ, columns), BF),
        "project_other",
        flops=flops,
    )
    head_count = lax.axis_size("head")
    pieces = partial_out.reshape(head_count, NREQ // head_count, columns)
    pieces = lax.all_to_all(pieces, "head", 0, 0, tiled=True)
    return jnp.sum(pieces.astype(F32), axis=0).astype(BF)


def solution(mesh):
    return jax.shard_map(
        on_device,
        mesh=mesh,
        in_specs=(
            P("req", "sec"),
            P("sec", "head"),
            P("req", "head"),
            P("req", "sec", "head", None),
            P("head", ("sec", "req")),
            P(),
            P(),
            P(),
            P("req"),
        ),
        out_specs=P("head", ("sec", "req")),
        check_vma=False,
    )
```

time: 69.9 us -> 63.1 us (0.903)
  matrix products: 5.49 us -> 0 us
  waiting for transfers between devices: 18.3 us -> 13.5 us
  starting transfers between devices: 14.6 us -> 18.8 us
  Pallas kernels: 3.37 us -> 6.61 us
  other arithmetic: 3.45 us -> 0.82 us
  blocking collectives: 19.1 us -> 17.7 us
    dot_general x2 -> x0, matrix products: 5.49 us -> none  [the longest x1 3.52 us: on_device(): part = jnp.dot(prompt_x, w_kv, preferred_element_type=F32).astype(BF)]
    ppermute x12 -> x14, waiting for transfers between devices: 18.3 us -> 13.5 us  [the longest x2 5.18 us: over(): return lax.ppermute(value, ('sec', 'req'), pairs)]
    ppermute x12 -> x14, starting transfers between devices: 14.6 us -> 18.8 us  [the longest x5 7.16 us: over(): lax.ppermute(value, 'sec', [(i, i ^ sec_flip) for i in range(sec_count)])]
    pallas_call x7 -> x8, Pallas kernels: 3.37 us -> 6.61 us  [call(): pl.pallas_call(kernel, out_shape=outs, in_specs=[spec for spec, _ in ins]...]
    unnamed x10 -> x16, local copies, waits for them, and re-layouts: 1.58 us -> 3.81 us
    concatenate x3 -> x0, other arithmetic: 1.5 us -> none  [on_device(): gathered = jnp.concatenate([gathered, over_req(gathered, flip)], axis=0)]
    all_to_all x1, blocking collectives: 19.1 us -> 17.7 us  [on_device(): pieces = lax.all_to_all(pieces, 'head', 0, 0, tiled=True)]
    dynamic_slice x1 -> x0, local copies, waits for them, and re-layouts: 1.27 us -> none  [on_device(): length = lax.dynamic_slice(blk_len, (base,), (count,))]
  transfers between devices with their start and end apart: 12 -> 14, of which waited for: 7 -> 10; matrix products, arithmetic and copies ran while one was open for 13% -> 0% of each run, Pallas kernels for 3% -> 9%
where the time goes in v2:
time: 63.1 us; the launch traced here: 62.2 us
  starting transfers between devices  18.8 us (30%)
  blocking collectives  17.7 us (28%)
  waiting for transfers between devices  13.5 us (21%)
  Pallas kernels  6.61 us (10%)
  local copies, waits for them, and re-layouts  4.6 us (7%)
  other arithmetic  0.82 us (1%)
    all_to_all x1, blocking collectives, on_device(): pieces = lax.all_to_all(pieces, 'head', 0, 0, tiled=True)  17.7 us
    ppermute x5, starting transfers between devices, over(): lax.ppermute(value, 'sec', [(i, i ^ sec_flip) for i in range(sec_count)])  7.16 us
    ppermute x7, starting transfers between devices, over(): lax.ppermute(value, 'req', [(i, i ^ req_flip) for i in range(req_count)])  6.73 us
    pallas_call x8, Pallas kernels, call(): pl.pallas_call(kernel, out_shape=outs, in_specs=[spec for spec, _ in ins]...  6.61 us
    ppermute x2, waiting for transfers between devices, over(): return lax.ppermute(value, ('sec', 'req'), pairs)  5.18 us
    ppermute x2, starting transfers between devices, over(): return lax.ppermute(value, ('sec', 'req'), pairs)  4.87 us
    ppermute x7, waiting for transfers between devices, over(): lax.ppermute(value, 'req', [(i, i ^ req_flip) for i in range(req_count)])  4.44 us
    ppermute x5, waiting for transfers between devices, over(): lax.ppermute(value, 'sec', [(i, i ^ sec_flip) for i in range(sec_count)])  3.92 us
  transfers between devices with their start and end apart: 14, of which 10 were waited for; matrix products, arithmetic and copies ran while one was open for 0% of the time, Pallas kernels for 9%

profile of v2, /device:TPU:2, one launch (start us, length us, event | category | flops | bytes accessed | tf_op | source)
XLA Modules:
  0.0 62.2 jit_solution(4790130263603738254)
XLA Ops:
  0.0 0.7 %tile.4 = bf16[8,2,2048]{2,1,0:T(2,128)(2,1)S(1)} broadcast(bf16[2,2048]{1,0:T(2,128)(2,1)} %param.11), dimensions={1,2} | broadcast | bytes 73728 | tf_op jit(solution)/shard_map/tile | solution.py:267
  0.8 0.1 fusion
  0.9 0.1 collective-permute-start
  1.0 1.2 %collective-permute-done = bf16[16,2048]{1,0:T(8,128)(2,1)S(1)} collective-permute-done((bf16[16,2048]{1,0:T(8,128)(2,1)S(1)}, bf16[16,2048]{1,0:T(8,128)(2,1)S(1)}, u32[]{:S(2)}, u32[]{:S(2)}) %collective-permute-start) | collective-permute-done | bytes 65568 | tf_op jit(solution)/shard_map/ppermute | solution.py:260
  2.2 0.1 fusion.1
  2.3 1.7 %collective-permute-start.1 = (bf16[16,2048]{1,0:T(8,128)(2,1)S(1)}, bf16[16,2048]{1,0:T(8,128)(2,1)S(1)}, u32[]{:S(2)}, u32[]{:S(2)}) collective-permute-start(bf16[16,2048]{1,0:T(8,128)(2,1)S(1)} %fusion.1), channel_id=1, source_target_pairs={{0,2},{1,3},{2,0},{3,1},{4,6},{5,7},{6,4},{7,5},{8,10},{9,11},{10,... | collective-permute-start | bytes 196616 | tf_op jit(solution)/shard_map/ppermute | solution.py:260
  4.0 0.0 copy-start.1
  4.0 2.2 %copy-done.1 = bf16[512,4096]{1,0:T(8,128)(2,1)S(1)} copy-done((bf16[512,4096]{1,0:T(8,128)(2,1)S(1)}, bf16[512,4096]{1,0:T(8,128)(2,1)}, u32[]{:S(2)}) %copy-start.1) | copy-done | bytes 4194328
  6.2 0.0 copy-start.2
  6.2 1.6 %copy-done.2 = bf16[4096,256]{1,0:T(8,128)(2,1)S(1)} copy-done((bf16[4096,256]{1,0:T(8,128)(2,1)S(1)}, bf16[4096,256]{1,0:T(8,128)(2,1)}, u32[]{:S(2)}) %copy-start.2) | copy-done | bytes 2097176
  7.8 0.0 copy-start.3
  7.8 0.0 copy-start.4
  7.8 0.0 copy-start.5
  7.8 0.0 copy-start.6
  7.8 0.0 copy-start.7
  7.8 3.4 %new_kv.1 = (bf16[128,256]{1,0:T(8,128)(2,1)S(1)}, bf16[128,256]{1,0:T(8,128)(2,1)S(1)}, bf16[128,256]{1,0:T(8,128)(2,1)S(1)}, bf16[128,256]{1,0:T(8,128)(2,1)S(1)}) custom-call(bf16[512,4096]{1,0:T(8,128)(2,1)S(1)} %copy-done.1, bf16[4096,256]{1,0:T(8,128)(2,1)S(1)} %copy-done.2), custom_call_target="tpu_custom_call" | custom-call | flops 1073741824 | bytes 6291456 | tf_op jit(solution)/shard_map/new_kv/pallas_call | solution.py:234
  11.2 0.0 copy-start
  11.2 4.7 %collective-permute-start.3 = (bf16[128,256]{1,0:T(8,128)(2,1)S(1)}, bf16[128,256]{1,0:T(8,128)(2,1)S(1)}, u32[]{:S(2)}, u32[]{:S(2)}) collective-permute-start(bf16[128,256]{1,0:T(8,128)(2,1)S(1)} %get-tuple-element.23), channel_id=1, source_target_pairs={{0,192},{64,128},{128,64},{192,0},{1,193},{65,129},{129,65},{193,1... | collective-permute-start | bytes 196616 | tf_op jit(solution)/shard_map/ppermute | solution.py:258
  16.0 0.0 collective-permute-done.1
  16.0 2.3 %collective-permute-start.2 = (bf16[16,2048]{1,0:T(8,128)(2,1)S(1)}, bf16[16,2048]{1,0:T(8,128)(2,1)S(1)}, u32[]{:S(2)}, u32[]{:S(2)}) collective-permute-start(bf16[16,2048]{1,0:T(8,128)(2,1)S(1)} %add.12), channel_id=1, source_target_pairs={{0,6},{1,7},{2,4},{3,5},{4,2},{5,3},{6,0},{7,1},{8,14},{9,15},{10,... | collective-permute-start | bytes 196616 | tf_op jit(solution)/shard_map/ppermute | solution.py:260
  18.3 0.0 collective-permute-start.4
  18.3 0.6 collective-permute-start.5
  18.8 0.0 copy-done.3
  18.8 0.0 copy-done.4
  18.9 0.0 copy-done.5
  18.9 0.0 copy-done.6
  18.9 0.0 copy-done.7
  18.9 2.1 %cached.1 = (f32[128,256]{1,0:T(8,128)S(1)}, f32[8,256]{1,0:T(8,128)S(1)}, f32[128,256]{1,0:T(8,128)S(1)}) custom-call(s32[256]{0:T(256)S(1)} %bitcast.3, s32[256]{0:T(256)S(1)} %copy-done.5, s32[256]{0:T(256)S(1)} %copy-done.6, s32[2]{0:T(128)S(1)} %copy-done.7, bf16[16,2048]{1,0:T(8,128)(2,1)S(1)} %tile.10.q_ref, bf16[2,1024,256]{2,1,0:T(8,128)(2,1)S(1)} %bitcast.2), custom_call_target="tpu_custom_call" | custom-call | flops 268435456 | bytes 1117192 | tf_op jit(solution)/shard_map/cached/pallas_call | solution.py:234
  21.0 0.6 collective-permute-done.2
  21.6 0.0 collective-permute-done.3.a_ref
  21.6 1.9 %collective-permute-done.4.b_ref = bf16[128,256]{1,0:T(8,128)(2,1)S(1)} collective-permute-done((bf16[128,256]{1,0:T(8,128)(2,1)S(1)}, bf16[128,256]{1,0:T(8,128)(2,1)S(1)}, u32[]{:S(2)}, u32[]{:S(2)}) %collective-permute-start.4) | collective-permute-done | bytes 65568 | tf_op jit(solution)/shard_map/ppermute | solution.py:258
  23.5 0.0 collective-permute-done.5.c_ref
  23.5 0.4 prompt.1
  23.9 0.1 collective-permute-start.6
  24.0 1.2 %collective-permute-done.6.refs_0_ = bf16[144,128]{1,0:T(8,128)(2,1)S(1)} collective-permute-done((bf16[144,128]{1,0:T(8,128)(2,1)S(1)}, bf16[144,128]{1,0:T(8,128)(2,1)S(1)}, u32[]{:S(2)}, u32[]{:S(2)}) %collective-permute-start.6) | collective-permute-done | bytes 36896 | tf_op jit(solution)/shard_map/ppermute | solution.py:260
  25.3 0.8 %collective-permute-start.9 = (bf16[144,128]{1,0:T(8,128)(2,1)S(1)}, bf16[144,128]{1,0:T(8,128)(2,1)S(1)}, u32[]{:S(2)}, u32[]{:S(2)}) collective-permute-start(bf16[144,128]{1,0:T(8,128)(2,1)S(1)} %get-tuple-element.33), channel_id=1, source_target_pairs={{0,2},{1,3},{2,0},{3,1},{4,6},{5,7},{6,4},{7,5},{8,10},{9,11},{10,... | collective-permute-start | bytes 110600 | tf_op jit(solution)/shard_map/ppermute | solution.py:260
  26.0 0.0 collective-permute-start.8
  26.0 2.8 %collective-permute-start.7 = (bf16[144,128]{1,0:T(8,128)(2,1)S(1)}, bf16[144,128]{1,0:T(8,128)(2,1)S(1)}, u32[]{:S(2)}, u32[]{:S(2)}) collective-permute-start(bf16[144,128]{1,0:T(8,128)(2,1)S(1)} %get-tuple-element.33), channel_id=1, source_target_pairs={{0,66},{1,67},{2,64},{3,65},{4,70},{5,71},{6,68},{7,69},{64,2},{65... | collective-permute-start | bytes 110600 | tf_op jit(solution)/shard_map/ppermute | solution.py:265
  28.8 0.5 collective-permute-done.9.refs_2_
  29.3 0.8 %collective-permute-done.8.refs_1_ = bf16[144,128]{1,0:T(8,128)(2,1)S(1)} collective-permute-done((bf16[144,128]{1,0:T(8,128)(2,1)S(1)}, bf16[144,128]{1,0:T(8,128)(2,1)S(1)}, u32[]{:S(2)}, u32[]{:S(2)}) %collective-permute-start.8) | collective-permute-done | bytes 36896 | tf_op jit(solution)/shard_map/ppermute | solution.py:258
  30.1 1.1 %collective-permute-done.7.refs_0_ = bf16[144,128]{1,0:T(8,128)(2,1)S(1)} collective-permute-done((bf16[144,128]{1,0:T(8,128)(2,1)S(1)}, bf16[144,128]{1,0:T(8,128)(2,1)S(1)}, u32[]{:S(2)}, u32[]{:S(2)}) %collective-permute-start.7) | collective-permute-done | bytes 36896 | tf_op jit(solution)/shard_map/ppermute | solution.py:265
  31.2 0.1 join_near.1
  31.2 1.8 %collective-permute-start.12 = (bf16[144,128]{1,0:T(8,128)(2,1)S(1)}, bf16[144,128]{1,0:T(8,128)(2,1)S(1)}, u32[]{:S(2)}, u32[]{:S(2)}) collective-permute-start(bf16[144,128]{1,0:T(8,128)(2,1)S(1)} %get-tuple-element.36), channel_id=1, source_target_pairs={{0,6},{1,7},{2,4},{3,5},{4,2},{5,3},{6,0},{7,1},{8,14},{9,15},{10,... | collective-permute-start | bytes 110600 | tf_op jit(solution)/shard_map/ppermute | solution.py:260
  33.0 1.9 %collective-permute-start.11 = (bf16[144,128]{1,0:T(8,128)(2,1)S(1)}, bf16[144,128]{1,0:T(8,128)(2,1)S(1)}, u32[]{:S(2)}, u32[]{:S(2)}) collective-permute-start(bf16[144,128]{1,0:T(8,128)(2,1)S(1)} %get-tuple-element.36), channel_id=1, source_target_pairs={{0,128},{64,192},{128,0},{192,64},{1,129},{65,193},{129,1},{193,65... | collective-permute-start | bytes 110600 | tf_op jit(solution)/shard_map/ppermute | solution.py:258
  34.8 2.1 %collective-permute-start.10 = (bf16[144,128]{1,0:T(8,128)(2,1)S(1)}, bf16[144,128]{1,0:T(8,128)(2,1)S(1)}, u32[]{:S(2)}, u32[]{:S(2)}) collective-permute-start(bf16[144,128]{1,0:T(8,128)(2,1)S(1)} %get-tuple-element.36), channel_id=1, source_target_pairs={{0,134},{1,135},{2,132},{3,133},{4,130},{5,131},{6,128},{7,129},{6... | collective-permute-start | bytes 110600 | tf_op jit(solution)/shard_map/ppermute | solution.py:265
  36.9 0.0 collective-permute-done.12.refs_2_
  36.9 1.2 %collective-permute-done.11.refs_1_ = bf16[144,128]{1,0:T(8,128)(2,1)S(1)} collective-permute-done((bf16[144,128]{1,0:T(8,128)(2,1)S(1)}, bf16[144,128]{1,0:T(8,128)(2,1)S(1)}, u32[]{:S(2)}, u32[]{:S(2)}) %collective-permute-start.11) | collective-permute-done | bytes 36896 | tf_op jit(solution)/shard_map/ppermute | solution.py:258
  38.1 4.1 %collective-permute-done.10.refs_0_ = bf16[144,128]{1,0:T(8,128)(2,1)S(1)} collective-permute-done((bf16[144,128]{1,0:T(8,128)(2,1)S(1)}, bf16[144,128]{1,0:T(8,128)(2,1)S(1)}, u32[]{:S(2)}, u32[]{:S(2)}) %collective-permute-start.10) | collective-permute-done | bytes 36896 | tf_op jit(solution)/shard_map/ppermute | solution.py:265
  42.2 0.1 join_far.1.mine_ref
  42.3 0.1 collective-permute-start.13
  42.4 0.0 copy-done
  42.4 0.3 project_mine.1.so_far_ref
  42.7 0.9 %collective-permute-done.13.other_ref = bf16[16,1024]{1,0:T(8,128)(2,1)S(1)} collective-permute-done((bf16[16,1024]{1,0:T(8,128)(2,1)S(1)}, bf16[16,1024]{1,0:T(8,128)(2,1)S(1)}, u32[]{:S(2)}, u32[]{:S(2)}) %collective-permute-start.13) | collective-permute-done | bytes 32800 | tf_op jit(solution)/shard_map/ppermute | solution.py:260
  43.6 0.2 project_other.1
  43.9 17.7 %all_to_all.5 = bf16[8,2,512]{2,1,0:T(2,128)(2,1)S(1)} all-to-all(bf16[8,2,512]{2,1,0:T(2,128)(2,1)S(1)} %reshape.7), channel_id=1, replica_groups=mesh['sec'=4,'head'=8,'req'=8] {'head'}, dimensions={0} | all-to-all | bytes 32768 | tf_op jit(solution)/shard_map/all_to_all | solution.py:349
  61.6 0.6 reduce_sum.12
  (7 shorter events, 0.1 us)
Async XLA Ops:
  0.9 1.3 %collective-permute-start = (bf16[16,2048]{1,0:T(8,128)(2,1)S(1)}, bf16[16,2048]{1,0:T(8,128)(2,1)S(1)}, u32[]{:S(2)}, u32[]{:S(2)}) collective-permute-start(bf16[16,2048]{1,0:T(8,128)(2,1)S(1)} %fusion), channel_id=1, source_target_pairs={{0,1},{1,0},{2,3},{3,2},{4,5},{5,4},{6,7},{7,6},{8,9},{9,8},{10,11... | collective-permute-start | bytes 196616 | tf_op jit(solution)/shard_map/ppermute | solution.py:260
  2.3 13.6 %collective-permute-start.1 = (bf16[16,2048]{1,0:T(8,128)(2,1)S(1)}, bf16[16,2048]{1,0:T(8,128)(2,1)S(1)}, u32[]{:S(2)}, u32[]{:S(2)}) collective-permute-start(bf16[16,2048]{1,0:T(8,128)(2,1)S(1)} %fusion.1), channel_id=1, source_target_pairs={{0,2},{1,3},{2,0},{3,1},{4,6},{5,7},{6,4},{7,5},{8,10},{9,11},{10,... | collective-permute-start | bytes 196616 | tf_op jit(solution)/shard_map/ppermute | solution.py:260
  4.0 2.2 %copy-start.1 = (bf16[512,4096]{1,0:T(8,128)(2,1)S(1)}, bf16[512,4096]{1,0:T(8,128)(2,1)}, u32[]{:S(2)}) copy-start(bf16[512,4096]{1,0:T(8,128)(2,1)} %x_ref.1) | copy-start | bytes 12582916
  6.2 1.6 %copy-start.2 = (bf16[4096,256]{1,0:T(8,128)(2,1)S(1)}, bf16[4096,256]{1,0:T(8,128)(2,1)}, u32[]{:S(2)}) copy-start(bf16[4096,256]{1,0:T(8,128)(2,1)} %w_ref.3) | copy-start | bytes 6291460
  7.8 11.1 %copy-start.3 = (bf16[2,1024,1,256]{3,1,2,0:T(8,128)(2,1)S(1)}, bf16[2,1024,1,256]{3,1,2,0:T(8,128)(2,1)}, u32[]{:S(2)}) copy-start(bf16[2,1024,1,256]{3,1,2,0:T(8,128)(2,1)} %param.12) | copy-start | bytes 3145732
  7.8 11.1 %copy-start.4 = (s32[256,1]{0,1:T(1,128)S(1)}, s32[256,1]{0,1:T(1,128)}, u32[]{:S(2)}) copy-start(s32[256,1]{0,1:T(1,128)} %param.14) | copy-start | bytes 3076
  7.8 11.1 %copy-start.5 = (s32[256]{0:T(256)S(1)}, s32[256]{0:T(256)}, u32[]{:S(2)}) copy-start(s32[256]{0:T(256)} %slot_ref.1) | copy-start | bytes 3076
  7.8 11.1 %copy-start.6 = (s32[256]{0:T(256)S(1)}, s32[256]{0:T(256)}, u32[]{:S(2)}) copy-start(s32[256]{0:T(256)} %len_ref.1) | copy-start | bytes 3076
  7.8 11.1 %copy-start.7 = (s32[2]{0:T(128)S(1)}, s32[2]{0:T(128)}, u32[]{:S(2)}) copy-start(s32[2]{0:T(128)} %ctx_ref.1) | copy-start | bytes 28
  11.2 31.2 %copy-start = (bf16[2048,512]{1,0:T(8,128)(2,1)S(1)}, bf16[2048,512]{1,0:T(8,128)(2,1)}, u32[]{:S(2)}) copy-start(bf16[2048,512]{1,0:T(8,128)(2,1)} %w_ref.5) | copy-start | bytes 6291460
  11.2 10.3 %collective-permute-start.3 = (bf16[128,256]{1,0:T(8,128)(2,1)S(1)}, bf16[128,256]{1,0:T(8,128)(2,1)S(1)}, u32[]{:S(2)}, u32[]{:S(2)}) collective-permute-start(bf16[128,256]{1,0:T(8,128)(2,1)S(1)} %get-tuple-element.23), channel_id=1, source_target_pairs={{0,192},{64,128},{128,64},{192,0},{1,193},{65,129},{129,65},{193,1... | collective-permute-start | bytes 196616 | tf_op jit(solution)/shard_map/ppermute | solution.py:258
  16.0 5.6 %collective-permute-start.2 = (bf16[16,2048]{1,0:T(8,128)(2,1)S(1)}, bf16[16,2048]{1,0:T(8,128)(2,1)S(1)}, u32[]{:S(2)}, u32[]{:S(2)}) collective-permute-start(bf16[16,2048]{1,0:T(8,128)(2,1)S(1)} %add.12), channel_id=1, source_target_pairs={{0,6},{1,7},{2,4},{3,5},{4,2},{5,3},{6,0},{7,1},{8,14},{9,15},{10,... | collective-permute-start | bytes 196616 | tf_op jit(solution)/shard_map/ppermute | solution.py:260
  18.3 5.2 %collective-permute-start.4 = (bf16[128,256]{1,0:T(8,128)(2,1)S(1)}, bf16[128,256]{1,0:T(8,128)(2,1)S(1)}, u32[]{:S(2)}, u32[]{:S(2)}) collective-permute-start(bf16[128,256]{1,0:T(8,128)(2,1)S(1)} %get-tuple-element.24), channel_id=1, source_target_pairs={{0,128},{64,192},{128,0},{192,64},{1,129},{65,193},{129,1},{193,65... | collective-permute-start | bytes 196616 | tf_op jit(solution)/shard_map/ppermute | solution.py:258
  18.3 5.3 %collective-permute-start.5 = (bf16[128,256]{1,0:T(8,128)(2,1)S(1)}, bf16[128,256]{1,0:T(8,128)(2,1)S(1)}, u32[]{:S(2)}, u32[]{:S(2)}) collective-permute-start(bf16[128,256]{1,0:T(8,128)(2,1)S(1)} %get-tuple-element.25), channel_id=1, source_target_pairs={{0,64},{64,0},{128,192},{192,128},{1,65},{65,1},{129,193},{193,129... | collective-permute-start | bytes 196616 | tf_op jit(solution)/shard_map/ppermute | solution.py:258
  23.9 1.3 %collective-permute-start.6 = (bf16[144,128]{1,0:T(8,128)(2,1)S(1)}, bf16[144,128]{1,0:T(8,128)(2,1)S(1)}, u32[]{:S(2)}, u32[]{:S(2)}) collective-permute-start(bf16[144,128]{1,0:T(8,128)(2,1)S(1)} %get-tuple-element.30), channel_id=1, source_target_pairs={{0,1},{1,0},{2,3},{3,2},{4,5},{5,4},{6,7},{7,6},{8,9},{9,8},{10,11... | collective-permute-start | bytes 110600 | tf_op jit(solution)/shard_map/ppermute | solution.py:260
  25.3 4.0 %collective-permute-start.9 = (bf16[144,128]{1,0:T(8,128)(2,1)S(1)}, bf16[144,128]{1,0:T(8,128)(2,1)S(1)}, u32[]{:S(2)}, u32[]{:S(2)}) collective-permute-start(bf16[144,128]{1,0:T(8,128)(2,1)S(1)} %get-tuple-element.33), channel_id=1, source_target_pairs={{0,2},{1,3},{2,0},{3,1},{4,6},{5,7},{6,4},{7,5},{8,10},{9,11},{10,... | collective-permute-start | bytes 110600 | tf_op jit(solution)/shard_map/ppermute | solution.py:260
  26.0 4.1 %collective-permute-start.8 = (bf16[144,128]{1,0:T(8,128)(2,1)S(1)}, bf16[144,128]{1,0:T(8,128)(2,1)S(1)}, u32[]{:S(2)}, u32[]{:S(2)}) collective-permute-start(bf16[144,128]{1,0:T(8,128)(2,1)S(1)} %get-tuple-element.33), channel_id=1, source_target_pairs={{0,64},{64,0},{128,192},{192,128},{1,65},{65,1},{129,193},{193,129... | collective-permute-start | bytes 110600 | tf_op jit(solution)/shard_map/ppermute | solution.py:258
  26.0 5.1 %collective-permute-start.7 = (bf16[144,128]{1,0:T(8,128)(2,1)S(1)}, bf16[144,128]{1,0:T(8,128)(2,1)S(1)}, u32[]{:S(2)}, u32[]{:S(2)}) collective-permute-start(bf16[144,128]{1,0:T(8,128)(2,1)S(1)} %get-tuple-element.33), channel_id=1, source_target_pairs={{0,66},{1,67},{2,64},{3,65},{4,70},{5,71},{6,68},{7,69},{64,2},{65... | collective-permute-start | bytes 110600 | tf_op jit(solution)/shard_map/ppermute | solution.py:265
  31.2 5.7 %collective-permute-start.12 = (bf16[144,128]{1,0:T(8,128)(2,1)S(1)}, bf16[144,128]{1,0:T(8,128)(2,1)S(1)}, u32[]{:S(2)}, u32[]{:S(2)}) collective-permute-start(bf16[144,128]{1,0:T(8,128)(2,1)S(1)} %get-tuple-element.36), channel_id=1, source_target_pairs={{0,6},{1,7},{2,4},{3,5},{4,2},{5,3},{6,0},{7,1},{8,14},{9,15},{10,... | collective-permute-start | bytes 110600 | tf_op jit(solution)/shard_map/ppermute | solution.py:260
  33.0 5.1 %collective-permute-start.11 = (bf16[144,128]{1,0:T(8,128)(2,1)S(1)}, bf16[144,128]{1,0:T(8,128)(2,1)S(1)}, u32[]{:S(2)}, u32[]{:S(2)}) collective-permute-start(bf16[144,128]{1,0:T(8,128)(2,1)S(1)} %get-tuple-element.36), channel_id=1, source_target_pairs={{0,128},{64,192},{128,0},{192,64},{1,129},{65,193},{129,1},{193,65... | collective-permute-start | bytes 110600 | tf_op jit(solution)/shard_map/ppermute | solution.py:258
  34.8 7.4 %collective-permute-start.10 = (bf16[144,128]{1,0:T(8,128)(2,1)S(1)}, bf16[144,128]{1,0:T(8,128)(2,1)S(1)}, u32[]{:S(2)}, u32[]{:S(2)}) collective-permute-start(bf16[144,128]{1,0:T(8,128)(2,1)S(1)} %get-tuple-element.36), channel_id=1, source_target_pairs={{0,134},{1,135},{2,132},{3,133},{4,130},{5,131},{6,128},{7,129},{6... | collective-permute-start | bytes 110600 | tf_op jit(solution)/shard_map/ppermute | solution.py:265
  42.3 1.3 %collective-permute-start.13 = (bf16[16,1024]{1,0:T(8,128)(2,1)S(1)}, bf16[16,1024]{1,0:T(8,128)(2,1)S(1)}, u32[]{:S(2)}, u32[]{:S(2)}) collective-permute-start(bf16[16,1024]{1,0:T(8,128)(2,1)S(1)} %join_far.1.mine_ref), channel_id=1, source_target_pairs={{0,1},{1,0},{2,3},{3,2},{4,5},{5,4},{6,7},{7,6},{8,9},{9,8},{10,11... | collective-permute-start | bytes 98312 | tf_op jit(solution)/shard_map/ppermute | solution.py:260

commit v3 on v2

--- a/solution.py
+++ b/solution.py
@@ -106,30 +106,49 @@
         outs[flips[turn]][...] = total.astype(BF)
 
 
+def place_kernel(mine_ref, other_ref, out_ref):
+    req_id = lax.axis_index("req")
+    place = lax.broadcasted_iota(jnp.int32, (NREQ, 2), 0)
+    row = lax.broadcasted_iota(jnp.int32, (NREQ, 2), 1)
+    mine = (place == req_id * 2 + row).astype(BF)
+    other = (place == (req_id ^ 1) * 2 + row).astype(BF)
+    placed = dot(mine, mine_ref[...], ((1,), (0,))) + dot(other, other_ref[...], ((1,), (0,)))
+    out_ref[...] = placed.astype(BF)
+
+
 def cached_kernel(
     owner_ref, slot_ref, len_ref, ctx_ref, q_ref, cache_ref, weighted_ref, stats_ref, live_ref
 ):
     sec_id, req_id = lax.axis_index("sec"), lax.axis_index("req")
-    queries = rows_of(q_ref[...])
     count = cache_ref.shape[1]
-    lane = lax.broadcasted_iota(jnp.int32, (count, LANES), 1) % NREQ
-    position = lax.broadcasted_iota(jnp.int32, (count, LANES), 0) + sec_id * count
-    first = req_id * 2
-    live0 = (lane == first) & (position < ctx_ref[0])
-    live1 = (lane == first + 1) & (position < ctx_ref[1])
-    live = live0 | live1
-    scores0 = dot(cache_ref[0, :, 0:HD], queries, ((1,), (1,)))
-    scores1 = dot(cache_ref[1, :, 0:HD], queries, ((1,), (1,)))
-    scores = jnp.where(live, jnp.where(lane == first, scores0, scores1) * FACTOR, LOW)
-    peak = jnp.max(scores, axis=0, keepdims=True)
-    weights = jnp.where(live, jnp.exp(scores - peak), 0.0)
-    total = jnp.sum(weights, axis=0, keepdims=True)
-    weights = weights.astype(BF)
-    zero = jnp.zeros_like(weights)
-    weighted_ref[...] = dot(
-        cache_ref[0, :, HD : 2 * HD], jnp.where(live0, weights, zero), ((0,), (0,))
-    ) + dot(cache_ref[1, :, HD : 2 * HD], jnp.where(live1, weights, zero), ((0,), (0,)))
-    stats_ref[...] = stat_rows(peak, total, 8)
+    position = lax.broadcasted_iota(jnp.int32, (GROUP, count), 1) + sec_id * count
+    lane = lax.broadcasted_iota(jnp.int32, (GROUP, LANES), 1)
+    head = lax.broadcasted_iota(jnp.int32, (GROUP, LANES), 0)
+    weighted = jnp.zeros((HD, LANES), F32)
+    peaks = jnp.full((1, LANES), LOW, F32)
+    totals = jnp.zeros((1, LANES), F32)
+    for slot in range(2):
+        queries = jnp.concatenate(
+            [q_ref[slot : slot + 1, h * HD : (h + 1) * HD] for h in range(GROUP)], axis=0
+        )
+        live = position < ctx_ref[slot]
+        scores = dot(queries, cache_ref[slot, :, 0:HD], ((1,), (1,))) * FACTOR
+        scores = jnp.where(live, scores, LOW)
+        peak = jnp.max(scores, axis=1, keepdims=True)
+        weights = jnp.where(live, jnp.exp(scores - peak), 0.0)
+        total = jnp.sum(weights, axis=1, keepdims=True)
+        summed = dot(weights.astype(BF), cache_ref[slot, :, HD : 2 * HD], ((1,), (0,)))
+        lane_of = lane == head * NREQ + req_id * 2 + slot
+        spread = lane_of.astype(BF)
+        high = summed.astype(BF)
+        low = (summed - high.astype(F32)).astype(BF)
+        weighted = weighted + dot(high, spread, ((0,), (0,))) + dot(low, spread, ((0,), (0,)))
+        peaks = jnp.maximum(
+            peaks, jnp.max(jnp.where(lane_of, peak, LOW), axis=0, keepdims=True)
+        )
+        totals = totals + jnp.sum(jnp.where(lane_of, total, 0.0), axis=0, keepdims=True)
+    weighted_ref[...] = weighted
+    stats_ref[...] = stat_rows(peaks, totals, 8)
     blocks = live_ref.shape[0] // BLK
     base = (req_id * lax.axis_size("sec") + sec_id) * blocks
     lane = lax.broadcasted_iota(jnp.int32, (BLK, LANES), 1) % NREQ
@@ -227,7 +246,7 @@
     return jax.ShapeDtypeStruct(dims, dtype)
 
 
-def call(kernel, ins, outs, name, flops=0, scratch=()):
+def call(kernel, ins, outs, name, flops=0, scratch=(), grant=32):
     moved = 0
     for _, value in ins:
         moved += value.size * value.dtype.itemsize
@@ -237,7 +256,7 @@
         in_specs=[spec for spec, _ in ins],
         out_specs=jax.tree.map(lambda _: vmem(), outs),
         scratch_shapes=scratch,
-        compiler_params=pltpu.CompilerParams(vmem_limit_bytes=32 * 1024 * 1024),
+        compiler_params=pltpu.CompilerParams(vmem_limit_bytes=grant * 1024 * 1024),
         cost_estimate=pl.CostEstimate(flops=flops, bytes_accessed=moved, transcendentals=0),
         name=name,
     )(*[value for _, value in ins])
@@ -264,16 +283,12 @@
                 pairs.append((i * req_count + j, (i ^ sec_flip) * req_count + (j ^ req_flip)))
         return lax.ppermute(value, ("sec", "req"), pairs)
 
-    tiled = jnp.tile(queries, (NREQ // 2, 1))
-    holder = lax.broadcasted_iota(jnp.int32, tiled.shape, 0) // 2
-    gathered = jnp.where(holder == req_id, tiled, jnp.zeros_like(tiled))
-    for flip in (1, 2, 6):
-        gathered = gathered + over(gathered, 0, flip)
-
     chunk = shape((rows, width), BF)
+    hbm = pl.BlockSpec(memory_space=pltpu.HBM)
+    other_queries = over(queries, 0, 1)
     chunks = call(
         kv_kernel,
-        [(pl.BlockSpec(memory_space=pltpu.HBM), prompt_x), (pl.BlockSpec(memory_space=pltpu.HBM), w_kv)],
+        [(hbm, prompt_x), (hbm, w_kv)],
         (chunk, chunk, chunk, chunk),
         "new_kv",
         flops=2 * prompt_x.size * width,
@@ -283,7 +298,18 @@
             pltpu.SemaphoreType.DMA((4,)),
             pltpu.SemaphoreType.DMA((4,)),
         ),
-    )
+        grant=52,
+    )
+    chunks, other_queries = lax.optimization_barrier((chunks, other_queries))
+
+    gathered = call(
+        place_kernel,
+        [(vmem(), queries), (vmem(), other_queries)],
+        shape((NREQ, queries.shape[1]), BF),
+        "place",
+    )
+    for flip in (2, 6):
+        gathered = gathered + over(gathered, 0, flip)
     arrived = [over(chunks[flip], flip, 0) for flip in (3, 2, 1)]
 
     cached = call(
@@ -293,7 +319,7 @@
             (smem(), blk_slot),
             (smem(), blk_len),
             (smem(), ctx_len),
-            (vmem(), tiled),
+            (vmem(), queries),
             (vmem(), cache[:, :, 0, :]),
         ],
         (shape((HD, LANES), F32), shape((8, LANES), F32), shape((rows, LANES), F32)),

time: 63.1 us -> 59.7 us (0.946)
  local copies, waits for them, and re-layouts: 4.6 us -> 0.06 us
  starting transfers between devices: 18.8 us -> 22.3 us
  waiting for transfers between devices: 13.5 us -> 10.1 us
  Pallas kernels: 6.61 us -> 7.98 us
    ppermute x5, starting transfers between devices: 7.16 us -> 11.8 us  [over(): lax.ppermute(value, 'sec', [(i, i ^ sec_flip) for i in range(sec_count)])]
    unnamed x16 -> x14, local copies, waits for them, and re-layouts: 3.81 us -> 0.03 us
    ppermute x5, waiting for transfers between devices: 3.92 us -> 1.89 us  [over(): lax.ppermute(value, 'sec', [(i, i ^ sec_flip) for i in range(sec_count)])]
    ppermute x7, waiting for transfers between devices: 4.44 us -> 2.61 us  [over(): lax.ppermute(value, 'req', [(i, i ^ req_flip) for i in range(req_count)])]
    pallas_call x8 -> x9, Pallas kernels: 6.61 us -> 7.98 us  [call(): pl.pallas_call(kernel, out_shape=outs, in_specs=[spec for spec, _ in ins]...]
    ppermute x7, starting transfers between devices: 6.73 us -> 5.86 us  [over(): lax.ppermute(value, 'req', [(i, i ^ req_flip) for i in range(req_count)])]
    another operation x2 -> x0, local copies, waits for them, and re-layouts: 0.77 us -> none  [on_device(): tiled = jnp.tile(queries, (NREQ // 2, 1))]
  transfers between devices with their start and end apart: 14 -> 14, of which waited for: 10 -> 8; matrix products, arithmetic and copies ran while one was open for 0% -> 0% of each run, Pallas kernels for 9% -> 12%
where the time goes in v3:
time: 59.7 us; the launch traced here: 58.9 us
  starting transfers between devices  22.3 us (37%)
  blocking collectives  17.6 us (29%)
  waiting for transfers between devices  10.1 us (17%)
  Pallas kernels  7.98 us (13%)
  other arithmetic  0.64 us (1%)
    all_to_all x1, blocking collectives, on_device(): pieces = lax.all_to_all(pieces, 'head', 0, 0, tiled=True)  17.6 us
    ppermute x5, starting transfers between devices, over(): lax.ppermute(value, 'sec', [(i, i ^ sec_flip) for i in range(sec_count)])  11.8 us
    pallas_call x9, Pallas kernels, call(): pl.pallas_call(kernel, out_shape=outs, in_specs=[spec for spec, _ in ins]...  7.98 us
    ppermute x7, starting transfers between devices, over(): lax.ppermute(value, 'req', [(i, i ^ req_flip) for i in range(req_count)])  5.86 us
    ppermute x2, waiting for transfers between devices, over(): return lax.ppermute(value, ('sec', 'req'), pairs)  5.6 us
    ppermute x2, starting transfers between devices, over(): return lax.ppermute(value, ('sec', 'req'), pairs)  4.6 us
    ppermute x7, waiting for transfers between devices, over(): lax.ppermute(value, 'req', [(i, i ^ req_flip) for i in range(req_count)])  2.61 us
    ppermute x5, waiting for transfers between devices, over(): lax.ppermute(value, 'sec', [(i, i ^ sec_flip) for i in range(sec_count)])  1.89 us
  transfers between devices with their start and end apart: 14, of which 8 were waited for; matrix products, arithmetic and copies ran while one was open for 0% of the time, Pallas kernels for 12%

profile of v3, /device:TPU:2, one launch (start us, length us, event | category | flops | bytes accessed | tf_op | source)
XLA Modules:
  0.0 58.9 jit_solution(8586252677607387745)
XLA Ops:
  0.0 0.0 copy-start.2
  0.0 0.0 copy-start.6
  0.0 0.0 copy-start.5
  0.0 0.0 copy-start.4
  0.0 0.0 copy-start.3
  0.0 0.0 copy-start.1
  0.0 0.1 collective-permute-start
  0.1 5.0 %new_kv.1 = (bf16[128,256]{1,0:T(8,128)(2,1)S(1)}, bf16[128,256]{1,0:T(8,128)(2,1)S(1)}, bf16[128,256]{1,0:T(8,128)(2,1)S(1)}, bf16[128,256]{1,0:T(8,128)(2,1)S(1)}) custom-call(bf16[512,4096]{1,0:T(8,128)(2,1)} %x_ref.1, bf16[4096,256]{1,0:T(8,128)(2,1)} %w_ref.3), custom_call_target="tpu_custom_call" | custom-call | flops 1073741824 | bytes 6291456 | tf_op jit(solution)/shard_map/new_kv/pallas_call | solution.py:253
  5.1 0.0 copy-start
  5.2 0.0 collective-permute-done.other_ref
  5.2 0.0 copy-done.2
  5.2 0.2 place.1
  5.3 1.7 %collective-permute-start.1 = (bf16[16,2048]{1,0:T(8,128)(2,1)S(1)}, bf16[16,2048]{1,0:T(8,128)(2,1)S(1)}, u32[]{:S(2)}, u32[]{:S(2)}) collective-permute-start(bf16[16,2048]{1,0:T(8,128)(2,1)S(1)} %place.1), channel_id=1, source_target_pairs={{0,2},{1,3},{2,0},{3,1},{4,6},{5,7},{6,4},{7,5},{8,10},{9,11},{10,... | collective-permute-start | bytes 196616 | tf_op jit(solution)/shard_map/ppermute | solution.py:279
  7.0 4.6 %collective-permute-start.3 = (bf16[128,256]{1,0:T(8,128)(2,1)S(1)}, bf16[128,256]{1,0:T(8,128)(2,1)S(1)}, u32[]{:S(2)}, u32[]{:S(2)}) collective-permute-start(bf16[128,256]{1,0:T(8,128)(2,1)S(1)} %get-tuple-element.33), channel_id=1, source_target_pairs={{0,192},{64,128},{128,64},{192,0},{1,193},{65,129},{129,65},{193,1... | collective-permute-start | bytes 196616 | tf_op jit(solution)/shard_map/ppermute | solution.py:277
  11.7 0.0 collective-permute-done.1
  11.7 2.3 %collective-permute-start.2 = (bf16[16,2048]{1,0:T(8,128)(2,1)S(1)}, bf16[16,2048]{1,0:T(8,128)(2,1)S(1)}, u32[]{:S(2)}, u32[]{:S(2)}) collective-permute-start(bf16[16,2048]{1,0:T(8,128)(2,1)S(1)} %add.6), channel_id=1, source_target_pairs={{0,6},{1,7},{2,4},{3,5},{4,2},{5,3},{6,0},{7,1},{8,14},{9,15},{10,... | collective-permute-start | bytes 196616 | tf_op jit(solution)/shard_map/ppermute | solution.py:279
  14.0 2.3 %collective-permute-start.4 = (bf16[128,256]{1,0:T(8,128)(2,1)S(1)}, bf16[128,256]{1,0:T(8,128)(2,1)S(1)}, u32[]{:S(2)}, u32[]{:S(2)}) collective-permute-start(bf16[128,256]{1,0:T(8,128)(2,1)S(1)} %get-tuple-element.34), channel_id=1, source_target_pairs={{0,128},{64,192},{128,0},{192,64},{1,129},{65,193},{129,1},{193,65... | collective-permute-start | bytes 196616 | tf_op jit(solution)/shard_map/ppermute | solution.py:277
  16.2 1.9 %collective-permute-start.5 = (bf16[128,256]{1,0:T(8,128)(2,1)S(1)}, bf16[128,256]{1,0:T(8,128)(2,1)S(1)}, u32[]{:S(2)}, u32[]{:S(2)}) collective-permute-start(bf16[128,256]{1,0:T(8,128)(2,1)S(1)} %get-tuple-element.35), channel_id=1, source_target_pairs={{0,64},{64,0},{128,192},{192,128},{1,65},{65,1},{129,193},{193,129... | collective-permute-start | bytes 196616 | tf_op jit(solution)/shard_map/ppermute | solution.py:277
  18.1 0.0 copy-done.6
  18.1 0.0 copy-done.5
  18.1 0.0 copy-done.4
  18.1 0.0 copy-done.3
  18.1 0.0 copy-done.1
  18.2 1.7 %cached.1 = (f32[128,256]{1,0:T(8,128)S(1)}, f32[8,256]{1,0:T(8,128)S(1)}, f32[128,256]{1,0:T(8,128)S(1)}) custom-call(s32[256]{0:T(256)S(1)} %bitcast.3, s32[256]{0:T(256)S(1)} %copy-done.4, s32[256]{0:T(256)S(1)} %copy-done.5, s32[2]{0:T(128)S(1)} %copy-done.6, bf16[2,2048]{1,0:T(2,128)(2,1)S(1)} %copy-done.2, bf16[2,1024,256]{2,1,0:T(8,128)(2,1)S(1)} %bitcast.2), custom_call_target="tpu_custom_call" | custom-call | flops 268435456 | bytes 1059848 | tf_op jit(solution)/shard_map/cached/pallas_call | solution.py:253
  19.9 0.0 collective-permute-done.2
  19.9 0.0 collective-permute-done.3.a_ref
  20.0 0.0 collective-permute-done.4.b_ref
  20.0 0.5 collective-permute-done.5.c_ref
  20.5 0.4 prompt.1
  20.9 0.1 collective-permute-start.6
  21.0 1.2 %collective-permute-done.6.refs_0_ = bf16[144,128]{1,0:T(8,128)(2,1)S(1)} collective-permute-done((bf16[144,128]{1,0:T(8,128)(2,1)S(1)}, bf16[144,128]{1,0:T(8,128)(2,1)S(1)}, u32[]{:S(2)}, u32[]{:S(2)}) %collective-permute-start.6) | collective-permute-done | bytes 36896 | tf_op jit(solution)/shard_map/ppermute | solution.py:279
  22.2 0.5 collective-permute-start.9
  22.7 1.7 %collective-permute-start.8 = (bf16[144,128]{1,0:T(8,128)(2,1)S(1)}, bf16[144,128]{1,0:T(8,128)(2,1)S(1)}, u32[]{:S(2)}, u32[]{:S(2)}) collective-permute-start(bf16[144,128]{1,0:T(8,128)(2,1)S(1)} %get-tuple-element.43), channel_id=1, source_target_pairs={{0,64},{64,0},{128,192},{192,128},{1,65},{65,1},{129,193},{193,129... | collective-permute-start | bytes 110600 | tf_op jit(solution)/shard_map/ppermute | solution.py:277
  24.4 1.4 %collective-permute-start.7 = (bf16[144,128]{1,0:T(8,128)(2,1)S(1)}, bf16[144,128]{1,0:T(8,128)(2,1)S(1)}, u32[]{:S(2)}, u32[]{:S(2)}) collective-permute-start(bf16[144,128]{1,0:T(8,128)(2,1)S(1)} %get-tuple-element.43), channel_id=1, source_target_pairs={{0,66},{1,67},{2,64},{3,65},{4,70},{5,71},{6,68},{7,69},{64,2},{65... | collective-permute-start | bytes 110600 | tf_op jit(solution)/shard_map/ppermute | solution.py:284
  25.8 0.5 collective-permute-done.9.refs_2_
  26.3 0.4 collective-permute-done.8.refs_1_
  26.7 2.5 %collective-permute-done.7.refs_0_ = bf16[144,128]{1,0:T(8,128)(2,1)S(1)} collective-permute-done((bf16[144,128]{1,0:T(8,128)(2,1)S(1)}, bf16[144,128]{1,0:T(8,128)(2,1)S(1)}, u32[]{:S(2)}, u32[]{:S(2)}) %collective-permute-start.7) | collective-permute-done | bytes 36896 | tf_op jit(solution)/shard_map/ppermute | solution.py:284
  29.2 0.1 join_near.1
  29.3 1.1 %collective-permute-start.12 = (bf16[144,128]{1,0:T(8,128)(2,1)S(1)}, bf16[144,128]{1,0:T(8,128)(2,1)S(1)}, u32[]{:S(2)}, u32[]{:S(2)}) collective-permute-start(bf16[144,128]{1,0:T(8,128)(2,1)S(1)} %get-tuple-element.46), channel_id=1, source_target_pairs={{0,6},{1,7},{2,4},{3,5},{4,2},{5,3},{6,0},{7,1},{8,14},{9,15},{10,... | collective-permute-start | bytes 110600 | tf_op jit(solution)/shard_map/ppermute | solution.py:279
  30.4 1.4 %collective-permute-start.11 = (bf16[144,128]{1,0:T(8,128)(2,1)S(1)}, bf16[144,128]{1,0:T(8,128)(2,1)S(1)}, u32[]{:S(2)}, u32[]{:S(2)}) collective-permute-start(bf16[144,128]{1,0:T(8,128)(2,1)S(1)} %get-tuple-element.46), channel_id=1, source_target_pairs={{0,128},{64,192},{128,0},{192,64},{1,129},{65,193},{129,1},{193,65... | collective-permute-start | bytes 110600 | tf_op jit(solution)/shard_map/ppermute | solution.py:277
  31.8 3.2 %collective-permute-start.10 = (bf16[144,128]{1,0:T(8,128)(2,1)S(1)}, bf16[144,128]{1,0:T(8,128)(2,1)S(1)}, u32[]{:S(2)}, u32[]{:S(2)}) collective-permute-start(bf16[144,128]{1,0:T(8,128)(2,1)S(1)} %get-tuple-element.46), channel_id=1, source_target_pairs={{0,134},{1,135},{2,132},{3,133},{4,130},{5,131},{6,128},{7,129},{6... | collective-permute-start | bytes 110600 | tf_op jit(solution)/shard_map/ppermute | solution.py:284
  35.0 0.0 collective-permute-done.12.refs_2_
  35.0 1.0 %collective-permute-done.11.refs_1_ = bf16[144,128]{1,0:T(8,128)(2,1)S(1)} collective-permute-done((bf16[144,128]{1,0:T(8,128)(2,1)S(1)}, bf16[144,128]{1,0:T(8,128)(2,1)S(1)}, u32[]{:S(2)}, u32[]{:S(2)}) %collective-permute-start.11) | collective-permute-done | bytes 36896 | tf_op jit(solution)/shard_map/ppermute | solution.py:277
  35.9 3.0 %collective-permute-done.10.refs_0_ = bf16[144,128]{1,0:T(8,128)(2,1)S(1)} collective-permute-done((bf16[144,128]{1,0:T(8,128)(2,1)S(1)}, bf16[144,128]{1,0:T(8,128)(2,1)S(1)}, u32[]{:S(2)}, u32[]{:S(2)}) %collective-permute-start.10) | collective-permute-done | bytes 36896 | tf_op jit(solution)/shard_map/ppermute | solution.py:284
  39.0 0.1 join_far.1.mine_ref
  39.1 0.1 collective-permute-start.13
  39.2 0.0 copy-done
  39.2 0.3 project_mine.1.so_far_ref
  39.5 0.9 %collective-permute-done.13.other_ref = bf16[16,1024]{1,0:T(8,128)(2,1)S(1)} collective-permute-done((bf16[16,1024]{1,0:T(8,128)(2,1)S(1)}, bf16[16,1024]{1,0:T(8,128)(2,1)S(1)}, u32[]{:S(2)}, u32[]{:S(2)}) %collective-permute-start.13) | collective-permute-done | bytes 32800 | tf_op jit(solution)/shard_map/ppermute | solution.py:279
  40.4 0.2 project_other.1
  40.7 17.6 %all_to_all.5 = bf16[8,2,512]{2,1,0:T(2,128)(2,1)S(1)} all-to-all(bf16[8,2,512]{2,1,0:T(2,128)(2,1)S(1)} %reshape.3), channel_id=1, replica_groups=mesh['sec'=4,'head'=8,'req'=8] {'head'}, dimensions={0} | all-to-all | bytes 32768 | tf_op jit(solution)/shard_map/all_to_all | solution.py:375
  58.3 0.6 %reduce_sum.12 = bf16[2,512]{1,0:T(2,128)(2,1)} reduce(bf16[8,2,512]{2,1,0:T(2,128)(2,1)S(1)} %all_to_all.5, bf16[]{:T(256)} %constant.2.clone.1), dimensions={0}, to_apply=%region_0.0 | reduce | flops 7168 | bytes 18434 | tf_op jit(solution)/shard_map/reduce_sum | solution.py:376
  (4 shorter events, 0.1 us)
Async XLA Ops:
  0.0 5.2 %copy-start.2 = (bf16[2,2048]{1,0:T(2,128)(2,1)S(1)}, bf16[2,2048]{1,0:T(2,128)(2,1)}, u32[]{:S(2)}) copy-start(bf16[2,2048]{1,0:T(2,128)(2,1)} %q_ref.1) | copy-start | bytes 24580
  0.0 18.1 %copy-start.6 = (s32[2]{0:T(128)S(1)}, s32[2]{0:T(128)}, u32[]{:S(2)}) copy-start(s32[2]{0:T(128)} %ctx_ref.1) | copy-start | bytes 28
  0.0 18.1 %copy-start.5 = (s32[256]{0:T(256)S(1)}, s32[256]{0:T(256)}, u32[]{:S(2)}) copy-start(s32[256]{0:T(256)} %len_ref.1) | copy-start | bytes 3076
  0.0 18.1 %copy-start.4 = (s32[256]{0:T(256)S(1)}, s32[256]{0:T(256)}, u32[]{:S(2)}) copy-start(s32[256]{0:T(256)} %slot_ref.1) | copy-start | bytes 3076
  0.0 18.1 %copy-start.3 = (s32[256,1]{0,1:T(1,128)S(1)}, s32[256,1]{0,1:T(1,128)}, u32[]{:S(2)}) copy-start(s32[256,1]{0,1:T(1,128)} %param.14) | copy-start | bytes 3076
  0.0 18.1 %copy-start.1 = (bf16[2,1024,1,256]{3,1,2,0:T(8,128)(2,1)S(1)}, bf16[2,1024,1,256]{3,1,2,0:T(8,128)(2,1)}, u32[]{:S(2)}) copy-start(bf16[2,1024,1,256]{3,1,2,0:T(8,128)(2,1)} %param.12) | copy-start | bytes 3145732
  0.0 5.1 %collective-permute-start = (bf16[2,2048]{1,0:T(2,128)(2,1)}, bf16[2,2048]{1,0:T(2,128)(2,1)S(1)}, u32[]{:S(2)}, u32[]{:S(2)}) collective-permute-start(bf16[2,2048]{1,0:T(2,128)(2,1)} %q_ref.1), channel_id=1, source_target_pairs={{0,1},{1,0},{2,3},{3,2},{4,5},{5,4},{6,7},{7,6},{8,9},{9,8},{10,11... | collective-permute-start | bytes 24584 | tf_op jit(solution)/shard_map/ppermute | solution.py:279
  5.1 34.1 %copy-start = (bf16[2048,512]{1,0:T(8,128)(2,1)S(1)}, bf16[2048,512]{1,0:T(8,128)(2,1)}, u32[]{:S(2)}) copy-start(bf16[2048,512]{1,0:T(8,128)(2,1)} %w_ref.5) | copy-start | bytes 6291460
  5.3 6.3 %collective-permute-start.1 = (bf16[16,2048]{1,0:T(8,128)(2,1)S(1)}, bf16[16,2048]{1,0:T(8,128)(2,1)S(1)}, u32[]{:S(2)}, u32[]{:S(2)}) collective-permute-start(bf16[16,2048]{1,0:T(8,128)(2,1)S(1)} %place.1), channel_id=1, source_target_pairs={{0,2},{1,3},{2,0},{3,1},{4,6},{5,7},{6,4},{7,5},{8,10},{9,11},{10,... | collective-permute-start | bytes 196616 | tf_op jit(solution)/shard_map/ppermute | solution.py:279
  7.0 12.9 %collective-permute-start.3 = (bf16[128,256]{1,0:T(8,128)(2,1)S(1)}, bf16[128,256]{1,0:T(8,128)(2,1)S(1)}, u32[]{:S(2)}, u32[]{:S(2)}) collective-permute-start(bf16[128,256]{1,0:T(8,128)(2,1)S(1)} %get-tuple-element.33), channel_id=1, source_target_pairs={{0,192},{64,128},{128,64},{192,0},{1,193},{65,129},{129,65},{193,1... | collective-permute-start | bytes 196616 | tf_op jit(solution)/shard_map/ppermute | solution.py:277
  11.7 8.2 %collective-permute-start.2 = (bf16[16,2048]{1,0:T(8,128)(2,1)S(1)}, bf16[16,2048]{1,0:T(8,128)(2,1)S(1)}, u32[]{:S(2)}, u32[]{:S(2)}) collective-permute-start(bf16[16,2048]{1,0:T(8,128)(2,1)S(1)} %add.6), channel_id=1, source_target_pairs={{0,6},{1,7},{2,4},{3,5},{4,2},{5,3},{6,0},{7,1},{8,14},{9,15},{10,... | collective-permute-start | bytes 196616 | tf_op jit(solution)/shard_map/ppermute | solution.py:279
  14.0 6.0 %collective-permute-start.4 = (bf16[128,256]{1,0:T(8,128)(2,1)S(1)}, bf16[128,256]{1,0:T(8,128)(2,1)S(1)}, u32[]{:S(2)}, u32[]{:S(2)}) collective-permute-start(bf16[128,256]{1,0:T(8,128)(2,1)S(1)} %get-tuple-element.34), channel_id=1, source_target_pairs={{0,128},{64,192},{128,0},{192,64},{1,129},{65,193},{129,1},{193,65... | collective-permute-start | bytes 196616 | tf_op jit(solution)/shard_map/ppermute | solution.py:277
  16.2 4.3 %collective-permute-start.5 = (bf16[128,256]{1,0:T(8,128)(2,1)S(1)}, bf16[128,256]{1,0:T(8,128)(2,1)S(1)}, u32[]{:S(2)}, u32[]{:S(2)}) collective-permute-start(bf16[128,256]{1,0:T(8,128)(2,1)S(1)} %get-tuple-element.35), channel_id=1, source_target_pairs={{0,64},{64,0},{128,192},{192,128},{1,65},{65,1},{129,193},{193,129... | collective-permute-start | bytes 196616 | tf_op jit(solution)/shard_map/ppermute | solution.py:277
  20.9 1.3 %collective-permute-start.6 = (bf16[144,128]{1,0:T(8,128)(2,1)S(1)}, bf16[144,128]{1,0:T(8,128)(2,1)S(1)}, u32[]{:S(2)}, u32[]{:S(2)}) collective-permute-start(bf16[144,128]{1,0:T(8,128)(2,1)S(1)} %get-tuple-element.40), channel_id=1, source_target_pairs={{0,1},{1,0},{2,3},{3,2},{4,5},{5,4},{6,7},{7,6},{8,9},{9,8},{10,11... | collective-permute-start | bytes 110600 | tf_op jit(solution)/shard_map/ppermute | solution.py:279
  22.2 4.0 %collective-permute-start.9 = (bf16[144,128]{1,0:T(8,128)(2,1)S(1)}, bf16[144,128]{1,0:T(8,128)(2,1)S(1)}, u32[]{:S(2)}, u32[]{:S(2)}) collective-permute-start(bf16[144,128]{1,0:T(8,128)(2,1)S(1)} %get-tuple-element.43), channel_id=1, source_target_pairs={{0,2},{1,3},{2,0},{3,1},{4,6},{5,7},{6,4},{7,5},{8,10},{9,11},{10,... | collective-permute-start | bytes 110600 | tf_op jit(solution)/shard_map/ppermute | solution.py:279
  22.7 4.0 %collective-permute-start.8 = (bf16[144,128]{1,0:T(8,128)(2,1)S(1)}, bf16[144,128]{1,0:T(8,128)(2,1)S(1)}, u32[]{:S(2)}, u32[]{:S(2)}) collective-permute-start(bf16[144,128]{1,0:T(8,128)(2,1)S(1)} %get-tuple-element.43), channel_id=1, source_target_pairs={{0,64},{64,0},{128,192},{192,128},{1,65},{65,1},{129,193},{193,129... | collective-permute-start | bytes 110600 | tf_op jit(solution)/shard_map/ppermute | solution.py:277
  24.4 4.9 %collective-permute-start.7 = (bf16[144,128]{1,0:T(8,128)(2,1)S(1)}, bf16[144,128]{1,0:T(8,128)(2,1)S(1)}, u32[]{:S(2)}, u32[]{:S(2)}) collective-permute-start(bf16[144,128]{1,0:T(8,128)(2,1)S(1)} %get-tuple-element.43), channel_id=1, source_target_pairs={{0,66},{1,67},{2,64},{3,65},{4,70},{5,71},{6,68},{7,69},{64,2},{65... | collective-permute-start | bytes 110600 | tf_op jit(solution)/shard_map/ppermute | solution.py:284
  29.3 5.7 %collective-permute-start.12 = (bf16[144,128]{1,0:T(8,128)(2,1)S(1)}, bf16[144,128]{1,0:T(8,128)(2,1)S(1)}, u32[]{:S(2)}, u32[]{:S(2)}) collective-permute-start(bf16[144,128]{1,0:T(8,128)(2,1)S(1)} %get-tuple-element.46), channel_id=1, source_target_pairs={{0,6},{1,7},{2,4},{3,5},{4,2},{5,3},{6,0},{7,1},{8,14},{9,15},{10,... | collective-permute-start | bytes 110600 | tf_op jit(solution)/shard_map/ppermute | solution.py:279
  30.4 5.5 %collective-permute-start.11 = (bf16[144,128]{1,0:T(8,128)(2,1)S(1)}, bf16[144,128]{1,0:T(8,128)(2,1)S(1)}, u32[]{:S(2)}, u32[]{:S(2)}) collective-permute-start(bf16[144,128]{1,0:T(8,128)(2,1)S(1)} %get-tuple-element.46), channel_id=1, source_target_pairs={{0,128},{64,192},{128,0},{192,64},{1,129},{65,193},{129,1},{193,65... | collective-permute-start | bytes 110600 | tf_op jit(solution)/shard_map/ppermute | solution.py:277
  31.8 7.2 %collective-permute-start.10 = (bf16[144,128]{1,0:T(8,128)(2,1)S(1)}, bf16[144,128]{1,0:T(8,128)(2,1)S(1)}, u32[]{:S(2)}, u32[]{:S(2)}) collective-permute-start(bf16[144,128]{1,0:T(8,128)(2,1)S(1)} %get-tuple-element.46), channel_id=1, source_target_pairs={{0,134},{1,135},{2,132},{3,133},{4,130},{5,131},{6,128},{7,129},{6... | collective-permute-start | bytes 110600 | tf_op jit(solution)/shard_map/ppermute | solution.py:284
  39.1 1.3 %collective-permute-start.13 = (bf16[16,1024]{1,0:T(8,128)(2,1)S(1)}, bf16[16,1024]{1,0:T(8,128)(2,1)S(1)}, u32[]{:S(2)}, u32[]{:S(2)}) collective-permute-start(bf16[16,1024]{1,0:T(8,128)(2,1)S(1)} %join_far.1.mine_ref), channel_id=1, source_target_pairs={{0,1},{1,0},{2,3},{3,2},{4,5},{5,4},{6,7},{7,6},{8,9},{9,8},{10,11... | collective-permute-start | bytes 98312 | tf_op jit(solution)/shard_map/ppermute | solution.py:279

commit v4 on v3

--- a/solution.py
+++ b/solution.py
@@ -12,7 +12,6 @@
 GROUP = 16
 NREQ = 16
 LANES = GROUP * NREQ
-HALF = LANES // 2
 STAT = 16
 LOW = -1e30
 FACTOR = 1.0 / math.sqrt(HD)
@@ -67,53 +66,27 @@
     ref[HD : HD + STAT, :] = packed_stats(peak, total)
 
 
-def kv_kernel(x_ref, w_ref, out0, out1, out2, out3, x_buf, w_buf, x_sem, w_sem):
-    me = lax.axis_index("sec")
+def kv_kernel(x_ref, w_ref, out0, out1, out2, out3, x_buf, w_buf, sems):
+    sec_id = lax.axis_index("sec")
     rows = out0.shape[0]
-    parts = w_sem.shape[0]
-    depth = w_ref.shape[0] // parts
-    flips = (3, 2, 1, 0)
-    outs = (out0, out1, out2, out3)
-
-    def x_copy(turn):
-        start = pl.multiple_of((me ^ flips[turn]) * rows, rows)
-        return pltpu.make_async_copy(
-            x_ref.at[pl.ds(start, rows), :],
-            x_buf.at[pl.ds(turn * rows, rows), :],
-            x_sem.at[turn],
-        )
-
-    def w_copy(part):
-        span = pl.ds(part * depth, depth)
-        return pltpu.make_async_copy(w_ref.at[span, :], w_buf.at[span, :], w_sem.at[part])
-
-    x_copy(0).start()
-    for part in range(parts):
-        w_copy(part).start()
-    for turn in range(1, 4):
-        x_copy(turn).start()
-    for turn in range(4):
-        x_copy(turn).wait()
-        mine = x_buf[turn * rows : (turn + 1) * rows, :]
-        if turn == 0:
-            total = jnp.zeros(out0.shape, F32)
-            for part in range(parts):
-                w_copy(part).wait()
-                span = slice(part * depth, (part + 1) * depth)
-                total = total + dot(mine[:, span], w_buf[span, :], ((1,), (0,)))
-        else:
-            total = dot(mine, w_buf[...], ((1,), (0,)))
-        outs[flips[turn]][...] = total.astype(BF)
-
-
-def place_kernel(mine_ref, other_ref, out_ref):
-    req_id = lax.axis_index("req")
-    place = lax.broadcasted_iota(jnp.int32, (NREQ, 2), 0)
-    row = lax.broadcasted_iota(jnp.int32, (NREQ, 2), 1)
-    mine = (place == req_id * 2 + row).astype(BF)
-    other = (place == (req_id ^ 1) * 2 + row).astype(BF)
-    placed = dot(mine, mine_ref[...], ((1,), (0,))) + dot(other, other_ref[...], ((1,), (0,)))
-    out_ref[...] = placed.astype(BF)
+    copies = (
+        pltpu.make_async_copy(w_ref, w_buf, sems.at[0]),
+        pltpu.make_async_copy(x_ref, x_buf, sems.at[1]),
+    )
+    for copy in copies:
+        copy.start()
+    for copy in copies:
+        copy.wait()
+    for flip, out in enumerate((out0, out1, out2, out3)):
+        start = pl.multiple_of((sec_id ^ flip) * rows, rows)
+        out[...] = dot(x_buf[pl.ds(start, rows), :], w_buf[...], ((1,), (0,))).astype(BF)
+
+
+def sum_kernel(own_ref, a_ref, b_ref, c_ref, out_ref):
+    summed = (own_ref[...].astype(F32) + a_ref[...].astype(F32)) + (
+        b_ref[...].astype(F32) + c_ref[...].astype(F32)
+    )
+    out_ref[...] = summed.astype(BF)
 
 
 def cached_kernel(
@@ -159,13 +132,18 @@
         live_ref[block * BLK : (block + 1) * BLK, :] = live_block.astype(F32)
 
 
-def prompt_kernel(
-    q_ref, live_ref, own_ref, a_ref, b_ref, c_ref, cw_ref, cs_ref, kw_ref, ks_ref, send_ref
-):
-    summed = (own_ref[...].astype(F32) + a_ref[...].astype(F32)) + (
-        b_ref[...].astype(F32) + c_ref[...].astype(F32)
-    )
-    new_kv = summed.astype(BF)
+def place_kernel(mine_ref, other_ref, out_ref):
+    req_id = lax.axis_index("req")
+    place = lax.broadcasted_iota(jnp.int32, (NREQ, 2), 0)
+    row = lax.broadcasted_iota(jnp.int32, (NREQ, 2), 1)
+    mine = (place == req_id * 2 + row).astype(BF)
+    other = (place == (req_id ^ 1) * 2 + row).astype(BF)
+    placed = dot(mine, mine_ref[...], ((1,), (0,))) + dot(other, other_ref[...], ((1,), (0,)))
+    out_ref[...] = placed.astype(BF)
+
+
+def prompt_kernel(q_ref, live_ref, kv_ref, cw_ref, cs_ref, kw_ref, ks_ref, send_ref):
+    new_kv = kv_ref[...]
     queries = rows_of(q_ref[...])
     live = live_ref[...] > 0.5
     scores = dot(new_kv[:, 0:HD], queries, ((1,), (1,))) * FACTOR
@@ -179,19 +157,9 @@
     scale, cached_scale = jnp.exp(peak - joint), jnp.exp(cached_peak - joint)
     weighted = weighted * scale + cw_ref[...] * cached_scale
     total = total * scale + cached_total * cached_scale
-    core = lax.axis_index("req") % 2
-
-    @pl.when(core == 0)
-    def _():
-        kw_ref[...] = weighted[:, :HALF]
-        ks_ref[...] = stat_rows(joint[:, :HALF], total[:, :HALF], 8)
-        store_packed(send_ref, weighted[:, HALF:], joint[:, HALF:], total[:, HALF:])
-
-    @pl.when(core == 1)
-    def _():
-        kw_ref[...] = weighted[:, HALF:]
-        ks_ref[...] = stat_rows(joint[:, HALF:], total[:, HALF:], 8)
-        store_packed(send_ref, weighted[:, :HALF], joint[:, :HALF], total[:, :HALF])
+    kw_ref[...] = weighted
+    ks_ref[...] = stat_rows(joint, total, 8)
+    store_packed(send_ref, weighted, joint, total)
 
 
 def joined(w_ref, s_ref, got_refs):
@@ -219,27 +187,13 @@
     store_packed(send_ref, weighted, peak, total)
 
 
-def last_kernel(w_ref, s_ref, *refs):
+def project_kernel(w_ref, s_ref, out_w_ref, *refs):
     weighted, _, total = joined(w_ref, s_ref, refs[:-1])
-    rows = (weighted / total).T
-    for h in range(GROUP // 2):
-        refs[-1][:, h * HD : (h + 1) * HD] = rows[h * NREQ : (h + 1) * NREQ, :].astype(BF)
-
-
-def half_rows(w_ref, core):
-    half = w_ref.shape[0] // 2
-    return w_ref[pl.ds(pl.multiple_of(core * half, half), half), :]
-
-
-def first_half_kernel(mine_ref, w_ref, out_ref):
-    core = lax.axis_index("req") % 2
-    out_ref[...] = dot(mine_ref[...], half_rows(w_ref, core), ((1,), (0,)))
-
-
-def second_half_kernel(other_ref, w_ref, so_far_ref, out_ref):
-    core = lax.axis_index("req") % 2
-    more = dot(other_ref[...], half_rows(w_ref, 1 - core), ((1,), (0,)))
-    out_ref[...] = (so_far_ref[...] + more).astype(BF)
+    rows = (weighted / total).T.astype(BF)
+    attended = jnp.concatenate(
+        [rows[h * NREQ : (h + 1) * NREQ, :] for h in range(GROUP)], axis=1
+    )
+    refs[-1][...] = dot(attended, out_w_ref[...], ((1,), (0,))).astype(BF)
 
 
 def shape(dims, dtype):
@@ -262,7 +216,7 @@
     )(*[value for _, value in ins])
 
 
-STATE = (shape((HD, HALF), F32), shape((8, HALF), F32), shape((HD + STAT, HALF), BF))
+STATE = (shape((HD, LANES), F32), shape((8, LANES), F32), shape((HD + STAT, LANES), BF))
 
 
 def on_device(prompt_x, w_kv, queries, cache, w_out, blk_owner, blk_slot, blk_len, ctx_len):
@@ -295,8 +249,7 @@
         scratch=(
             pltpu.VMEM(prompt_x.shape, BF),
             pltpu.VMEM(w_kv.shape, BF),
-            pltpu.SemaphoreType.DMA((4,)),
-            pltpu.SemaphoreType.DMA((4,)),
+            pltpu.SemaphoreType.DMA((2,)),
         ),
         grant=52,
     )
@@ -308,11 +261,10 @@
         shape((NREQ, queries.shape[1]), BF),
         "place",
     )
-    for flip in (2, 6):
-        gathered = gathered + over(gathered, 0, flip)
+    gathered = gathered + over(gathered, 0, 2)
     arrived = [over(chunks[flip], flip, 0) for flip in (3, 2, 1)]
-
-    cached = call(
+    gathered = gathered + over(gathered, 0, 6)
+    cached_weighted, cached_stats, live = call(
         cached_kernel,
         [
             (smem(), blk_owner[:, 0]),
@@ -326,49 +278,34 @@
         "cached",
         flops=2 * 4 * cache.shape[1] * HD * LANES,
     )
+    new_kv = call(
+        sum_kernel, [(vmem(), value) for value in (chunks[0], *arrived)], chunk, "kv_sum"
+    )
     kept = call(
         prompt_kernel,
         [
-            (vmem(), value)
-            for value in (gathered, cached[2], chunks[0], *arrived, cached[0], cached[1])
+            (vmem(), value) for value in (gathered, live, new_kv, cached_weighted, cached_stats)
         ],
         STATE,
         "prompt",
         flops=2 * 2 * rows * HD * LANES,
     )
-    kept = call(
-        join_kernel,
-        [(vmem(), value) for value in (kept[0], kept[1], over(kept[2], 0, 1))],
-        STATE,
-        "join_core",
-    )
-    got = [over(kept[2], *flips) for flips in ((1, 2), (1, 0), (0, 2))]
-    kept = call(
-        join_kernel, [(vmem(), value) for value in (kept[0], kept[1], *got)], STATE, "join_near"
-    )
+    for name, moves in (
+        ("join_core", ((0, 1),)),
+        ("join_near", ((1, 2), (1, 0), (0, 2))),
+    ):
+        got = [over(kept[2], *flips) for flips in moves]
+        kept = call(
+            join_kernel, [(vmem(), value) for value in (kept[0], kept[1], *got)], STATE, name
+        )
     got = [over(kept[2], *flips) for flips in ((2, 6), (2, 0), (0, 6))]
-    mine = call(
-        last_kernel,
-        [(vmem(), value) for value in (kept[0], kept[1], *got)],
-        shape((NREQ, HALF // NREQ * HD), BF),
-        "join_far",
-    )
-    other = over(mine, 0, 1)
     columns = w_out.shape[1]
-    flops = w_out.size * NREQ
-    so_far = call(
-        first_half_kernel,
-        [(vmem(), mine), (vmem(), w_out)],
-        shape((NREQ, columns), F32),
-        "project_mine",
-        flops=flops,
-    )
     partial_out = call(
-        second_half_kernel,
-        [(vmem(), other), (vmem(), w_out), (vmem(), so_far)],
+        project_kernel,
+        [(vmem(), value) for value in (kept[0], kept[1], w_out, *got)],
         shape((NREQ, columns), BF),
-        "project_other",
-        flops=flops,
+        "join_far_project",
+        flops=2 * w_out.size * NREQ,
     )
     head_count = lax.axis_size("head")
     pieces = partial_out.reshape(head_count, NREQ // head_count, columns)

time: 59.7 us -> 58.3 us (0.977); the launches traced: 58.9 us -> 58.2 us
  starting transfers between devices: 22.3 us -> 18.6 us
  waiting for transfers between devices: 10.1 us -> 12.9 us
  blocking collectives: 17.6 us -> 18.6 us
  Pallas kernels: 7.98 us -> 7.12 us
    ppermute x5, waiting for transfers between devices: 1.89 us -> 4.81 us  [over(): lax.ppermute(value, 'sec', [(i, i ^ sec_flip) for i in range(sec_count)])]
    ppermute x5, starting transfers between devices: 11.8 us -> 9.1 us  [over(): lax.ppermute(value, 'sec', [(i, i ^ sec_flip) for i in range(sec_count)])]
    ppermute x2, starting transfers between devices: 4.6 us -> 2.88 us  [over(): return lax.ppermute(value, ('sec', 'req'), pairs)]
    all_to_all x1, blocking collectives: 17.6 us -> 18.6 us  [on_device(): pieces = lax.all_to_all(pieces, 'head', 0, 0, tiled=True)]
    pallas_call x9 -> x8, Pallas kernels: 7.98 us -> 7.12 us  [call(): pl.pallas_call(kernel, out_shape=outs, in_specs=[spec for spec, _ in ins]...]
    ppermute x7 -> x6, starting transfers between devices: 5.86 us -> 6.6 us  [over(): lax.ppermute(value, 'req', [(i, i ^ req_flip) for i in range(req_count)])]
    ppermute x7 -> x6, waiting for transfers between devices: 2.61 us -> 2.58 us  [over(): lax.ppermute(value, 'req', [(i, i ^ req_flip) for i in range(req_count)])]
  transfers between devices with their start and end apart: 14 -> 13, of which waited for: 8 -> 9; matrix products, arithmetic and copies ran while one was open for 0% -> 0% of each run, Pallas kernels for 12% -> 10%
where the time goes in v4:
time: 58.3 us; the launch traced here: 58.2 us
  starting transfers between devices  18.6 us (32%)
  blocking collectives  18.6 us (32%)
  waiting for transfers between devices  12.9 us (22%)
  Pallas kernels  7.12 us (12%)
  other arithmetic  0.64 us (1%)
    all_to_all x1, blocking collectives, on_device(): pieces = lax.all_to_all(pieces, 'head', 0, 0, tiled=True)  18.6 us
    ppermute x5, starting transfers between devices, over(): lax.ppermute(value, 'sec', [(i, i ^ sec_flip) for i in range(sec_count)])  9.1 us
    pallas_call x8, Pallas kernels, call(): pl.pallas_call(kernel, out_shape=outs, in_specs=[spec for spec, _ in ins]...  7.12 us
    ppermute x6, starting transfers between devices, over(): lax.ppermute(value, 'req', [(i, i ^ req_flip) for i in range(req_count)])  6.6 us
    ppermute x2, waiting for transfers between devices, over(): return lax.ppermute(value, ('sec', 'req'), pairs)  5.55 us
    ppermute x5, waiting for transfers between devices, over(): lax.ppermute(value, 'sec', [(i, i ^ sec_flip) for i in range(sec_count)])  4.81 us
    ppermute x2, starting transfers between devices, over(): return lax.ppermute(value, ('sec', 'req'), pairs)  2.88 us
    ppermute x6, waiting for transfers between devices, over(): lax.ppermute(value, 'req', [(i, i ^ req_flip) for i in range(req_count)])  2.58 us
  transfers between devices with their start and end apart: 13, of which 9 were waited for; matrix products, arithmetic and copies ran while one was open for 0% of the time, Pallas kernels for 10%

profile of v4, /device:TPU:2, one launch (start us, length us, event | category | flops | bytes accessed | tf_op | source)
XLA Modules:
  0.0 58.2 jit_solution(9643105103329227939)
XLA Ops:
  0.0 0.0 copy-start.2
  0.0 0.0 copy-start.6
  0.0 0.0 copy-start.5
  0.0 0.0 copy-start.4
  0.0 0.0 copy-start.3
  0.0 0.0 copy-start.1
  0.0 0.1 collective-permute-start
  0.1 4.2 %new_kv.1 = (bf16[128,256]{1,0:T(8,128)(2,1)S(1)}, bf16[128,256]{1,0:T(8,128)(2,1)S(1)}, bf16[128,256]{1,0:T(8,128)(2,1)S(1)}, bf16[128,256]{1,0:T(8,128)(2,1)S(1)}) custom-call(bf16[512,4096]{1,0:T(8,128)(2,1)} %x_ref.1, bf16[4096,256]{1,0:T(8,128)(2,1)} %w_ref.1), custom_call_target="tpu_custom_call" | custom-call | flops 1073741824 | bytes 6291456 | tf_op jit(solution)/shard_map/new_kv/pallas_call | solution.py:207
  4.4 0.0 copy-start
  4.4 0.0 collective-permute-done.other_ref
  4.4 0.0 copy-done.2
  4.4 0.2 place.1
  4.6 1.7 %collective-permute-start.1 = (bf16[16,2048]{1,0:T(8,128)(2,1)S(1)}, bf16[16,2048]{1,0:T(8,128)(2,1)S(1)}, u32[]{:S(2)}, u32[]{:S(2)}) collective-permute-start(bf16[16,2048]{1,0:T(8,128)(2,1)S(1)} %place.1), channel_id=1, source_target_pairs={{0,2},{1,3},{2,0},{3,1},{4,6},{5,7},{6,4},{7,5},{8,10},{9,11},{10,... | collective-permute-start | bytes 196616 | tf_op jit(solution)/shard_map/ppermute | solution.py:233
  6.2 4.6 %collective-permute-start.3 = (bf16[128,256]{1,0:T(8,128)(2,1)S(1)}, bf16[128,256]{1,0:T(8,128)(2,1)S(1)}, u32[]{:S(2)}, u32[]{:S(2)}) collective-permute-start(bf16[128,256]{1,0:T(8,128)(2,1)S(1)} %get-tuple-element.33), channel_id=1, source_target_pairs={{0,192},{64,128},{128,64},{192,0},{1,193},{65,129},{129,65},{193,1... | collective-permute-start | bytes 196616 | tf_op jit(solution)/shard_map/ppermute | solution.py:231
  10.9 0.0 collective-permute-start.4
  10.9 0.6 collective-permute-start.5
  11.4 0.0 collective-permute-done.1
  11.5 2.3 %collective-permute-start.2 = (bf16[16,2048]{1,0:T(8,128)(2,1)S(1)}, bf16[16,2048]{1,0:T(8,128)(2,1)S(1)}, u32[]{:S(2)}, u32[]{:S(2)}) collective-permute-start(bf16[16,2048]{1,0:T(8,128)(2,1)S(1)} %add.6), channel_id=1, source_target_pairs={{0,6},{1,7},{2,4},{3,5},{4,2},{5,3},{6,0},{7,1},{8,14},{9,15},{10,... | collective-permute-start | bytes 196616 | tf_op jit(solution)/shard_map/ppermute | solution.py:233
  13.7 0.0 copy-done.6
  13.7 0.0 copy-done.5
  13.7 0.0 copy-done.4
  13.7 0.0 copy-done.3
  13.8 0.0 copy-done.1
  13.8 1.7 %cached.1 = (f32[128,256]{1,0:T(8,128)S(1)}, f32[8,256]{1,0:T(8,128)S(1)}, f32[128,256]{1,0:T(8,128)S(1)}) custom-call(s32[256]{0:T(256)S(1)} %bitcast.3, s32[256]{0:T(256)S(1)} %copy-done.4, s32[256]{0:T(256)S(1)} %copy-done.5, s32[2]{0:T(128)S(1)} %copy-done.6, bf16[2,2048]{1,0:T(2,128)(2,1)S(1)} %copy-done.2, bf16[2,1024,256]{2,1,0:T(8,128)(2,1)S(1)} %bitcast.2), custom_call_target="tpu_custom_call" | custom-call | flops 268435456 | bytes 1059848 | tf_op jit(solution)/shard_map/cached/pallas_call | solution.py:207
  15.5 0.0 collective-permute-done.3.a_ref
  15.5 0.7 %collective-permute-done.4.b_ref = bf16[128,256]{1,0:T(8,128)(2,1)S(1)} collective-permute-done((bf16[128,256]{1,0:T(8,128)(2,1)S(1)}, bf16[128,256]{1,0:T(8,128)(2,1)S(1)}, u32[]{:S(2)}, u32[]{:S(2)}) %collective-permute-start.4) | collective-permute-done | bytes 65568 | tf_op jit(solution)/shard_map/ppermute | solution.py:231
  16.2 0.3 collective-permute-done.5.c_ref
  16.6 0.5 collective-permute-done.2
  17.1 0.4 prompt.1
  17.4 0.1 collective-permute-start.6
  17.5 1.3 %collective-permute-done.6.refs_0_ = bf16[144,256]{1,0:T(8,128)(2,1)S(1)} collective-permute-done((bf16[144,256]{1,0:T(8,128)(2,1)S(1)}, bf16[144,256]{1,0:T(8,128)(2,1)S(1)}, u32[]{:S(2)}, u32[]{:S(2)}) %collective-permute-start.6) | collective-permute-done | bytes 73760 | tf_op jit(solution)/shard_map/ppermute | solution.py:233
  18.8 0.1 join_core.1
  18.9 0.1 collective-permute-start.9
  19.0 1.5 %collective-permute-start.8 = (bf16[144,256]{1,0:T(8,128)(2,1)S(1)}, bf16[144,256]{1,0:T(8,128)(2,1)S(1)}, u32[]{:S(2)}, u32[]{:S(2)}) collective-permute-start(bf16[144,256]{1,0:T(8,128)(2,1)S(1)} %get-tuple-element.43), channel_id=1, source_target_pairs={{0,64},{64,0},{128,192},{192,128},{1,65},{65,1},{129,193},{193,129... | collective-permute-start | bytes 221192 | tf_op jit(solution)/shard_map/ppermute | solution.py:231
  20.5 1.9 %collective-permute-start.7 = (bf16[144,256]{1,0:T(8,128)(2,1)S(1)}, bf16[144,256]{1,0:T(8,128)(2,1)S(1)}, u32[]{:S(2)}, u32[]{:S(2)}) collective-permute-start(bf16[144,256]{1,0:T(8,128)(2,1)S(1)} %get-tuple-element.43), channel_id=1, source_target_pairs={{0,66},{1,67},{2,64},{3,65},{4,70},{5,71},{6,68},{7,69},{64,2},{65... | collective-permute-start | bytes 221192 | tf_op jit(solution)/shard_map/ppermute | solution.py:238
  22.4 0.9 %collective-permute-done.9.refs_2_ = bf16[144,256]{1,0:T(8,128)(2,1)S(1)} collective-permute-done((bf16[144,256]{1,0:T(8,128)(2,1)S(1)}, bf16[144,256]{1,0:T(8,128)(2,1)S(1)}, u32[]{:S(2)}, u32[]{:S(2)}) %collective-permute-start.9) | collective-permute-done | bytes 73760 | tf_op jit(solution)/shard_map/ppermute | solution.py:233
  23.3 0.1 collective-permute-done.8.refs_1_
  23.4 2.8 %collective-permute-done.7.refs_0_ = bf16[144,256]{1,0:T(8,128)(2,1)S(1)} collective-permute-done((bf16[144,256]{1,0:T(8,128)(2,1)S(1)}, bf16[144,256]{1,0:T(8,128)(2,1)S(1)}, u32[]{:S(2)}, u32[]{:S(2)}) %collective-permute-start.7) | collective-permute-done | bytes 73760 | tf_op jit(solution)/shard_map/ppermute | solution.py:238
  26.2 0.1 join_near.1
  26.3 2.4 %collective-permute-start.12 = (bf16[144,256]{1,0:T(8,128)(2,1)S(1)}, bf16[144,256]{1,0:T(8,128)(2,1)S(1)}, u32[]{:S(2)}, u32[]{:S(2)}) collective-permute-start(bf16[144,256]{1,0:T(8,128)(2,1)S(1)} %get-tuple-element.46), channel_id=1, source_target_pairs={{0,6},{1,7},{2,4},{3,5},{4,2},{5,3},{6,0},{7,1},{8,14},{9,15},{10,... | collective-permute-start | bytes 221192 | tf_op jit(solution)/shard_map/ppermute | solution.py:233
  28.7 2.4 %collective-permute-start.11 = (bf16[144,256]{1,0:T(8,128)(2,1)S(1)}, bf16[144,256]{1,0:T(8,128)(2,1)S(1)}, u32[]{:S(2)}, u32[]{:S(2)}) collective-permute-start(bf16[144,256]{1,0:T(8,128)(2,1)S(1)} %get-tuple-element.46), channel_id=1, source_target_pairs={{0,128},{64,192},{128,0},{192,64},{1,129},{65,193},{129,1},{193,65... | collective-permute-start | bytes 221192 | tf_op jit(solution)/shard_map/ppermute | solution.py:231
  31.1 1.0 %collective-permute-start.10 = (bf16[144,256]{1,0:T(8,128)(2,1)S(1)}, bf16[144,256]{1,0:T(8,128)(2,1)S(1)}, u32[]{:S(2)}, u32[]{:S(2)}) collective-permute-start(bf16[144,256]{1,0:T(8,128)(2,1)S(1)} %get-tuple-element.46), channel_id=1, source_target_pairs={{0,134},{1,135},{2,132},{3,133},{4,130},{5,131},{6,128},{7,129},{6... | collective-permute-start | bytes 221192 | tf_op jit(solution)/shard_map/ppermute | solution.py:238
  32.0 0.0 collective-permute-done.12.refs_2_
  32.0 3.7 %collective-permute-done.11.refs_1_ = bf16[144,256]{1,0:T(8,128)(2,1)S(1)} collective-permute-done((bf16[144,256]{1,0:T(8,128)(2,1)S(1)}, bf16[144,256]{1,0:T(8,128)(2,1)S(1)}, u32[]{:S(2)}, u32[]{:S(2)}) %collective-permute-start.11) | collective-permute-done | bytes 73760 | tf_op jit(solution)/shard_map/ppermute | solution.py:231
  35.7 2.7 %collective-permute-done.10.refs_0_ = bf16[144,256]{1,0:T(8,128)(2,1)S(1)} collective-permute-done((bf16[144,256]{1,0:T(8,128)(2,1)S(1)}, bf16[144,256]{1,0:T(8,128)(2,1)S(1)}, u32[]{:S(2)}, u32[]{:S(2)}) %collective-permute-start.10) | collective-permute-done | bytes 73760 | tf_op jit(solution)/shard_map/ppermute | solution.py:238
  38.4 0.0 copy-done
  38.4 0.5 join_far_project.1
  38.9 18.6 %all_to_all.5 = bf16[8,2,512]{2,1,0:T(2,128)(2,1)S(1)} all-to-all(bf16[8,2,512]{2,1,0:T(2,128)(2,1)S(1)} %reshape.3), channel_id=1, replica_groups=mesh['sec'=4,'head'=8,'req'=8] {'head'}, dimensions={0} | all-to-all | bytes 32768 | tf_op jit(solution)/shard_map/all_to_all | solution.py:312
  57.5 0.6 %reduce_sum.12 = bf16[2,512]{1,0:T(2,128)(2,1)} reduce(bf16[8,2,512]{2,1,0:T(2,128)(2,1)S(1)} %all_to_all.5, bf16[]{:T(256)} %constant.2.clone.1), dimensions={0}, to_apply=%region_0.0 | reduce | flops 7168 | bytes 18434 | tf_op jit(solution)/shard_map/reduce_sum | solution.py:313
  (4 shorter events, 0.1 us)
Async XLA Ops:
  0.0 4.4 %copy-start.2 = (bf16[2,2048]{1,0:T(2,128)(2,1)S(1)}, bf16[2,2048]{1,0:T(2,128)(2,1)}, u32[]{:S(2)}) copy-start(bf16[2,2048]{1,0:T(2,128)(2,1)} %q_ref.1) | copy-start | bytes 24580
  0.0 13.7 %copy-start.6 = (s32[2]{0:T(128)S(1)}, s32[2]{0:T(128)}, u32[]{:S(2)}) copy-start(s32[2]{0:T(128)} %ctx_ref.1) | copy-start | bytes 28
  0.0 13.7 %copy-start.5 = (s32[256]{0:T(256)S(1)}, s32[256]{0:T(256)}, u32[]{:S(2)}) copy-start(s32[256]{0:T(256)} %len_ref.1) | copy-start | bytes 3076
  0.0 13.7 %copy-start.4 = (s32[256]{0:T(256)S(1)}, s32[256]{0:T(256)}, u32[]{:S(2)}) copy-start(s32[256]{0:T(256)} %slot_ref.1) | copy-start | bytes 3076
  0.0 13.7 %copy-start.3 = (s32[256,1]{0,1:T(1,128)S(1)}, s32[256,1]{0,1:T(1,128)}, u32[]{:S(2)}) copy-start(s32[256,1]{0,1:T(1,128)} %param.14) | copy-start | bytes 3076
  0.0 13.7 %copy-start.1 = (bf16[2,1024,1,256]{3,1,2,0:T(8,128)(2,1)S(1)}, bf16[2,1024,1,256]{3,1,2,0:T(8,128)(2,1)}, u32[]{:S(2)}) copy-start(bf16[2,1024,1,256]{3,1,2,0:T(8,128)(2,1)} %param.12) | copy-start | bytes 3145732
  0.0 4.3 %collective-permute-start = (bf16[2,2048]{1,0:T(2,128)(2,1)}, bf16[2,2048]{1,0:T(2,128)(2,1)S(1)}, u32[]{:S(2)}, u32[]{:S(2)}) collective-permute-start(bf16[2,2048]{1,0:T(2,128)(2,1)} %q_ref.1), channel_id=1, source_target_pairs={{0,1},{1,0},{2,3},{3,2},{4,5},{5,4},{6,7},{7,6},{8,9},{9,8},{10,11... | collective-permute-start | bytes 24584 | tf_op jit(solution)/shard_map/ppermute | solution.py:233
  4.4 34.1 %copy-start = (bf16[2048,512]{1,0:T(8,128)(2,1)S(1)}, bf16[2048,512]{1,0:T(8,128)(2,1)}, u32[]{:S(2)}) copy-start(bf16[2048,512]{1,0:T(8,128)(2,1)} %out_w_ref.1) | copy-start | bytes 6291460
  4.6 6.9 %collective-permute-start.1 = (bf16[16,2048]{1,0:T(8,128)(2,1)S(1)}, bf16[16,2048]{1,0:T(8,128)(2,1)S(1)}, u32[]{:S(2)}, u32[]{:S(2)}) collective-permute-start(bf16[16,2048]{1,0:T(8,128)(2,1)S(1)} %place.1), channel_id=1, source_target_pairs={{0,2},{1,3},{2,0},{3,1},{4,6},{5,7},{6,4},{7,5},{8,10},{9,11},{10,... | collective-permute-start | bytes 196616 | tf_op jit(solution)/shard_map/ppermute | solution.py:233
  6.2 9.3 %collective-permute-start.3 = (bf16[128,256]{1,0:T(8,128)(2,1)S(1)}, bf16[128,256]{1,0:T(8,128)(2,1)S(1)}, u32[]{:S(2)}, u32[]{:S(2)}) collective-permute-start(bf16[128,256]{1,0:T(8,128)(2,1)S(1)} %get-tuple-element.33), channel_id=1, source_target_pairs={{0,192},{64,128},{128,64},{192,0},{1,193},{65,129},{129,65},{193,1... | collective-permute-start | bytes 196616 | tf_op jit(solution)/shard_map/ppermute | solution.py:231
  10.9 5.3 %collective-permute-start.4 = (bf16[128,256]{1,0:T(8,128)(2,1)S(1)}, bf16[128,256]{1,0:T(8,128)(2,1)S(1)}, u32[]{:S(2)}, u32[]{:S(2)}) collective-permute-start(bf16[128,256]{1,0:T(8,128)(2,1)S(1)} %get-tuple-element.34), channel_id=1, source_target_pairs={{0,128},{64,192},{128,0},{192,64},{1,129},{65,193},{129,1},{193,65... | collective-permute-start | bytes 196616 | tf_op jit(solution)/shard_map/ppermute | solution.py:231
  10.9 5.7 %collective-permute-start.5 = (bf16[128,256]{1,0:T(8,128)(2,1)S(1)}, bf16[128,256]{1,0:T(8,128)(2,1)S(1)}, u32[]{:S(2)}, u32[]{:S(2)}) collective-permute-start(bf16[128,256]{1,0:T(8,128)(2,1)S(1)} %get-tuple-element.35), channel_id=1, source_target_pairs={{0,64},{64,0},{128,192},{192,128},{1,65},{65,1},{129,193},{193,129... | collective-permute-start | bytes 196616 | tf_op jit(solution)/shard_map/ppermute | solution.py:231
  11.5 5.6 %collective-permute-start.2 = (bf16[16,2048]{1,0:T(8,128)(2,1)S(1)}, bf16[16,2048]{1,0:T(8,128)(2,1)S(1)}, u32[]{:S(2)}, u32[]{:S(2)}) collective-permute-start(bf16[16,2048]{1,0:T(8,128)(2,1)S(1)} %add.6), channel_id=1, source_target_pairs={{0,6},{1,7},{2,4},{3,5},{4,2},{5,3},{6,0},{7,1},{8,14},{9,15},{10,... | collective-permute-start | bytes 196616 | tf_op jit(solution)/shard_map/ppermute | solution.py:233
  17.4 1.4 %collective-permute-start.6 = (bf16[144,256]{1,0:T(8,128)(2,1)S(1)}, bf16[144,256]{1,0:T(8,128)(2,1)S(1)}, u32[]{:S(2)}, u32[]{:S(2)}) collective-permute-start(bf16[144,256]{1,0:T(8,128)(2,1)S(1)} %get-tuple-element.40), channel_id=1, source_target_pairs={{0,1},{1,0},{2,3},{3,2},{4,5},{5,4},{6,7},{7,6},{8,9},{9,8},{10,11... | collective-permute-start | bytes 221192 | tf_op jit(solution)/shard_map/ppermute | solution.py:233
  18.9 4.4 %collective-permute-start.9 = (bf16[144,256]{1,0:T(8,128)(2,1)S(1)}, bf16[144,256]{1,0:T(8,128)(2,1)S(1)}, u32[]{:S(2)}, u32[]{:S(2)}) collective-permute-start(bf16[144,256]{1,0:T(8,128)(2,1)S(1)} %get-tuple-element.43), channel_id=1, source_target_pairs={{0,2},{1,3},{2,0},{3,1},{4,6},{5,7},{6,4},{7,5},{8,10},{9,11},{10,... | collective-permute-start | bytes 221192 | tf_op jit(solution)/shard_map/ppermute | solution.py:233
  19.0 4.4 %collective-permute-start.8 = (bf16[144,256]{1,0:T(8,128)(2,1)S(1)}, bf16[144,256]{1,0:T(8,128)(2,1)S(1)}, u32[]{:S(2)}, u32[]{:S(2)}) collective-permute-start(bf16[144,256]{1,0:T(8,128)(2,1)S(1)} %get-tuple-element.43), channel_id=1, source_target_pairs={{0,64},{64,0},{128,192},{192,128},{1,65},{65,1},{129,193},{193,129... | collective-permute-start | bytes 221192 | tf_op jit(solution)/shard_map/ppermute | solution.py:231
  20.5 5.7 %collective-permute-start.7 = (bf16[144,256]{1,0:T(8,128)(2,1)S(1)}, bf16[144,256]{1,0:T(8,128)(2,1)S(1)}, u32[]{:S(2)}, u32[]{:S(2)}) collective-permute-start(bf16[144,256]{1,0:T(8,128)(2,1)S(1)} %get-tuple-element.43), channel_id=1, source_target_pairs={{0,66},{1,67},{2,64},{3,65},{4,70},{5,71},{6,68},{7,69},{64,2},{65... | collective-permute-start | bytes 221192 | tf_op jit(solution)/shard_map/ppermute | solution.py:238
  26.3 5.7 %collective-permute-start.12 = (bf16[144,256]{1,0:T(8,128)(2,1)S(1)}, bf16[144,256]{1,0:T(8,128)(2,1)S(1)}, u32[]{:S(2)}, u32[]{:S(2)}) collective-permute-start(bf16[144,256]{1,0:T(8,128)(2,1)S(1)} %get-tuple-element.46), channel_id=1, source_target_pairs={{0,6},{1,7},{2,4},{3,5},{4,2},{5,3},{6,0},{7,1},{8,14},{9,15},{10,... | collective-permute-start | bytes 221192 | tf_op jit(solution)/shard_map/ppermute | solution.py:233
  28.7 7.0 %collective-permute-start.11 = (bf16[144,256]{1,0:T(8,128)(2,1)S(1)}, bf16[144,256]{1,0:T(8,128)(2,1)S(1)}, u32[]{:S(2)}, u32[]{:S(2)}) collective-permute-start(bf16[144,256]{1,0:T(8,128)(2,1)S(1)} %get-tuple-element.46), channel_id=1, source_target_pairs={{0,128},{64,192},{128,0},{192,64},{1,129},{65,193},{129,1},{193,65... | collective-permute-start | bytes 221192 | tf_op jit(solution)/shard_map/ppermute | solution.py:231
  31.1 7.4 %collective-permute-start.10 = (bf16[144,256]{1,0:T(8,128)(2,1)S(1)}, bf16[144,256]{1,0:T(8,128)(2,1)S(1)}, u32[]{:S(2)}, u32[]{:S(2)}) collective-permute-start(bf16[144,256]{1,0:T(8,128)(2,1)S(1)} %get-tuple-element.46), channel_id=1, source_target_pairs={{0,134},{1,135},{2,132},{3,133},{4,130},{5,131},{6,128},{7,129},{6... | collective-permute-start | bytes 221192 | tf_op jit(solution)/shard_map/ppermute | solution.py:238

commit v5 on v4

--- a/solution.py
+++ b/solution.py
@@ -21,10 +21,6 @@
 
 def vmem():
     return pl.BlockSpec(memory_space=pltpu.VMEM)
-
-
-def smem():
-    return pl.BlockSpec(memory_space=pltpu.SMEM)
 
 
 def dot(a, b, dims):
@@ -104,7 +100,7 @@
         queries = jnp.concatenate(
             [q_ref[slot : slot + 1, h * HD : (h + 1) * HD] for h in range(GROUP)], axis=0
         )
-        live = position < ctx_ref[slot]
+        live = position < ctx_ref[0:1, slot : slot + 1]
         scores = dot(queries, cache_ref[slot, :, 0:HD], ((1,), (1,))) * FACTOR
         scores = jnp.where(live, scores, LOW)
         peak = jnp.max(scores, axis=1, keepdims=True)
@@ -122,29 +118,49 @@
         totals = totals + jnp.sum(jnp.where(lane_of, total, 0.0), axis=0, keepdims=True)
     weighted_ref[...] = weighted
     stats_ref[...] = stat_rows(peaks, totals, 8)
-    blocks = live_ref.shape[0] // BLK
-    base = (req_id * lax.axis_size("sec") + sec_id) * blocks
-    lane = lax.broadcasted_iota(jnp.int32, (BLK, LANES), 1) % NREQ
-    place = lax.broadcasted_iota(jnp.int32, (BLK, LANES), 0)
-    for block in range(blocks):
-        holder = owner_ref[base + block] * 2 + slot_ref[base + block]
-        live_block = (lane == holder) & (place < len_ref[base + block])
-        live_ref[block * BLK : (block + 1) * BLK, :] = live_block.astype(F32)
-
-
-def place_kernel(mine_ref, other_ref, out_ref):
+
+    rows, blocks = live_ref.shape[0], owner_ref.shape[1]
+    first = (req_id * lax.axis_size("sec") + sec_id) * (rows // BLK)
+    token = lax.broadcasted_iota(jnp.int32, (rows, blocks), 0)
+    block = lax.broadcasted_iota(jnp.int32, (rows, blocks), 1)
+    mine = block == token // BLK + first
+    holder = owner_ref[...] * 2 + slot_ref[...]
+    holder = jnp.sum(jnp.where(mine, holder, 0).astype(F32), axis=1, keepdims=True)
+    length = jnp.sum(jnp.where(mine, len_ref[...], 0).astype(F32), axis=1, keepdims=True)
+    lane = lax.broadcasted_iota(jnp.int32, (rows, LANES), 1) % NREQ
+    place = lax.broadcasted_iota(jnp.int32, (rows, LANES), 0) % BLK
+    live = (lane.astype(F32) == holder) & (place.astype(F32) < length)
+    live_ref[...] = live.astype(F32)
+
+
+def pair_up(mine, other, mine_is_first):
+    rows = mine.shape[0]
+    place = lax.broadcasted_iota(jnp.int32, (2 * rows, rows), 0)
+    row = lax.broadcasted_iota(jnp.int32, (2 * rows, rows), 1)
+    lower, upper = (place == row).astype(F32), (place == row + rows).astype(F32)
+    first = mine_is_first.astype(F32)
+    mine_place = (lower * first + upper * (1.0 - first)).astype(BF)
+    other_place = (upper * first + lower * (1.0 - first)).astype(BF)
+    both = dot(mine_place, mine, ((1,), (0,))) + dot(other_place, other, ((1,), (0,)))
+    return both.astype(BF)
+
+
+def core_pair_kernel(mine_ref, other_ref, out_ref):
     req_id = lax.axis_index("req")
-    place = lax.broadcasted_iota(jnp.int32, (NREQ, 2), 0)
-    row = lax.broadcasted_iota(jnp.int32, (NREQ, 2), 1)
-    mine = (place == req_id * 2 + row).astype(BF)
-    other = (place == (req_id ^ 1) * 2 + row).astype(BF)
-    placed = dot(mine, mine_ref[...], ((1,), (0,))) + dot(other, other_ref[...], ((1,), (0,)))
-    out_ref[...] = placed.astype(BF)
-
-
-def prompt_kernel(q_ref, live_ref, kv_ref, cw_ref, cs_ref, kw_ref, ks_ref, send_ref):
+    out_ref[...] = pair_up(mine_ref[...], other_ref[...], req_id % 2 == 0)
+
+
+def y_pair_kernel(mine_ref, other_ref, out_ref):
+    req_id = lax.axis_index("req")
+    out_ref[...] = pair_up(mine_ref[...], other_ref[...], req_id // 2 % 2 == 0)
+
+
+def prompt_kernel(
+    mine_ref, other_ref, live_ref, kv_ref, cw_ref, cs_ref, kw_ref, ks_ref, send_ref
+):
     new_kv = kv_ref[...]
-    queries = rows_of(q_ref[...])
+    req_id = lax.axis_index("req")
+    queries = rows_of(pair_up(mine_ref[...], other_ref[...], req_id < lax.axis_size("req") // 2))
     live = live_ref[...] > 0.5
     scores = dot(new_kv[:, 0:HD], queries, ((1,), (1,))) * FACTOR
     scores = jnp.where(live, scores, LOW)
@@ -187,13 +203,31 @@
     store_packed(send_ref, weighted, peak, total)
 
 
-def project_kernel(w_ref, s_ref, out_w_ref, *refs):
-    weighted, _, total = joined(w_ref, s_ref, refs[:-1])
+def far_kernel(first_ref, second_ref, kw_ref, ks_ref, send_ref):
+    use_second = (lax.axis_index("req") % 2).astype(F32)
+    peak, total = unpacked_stats(first_ref[HD : HD + STAT, :])
+    peak_2, total_2 = unpacked_stats(second_ref[HD : HD + STAT, :])
+    joint = jnp.maximum(peak, peak_2)
+    scale, scale_2 = jnp.exp(peak - joint), jnp.exp(peak_2 - joint) * use_second
+    weighted = first_ref[0:HD, :].astype(F32) * scale + second_ref[0:HD, :].astype(F32) * scale_2
+    total = total * scale + total_2 * scale_2
+    kw_ref[...] = weighted
+    ks_ref[...] = stat_rows(joint, total, 8)
+    store_packed(send_ref, weighted, joint, total)
+
+
+def project_kernel(w_ref, s_ref, far_w_ref, far_s_ref, out_w_ref, got_ref, out_ref):
+    weighted, peak, total = joined(w_ref, s_ref, (got_ref,))
+    far_peak, far_total = far_s_ref[0:1, :], far_s_ref[1:2, :]
+    joint = jnp.maximum(peak, far_peak)
+    scale, far_scale = jnp.exp(peak - joint), jnp.exp(far_peak - joint)
+    weighted = weighted * scale + far_w_ref[...] * far_scale
+    total = total * scale + far_total * far_scale
     rows = (weighted / total).T.astype(BF)
     attended = jnp.concatenate(
         [rows[h * NREQ : (h + 1) * NREQ, :] for h in range(GROUP)], axis=1
     )
-    refs[-1][...] = dot(attended, out_w_ref[...], ((1,), (0,))).astype(BF)
+    out_ref[...] = dot(attended, out_w_ref[...], ((1,), (0,))).astype(BF)
 
 
 def shape(dims, dtype):
@@ -231,9 +265,13 @@
             return lax.ppermute(value, "sec", [(i, i ^ sec_flip) for i in range(sec_count)])
         if sec_flip == 0:
             return lax.ppermute(value, "req", [(i, i ^ req_flip) for i in range(req_count)])
+        return over_cores(value, (sec_flip, req_flip), (sec_flip, req_flip))
+
+    def over_cores(value, flips_0, flips_1):
         pairs = []
         for i in range(sec_count):
             for j in range(req_count):
+                sec_flip, req_flip = flips_1 if j % 2 else flips_0
                 pairs.append((i * req_count + j, (i ^ sec_flip) * req_count + (j ^ req_flip)))
         return lax.ppermute(value, ("sec", "req"), pairs)
 
@@ -255,22 +293,25 @@
     )
     chunks, other_queries = lax.optimization_barrier((chunks, other_queries))
 
-    gathered = call(
-        place_kernel,
-        [(vmem(), queries), (vmem(), other_queries)],
-        shape((NREQ, queries.shape[1]), BF),
-        "place",
-    )
-    gathered = gathered + over(gathered, 0, 2)
+    def paired(kernel, mine, other, name):
+        return call(
+            kernel,
+            [(vmem(), mine), (vmem(), other)],
+            shape((2 * mine.shape[0], mine.shape[1]), BF),
+            name,
+        )
+
+    of_chip = paired(core_pair_kernel, queries, other_queries, "core_pair")
     arrived = [over(chunks[flip], flip, 0) for flip in (3, 2, 1)]
-    gathered = gathered + over(gathered, 0, 6)
+    of_half = paired(y_pair_kernel, of_chip, over(of_chip, 0, 2), "y_pair")
+    of_other_half = over(of_half, 0, 6)
     cached_weighted, cached_stats, live = call(
         cached_kernel,
         [
-            (smem(), blk_owner[:, 0]),
-            (smem(), blk_slot),
-            (smem(), blk_len),
-            (smem(), ctx_len),
+            (vmem(), blk_owner.reshape(1, -1)),
+            (vmem(), blk_slot.reshape(1, -1)),
+            (vmem(), blk_len.reshape(1, -1)),
+            (vmem(), ctx_len.reshape(1, -1)),
             (vmem(), queries),
             (vmem(), cache[:, :, 0, :]),
         ],
@@ -284,7 +325,8 @@
     kept = call(
         prompt_kernel,
         [
-            (vmem(), value) for value in (gathered, live, new_kv, cached_weighted, cached_stats)
+            (vmem(), value)
+            for value in (of_half, of_other_half, live, new_kv, cached_weighted, cached_stats)
         ],
         STATE,
         "prompt",
@@ -298,13 +340,19 @@
         kept = call(
             join_kernel, [(vmem(), value) for value in (kept[0], kept[1], *got)], STATE, name
         )
-    got = [over(kept[2], *flips) for flips in ((2, 6), (2, 0), (0, 6))]
+    got = [
+        over_cores(kept[2], (0, 6), flips) for flips in ((2, 0), (2, 6))
+    ]
+    far = call(far_kernel, [(vmem(), value) for value in got], STATE, "join_far")
     columns = w_out.shape[1]
     partial_out = call(
         project_kernel,
-        [(vmem(), value) for value in (kept[0], kept[1], w_out, *got)],
+        [
+            (vmem(), value)
+            for value in (kept[0], kept[1], far[0], far[1], w_out, over(far[2], 0, 1))
+        ],
         shape((NREQ, columns), BF),
-        "join_far_project",
+        "project",
         flops=2 * w_out.size * NREQ,
     )
     head_count = lax.axis_size("head")

time: 58.3 us -> 59.3 us (1.017); the launches traced: 58.2 us -> 58.6 us
  waiting for transfers between devices: 12.9 us -> 14.3 us
  starting transfers between devices: 18.6 us -> 17.6 us
    ppermute x5 -> x4, waiting for transfers between devices: 4.81 us -> 0.37 us  [over(): lax.ppermute(value, 'sec', [(i, i ^ sec_flip) for i in range(sec_count)])]
    ppermute x6, waiting for transfers between devices: 2.58 us -> 6.09 us  [over(): lax.ppermute(value, 'req', [(i, i ^ req_flip) for i in range(req_count)])]
    ppermute x5 -> x4, starting transfers between devices: 9.1 us -> 6.77 us  [over(): lax.ppermute(value, 'sec', [(i, i ^ sec_flip) for i in range(sec_count)])]
    ppermute x2 -> x3, waiting for transfers between devices: 5.55 us -> 7.83 us  [over_cores(): return lax.ppermute(value, ('sec', 'req'), pairs)]
    ppermute x2 -> x3, starting transfers between devices: 2.88 us -> 5.08 us  [over_cores(): return lax.ppermute(value, ('sec', 'req'), pairs)]
    ppermute x6, starting transfers between devices: 6.6 us -> 5.78 us  [over(): lax.ppermute(value, 'req', [(i, i ^ req_flip) for i in range(req_count)])]
    pallas_call x8 -> x10, Pallas kernels: 7.12 us -> 6.94 us  [call(): pl.pallas_call(kernel, out_shape=outs, in_specs=[spec for spec, _ in ins]...]
where the time goes in v5:
time: 59.3 us; the launch traced here: 58.6 us
  blocking collectives  18.9 us (32%)
  starting transfers between devices  17.6 us (30%)
  waiting for transfers between devices  14.3 us (24%)
  Pallas kernels  6.94 us (12%)
  other arithmetic  0.6 us (1%)
    all_to_all x1, blocking collectives, on_device(): pieces = lax.all_to_all(pieces, 'head', 0, 0, tiled=True)  18.9 us
    ppermute x3, waiting for transfers between devices, over_cores(): return lax.ppermute(value, ('sec', 'req'), pairs)  7.83 us
    pallas_call x10, Pallas kernels, call(): pl.pallas_call(kernel, out_shape=outs, in_specs=[spec for spec, _ in ins]...  6.94 us
    ppermute x4, starting transfers between devices, over(): lax.ppermute(value, 'sec', [(i, i ^ sec_flip) for i in range(sec_count)])  6.77 us
    ppermute x6, waiting for transfers between devices, over(): lax.ppermute(value, 'req', [(i, i ^ req_flip) for i in range(req_count)])  6.09 us
    ppermute x6, starting transfers between devices, over(): lax.ppermute(value, 'req', [(i, i ^ req_flip) for i in range(req_count)])  5.78 us
    ppermute x3, starting transfers between devices, over_cores(): return lax.ppermute(value, ('sec', 'req'), pairs)  5.08 us
  transfers between devices with their start and end apart: 13, of which 9 were waited for; matrix products, arithmetic and copies ran while one was open for 0% of the time, Pallas kernels for 10%

profile of v5, /device:TPU:2, one launch (start us, length us, event | category | flops | bytes accessed | tf_op | source)
XLA Modules:
  0.0 58.6 jit_solution(3580335837891209624)
XLA Ops:
  0.0 0.0 copy-start.2
  0.0 0.0 copy-start.6
  0.0 0.0 copy-start.5
  0.0 0.0 copy-start.4
  0.0 0.0 copy-start.3
  0.0 0.0 copy-start.1
  0.0 0.1 collective-permute-start
  0.1 4.2 %new_kv.1 = (bf16[128,256]{1,0:T(8,128)(2,1)S(1)}, bf16[128,256]{1,0:T(8,128)(2,1)S(1)}, bf16[128,256]{1,0:T(8,128)(2,1)S(1)}, bf16[128,256]{1,0:T(8,128)(2,1)S(1)}) custom-call(bf16[512,4096]{1,0:T(8,128)(2,1)} %x_ref.1, bf16[4096,256]{1,0:T(8,128)(2,1)} %w_ref.1), custom_call_target="tpu_custom_call" | custom-call | flops 1073741824 | bytes 6291456 | tf_op jit(solution)/shard_map/new_kv/pallas_call | solution.py:241
  4.4 0.0 copy-start
  4.4 0.0 collective-permute-done.other_ref
  4.4 4.7 %collective-permute-start.3 = (bf16[128,256]{1,0:T(8,128)(2,1)S(1)}, bf16[128,256]{1,0:T(8,128)(2,1)S(1)}, u32[]{:S(2)}, u32[]{:S(2)}) collective-permute-start(bf16[128,256]{1,0:T(8,128)(2,1)S(1)} %get-tuple-element.36), channel_id=1, source_target_pairs={{0,192},{64,128},{128,64},{192,0},{1,193},{65,129},{129,65},{193,1... | collective-permute-start | bytes 196616 | tf_op jit(solution)/shard_map/ppermute | solution.py:265
  9.1 0.0 collective-permute-start.4
  9.1 0.7 %collective-permute-start.5 = (bf16[128,256]{1,0:T(8,128)(2,1)S(1)}, bf16[128,256]{1,0:T(8,128)(2,1)S(1)}, u32[]{:S(2)}, u32[]{:S(2)}) collective-permute-start(bf16[128,256]{1,0:T(8,128)(2,1)S(1)} %get-tuple-element.38), channel_id=1, source_target_pairs={{0,64},{64,0},{128,192},{192,128},{1,65},{65,1},{129,193},{193,129... | collective-permute-start | bytes 196616 | tf_op jit(solution)/shard_map/ppermute | solution.py:265
  9.8 0.0 copy-done.2
  9.8 0.2 core_pair.1.mine_ref
  10.0 1.7 %collective-permute-start.1 = (bf16[4,2048]{1,0:T(4,128)(2,1)S(1)}, bf16[4,2048]{1,0:T(4,128)(2,1)S(1)}, u32[]{:S(2)}, u32[]{:S(2)}) collective-permute-start(bf16[4,2048]{1,0:T(4,128)(2,1)S(1)} %core_pair.1.mine_ref), channel_id=1, source_target_pairs={{0,2},{1,3},{2,0},{3,1},{4,6},{5,7},{6,4},{7,5},{8,10},{9,11},{10,... | collective-permute-start | bytes 49160 | tf_op jit(solution)/shard_map/ppermute | solution.py:267
  11.6 2.2 %collective-permute-done.1.other_ref = bf16[4,2048]{1,0:T(4,128)(2,1)S(1)} collective-permute-done((bf16[4,2048]{1,0:T(4,128)(2,1)S(1)}, bf16[4,2048]{1,0:T(4,128)(2,1)S(1)}, u32[]{:S(2)}, u32[]{:S(2)}) %collective-permute-start.1) | collective-permute-done | bytes 16416 | tf_op jit(solution)/shard_map/ppermute | solution.py:267
  13.8 0.2 y_pair.1.mine_ref
  14.0 3.1 %collective-permute-start.2 = (bf16[8,2048]{1,0:T(8,128)(2,1)S(1)}, bf16[8,2048]{1,0:T(8,128)(2,1)S(1)}, u32[]{:S(2)}, u32[]{:S(2)}) collective-permute-start(bf16[8,2048]{1,0:T(8,128)(2,1)S(1)} %y_pair.1.mine_ref), channel_id=1, source_target_pairs={{0,6},{1,7},{2,4},{3,5},{4,2},{5,3},{6,0},{7,1},{8,14},{9,15},{10,... | collective-permute-start | bytes 98312 | tf_op jit(solution)/shard_map/ppermute | solution.py:267
  17.1 0.0 copy-done.6
  17.1 0.0 copy-done.5
  17.1 0.0 copy-done.4
  17.1 0.0 copy-done.3
  17.1 0.0 copy-done.1
  17.1 1.2 %cached.1 = (f32[128,256]{1,0:T(8,128)S(1)}, f32[8,256]{1,0:T(8,128)S(1)}, f32[128,256]{1,0:T(8,128)S(1)}) custom-call(s32[1,256]{1,0:T(1,128)S(1)} %bitcast.6, s32[1,256]{1,0:T(1,128)S(1)} %bitcast.7, s32[1,256]{1,0:T(1,128)S(1)} %bitcast.8, s32[1,2]{1,0:T(1,128)S(1)} %bitcast.9, bf16[2,2048]{1,0:T(2,128)(2,1)S(1)} %copy-done.2, ...), custom_call_target="tpu_custom_call" | custom-call | flops 268435456 | bytes 1059848 | tf_op jit(solution)/shard_map/cached/pallas_call | solution.py:241
  18.3 0.0 collective-permute-done.3.a_ref
  18.3 0.0 collective-permute-done.4.b_ref
  18.3 0.0 collective-permute-done.5.c_ref
  18.3 0.8 %collective-permute-done.2.other_ref = bf16[8,2048]{1,0:T(8,128)(2,1)S(1)} collective-permute-done((bf16[8,2048]{1,0:T(8,128)(2,1)S(1)}, bf16[8,2048]{1,0:T(8,128)(2,1)S(1)}, u32[]{:S(2)}, u32[]{:S(2)}) %collective-permute-start.2) | collective-permute-done | bytes 32800 | tf_op jit(solution)/shard_map/ppermute | solution.py:267
  19.2 0.5 prompt.1
  19.7 0.1 collective-permute-start.6
  19.8 1.3 %collective-permute-done.6.refs_0_ = bf16[144,256]{1,0:T(8,128)(2,1)S(1)} collective-permute-done((bf16[144,256]{1,0:T(8,128)(2,1)S(1)}, bf16[144,256]{1,0:T(8,128)(2,1)S(1)}, u32[]{:S(2)}, u32[]{:S(2)}) %collective-permute-start.6) | collective-permute-done | bytes 73760 | tf_op jit(solution)/shard_map/ppermute | solution.py:267
  21.1 0.1 join_core.1
  21.1 0.4 collective-permute-start.9
  21.6 1.4 %collective-permute-start.8 = (bf16[144,256]{1,0:T(8,128)(2,1)S(1)}, bf16[144,256]{1,0:T(8,128)(2,1)S(1)}, u32[]{:S(2)}, u32[]{:S(2)}) collective-permute-start(bf16[144,256]{1,0:T(8,128)(2,1)S(1)} %get-tuple-element.46), channel_id=1, source_target_pairs={{0,64},{64,0},{128,192},{192,128},{1,65},{65,1},{129,193},{193,129... | collective-permute-start | bytes 221192 | tf_op jit(solution)/shard_map/ppermute | solution.py:265
  23.0 1.8 %collective-permute-start.7 = (bf16[144,256]{1,0:T(8,128)(2,1)S(1)}, bf16[144,256]{1,0:T(8,128)(2,1)S(1)}, u32[]{:S(2)}, u32[]{:S(2)}) collective-permute-start(bf16[144,256]{1,0:T(8,128)(2,1)S(1)} %get-tuple-element.46), channel_id=1, source_target_pairs={{0,66},{1,67},{2,64},{3,65},{4,70},{5,71},{6,68},{7,69},{64,2},{65... | collective-permute-start | bytes 221192 | tf_op jit(solution)/shard_map/ppermute | solution.py:276
  24.7 0.9 %collective-permute-done.9.refs_2_ = bf16[144,256]{1,0:T(8,128)(2,1)S(1)} collective-permute-done((bf16[144,256]{1,0:T(8,128)(2,1)S(1)}, bf16[144,256]{1,0:T(8,128)(2,1)S(1)}, u32[]{:S(2)}, u32[]{:S(2)}) %collective-permute-start.9) | collective-permute-done | bytes 73760 | tf_op jit(solution)/shard_map/ppermute | solution.py:267
  25.6 0.4 collective-permute-done.8.refs_1_
  25.9 2.5 %collective-permute-done.7.refs_0_ = bf16[144,256]{1,0:T(8,128)(2,1)S(1)} collective-permute-done((bf16[144,256]{1,0:T(8,128)(2,1)S(1)}, bf16[144,256]{1,0:T(8,128)(2,1)S(1)}, u32[]{:S(2)}, u32[]{:S(2)}) %collective-permute-start.7) | collective-permute-done | bytes 73760 | tf_op jit(solution)/shard_map/ppermute | solution.py:276
  28.4 0.1 join_near.1
  28.5 3.1 %collective-permute-start.11 = (bf16[144,256]{1,0:T(8,128)(2,1)S(1)}, bf16[144,256]{1,0:T(8,128)(2,1)S(1)}, u32[]{:S(2)}, u32[]{:S(2)}) collective-permute-start(bf16[144,256]{1,0:T(8,128)(2,1)S(1)} %get-tuple-element.49), channel_id=1, source_target_pairs={{0,6},{1,135},{2,4},{3,133},{4,2},{5,131},{6,0},{7,129},{64,70},{6... | collective-permute-start | bytes 221192 | tf_op jit(solution)/shard_map/ppermute | solution.py:276
  31.6 0.2 collective-permute-start.10
  31.8 2.9 %collective-permute-done.11.second_ref = bf16[144,256]{1,0:T(8,128)(2,1)S(1)} collective-permute-done((bf16[144,256]{1,0:T(8,128)(2,1)S(1)}, bf16[144,256]{1,0:T(8,128)(2,1)S(1)}, u32[]{:S(2)}, u32[]{:S(2)}) %collective-permute-start.11) | collective-permute-done | bytes 73760 | tf_op jit(solution)/shard_map/ppermute | solution.py:276
  34.8 2.4 %collective-permute-done.10.first_ref = bf16[144,256]{1,0:T(8,128)(2,1)S(1)} collective-permute-done((bf16[144,256]{1,0:T(8,128)(2,1)S(1)}, bf16[144,256]{1,0:T(8,128)(2,1)S(1)}, u32[]{:S(2)}, u32[]{:S(2)}) %collective-permute-start.10) | collective-permute-done | bytes 73760 | tf_op jit(solution)/shard_map/ppermute | solution.py:276
  37.2 0.4 collective-permute-start.12
  37.6 1.0 %collective-permute-done.12.got_ref = bf16[144,256]{1,0:T(8,128)(2,1)S(1)} collective-permute-done((bf16[144,256]{1,0:T(8,128)(2,1)S(1)}, bf16[144,256]{1,0:T(8,128)(2,1)S(1)}, u32[]{:S(2)}, u32[]{:S(2)}) %collective-permute-start.12) | collective-permute-done | bytes 73760 | tf_op jit(solution)/shard_map/ppermute | solution.py:267
  38.6 0.0 copy-done
  38.6 0.5 project.1
  39.1 18.9 %all_to_all.5 = bf16[8,2,512]{2,1,0:T(2,128)(2,1)S(1)} all-to-all(bf16[8,2,512]{2,1,0:T(2,128)(2,1)S(1)} %reshape.19), channel_id=1, replica_groups=mesh['sec'=4,'head'=8,'req'=8] {'head'}, dimensions={0} | all-to-all | bytes 32768 | tf_op jit(solution)/shard_map/all_to_all | solution.py:360
  58.0 0.6 %reduce_sum.12 = bf16[2,512]{1,0:T(2,128)(2,1)} reduce(bf16[8,2,512]{2,1,0:T(2,128)(2,1)S(1)} %all_to_all.5, bf16[]{:T(256)} %constant.2.clone.1), dimensions={0}, to_apply=%region_0.0 | reduce | flops 7168 | bytes 18434 | tf_op jit(solution)/shard_map/reduce_sum | solution.py:361
  (3 shorter events, 0.1 us)
Async XLA Ops:
  0.0 9.8 %copy-start.2 = (bf16[2,2048]{1,0:T(2,128)(2,1)S(1)}, bf16[2,2048]{1,0:T(2,128)(2,1)}, u32[]{:S(2)}) copy-start(bf16[2,2048]{1,0:T(2,128)(2,1)} %q_ref.1) | copy-start | bytes 24580
  0.0 17.1 %copy-start.6 = (s32[2]{0:T(128)S(1)}, s32[2]{0:T(128)}, u32[]{:S(2)}) copy-start(s32[2]{0:T(128)} %param.17) | copy-start | bytes 28
  0.0 17.1 %copy-start.5 = (s32[256]{0:T(256)S(1)}, s32[256]{0:T(256)}, u32[]{:S(2)}) copy-start(s32[256]{0:T(256)} %param.16) | copy-start | bytes 3076
  0.0 17.1 %copy-start.4 = (s32[256]{0:T(256)S(1)}, s32[256]{0:T(256)}, u32[]{:S(2)}) copy-start(s32[256]{0:T(256)} %param.15) | copy-start | bytes 3076
  0.0 17.1 %copy-start.3 = (s32[256,1]{0,1:T(1,128)S(1)}, s32[256,1]{0,1:T(1,128)}, u32[]{:S(2)}) copy-start(s32[256,1]{0,1:T(1,128)} %param.14) | copy-start | bytes 3076
  0.0 17.1 %copy-start.1 = (bf16[2,1024,1,256]{3,1,2,0:T(8,128)(2,1)S(1)}, bf16[2,1024,1,256]{3,1,2,0:T(8,128)(2,1)}, u32[]{:S(2)}) copy-start(bf16[2,1024,1,256]{3,1,2,0:T(8,128)(2,1)} %param.12) | copy-start | bytes 3145732
  0.0 4.3 %collective-permute-start = (bf16[2,2048]{1,0:T(2,128)(2,1)}, bf16[2,2048]{1,0:T(2,128)(2,1)S(1)}, u32[]{:S(2)}, u32[]{:S(2)}) collective-permute-start(bf16[2,2048]{1,0:T(2,128)(2,1)} %q_ref.1), channel_id=1, source_target_pairs={{0,1},{1,0},{2,3},{3,2},{4,5},{5,4},{6,7},{7,6},{8,9},{9,8},{10,11... | collective-permute-start | bytes 24584 | tf_op jit(solution)/shard_map/ppermute | solution.py:267
  4.4 34.2 %copy-start = (bf16[2048,512]{1,0:T(8,128)(2,1)S(1)}, bf16[2048,512]{1,0:T(8,128)(2,1)}, u32[]{:S(2)}) copy-start(bf16[2048,512]{1,0:T(8,128)(2,1)} %out_w_ref.1) | copy-start | bytes 6291460
  4.4 13.9 %collective-permute-start.3 = (bf16[128,256]{1,0:T(8,128)(2,1)S(1)}, bf16[128,256]{1,0:T(8,128)(2,1)S(1)}, u32[]{:S(2)}, u32[]{:S(2)}) collective-permute-start(bf16[128,256]{1,0:T(8,128)(2,1)S(1)} %get-tuple-element.36), channel_id=1, source_target_pairs={{0,192},{64,128},{128,64},{192,0},{1,193},{65,129},{129,65},{193,1... | collective-permute-start | bytes 196616 | tf_op jit(solution)/shard_map/ppermute | solution.py:265
  9.1 9.2 %collective-permute-start.4 = (bf16[128,256]{1,0:T(8,128)(2,1)S(1)}, bf16[128,256]{1,0:T(8,128)(2,1)S(1)}, u32[]{:S(2)}, u32[]{:S(2)}) collective-permute-start(bf16[128,256]{1,0:T(8,128)(2,1)S(1)} %get-tuple-element.37), channel_id=1, source_target_pairs={{0,128},{64,192},{128,0},{192,64},{1,129},{65,193},{129,1},{193,65... | collective-permute-start | bytes 196616 | tf_op jit(solution)/shard_map/ppermute | solution.py:265
  9.1 9.2 %collective-permute-start.5 = (bf16[128,256]{1,0:T(8,128)(2,1)S(1)}, bf16[128,256]{1,0:T(8,128)(2,1)S(1)}, u32[]{:S(2)}, u32[]{:S(2)}) collective-permute-start(bf16[128,256]{1,0:T(8,128)(2,1)S(1)} %get-tuple-element.38), channel_id=1, source_target_pairs={{0,64},{64,0},{128,192},{192,128},{1,65},{65,1},{129,193},{193,129... | collective-permute-start | bytes 196616 | tf_op jit(solution)/shard_map/ppermute | solution.py:265
  10.0 3.8 %collective-permute-start.1 = (bf16[4,2048]{1,0:T(4,128)(2,1)S(1)}, bf16[4,2048]{1,0:T(4,128)(2,1)S(1)}, u32[]{:S(2)}, u32[]{:S(2)}) collective-permute-start(bf16[4,2048]{1,0:T(4,128)(2,1)S(1)} %core_pair.1.mine_ref), channel_id=1, source_target_pairs={{0,2},{1,3},{2,0},{3,1},{4,6},{5,7},{6,4},{7,5},{8,10},{9,11},{10,... | collective-permute-start | bytes 49160 | tf_op jit(solution)/shard_map/ppermute | solution.py:267
  14.0 5.2 %collective-permute-start.2 = (bf16[8,2048]{1,0:T(8,128)(2,1)S(1)}, bf16[8,2048]{1,0:T(8,128)(2,1)S(1)}, u32[]{:S(2)}, u32[]{:S(2)}) collective-permute-start(bf16[8,2048]{1,0:T(8,128)(2,1)S(1)} %y_pair.1.mine_ref), channel_id=1, source_target_pairs={{0,6},{1,7},{2,4},{3,5},{4,2},{5,3},{6,0},{7,1},{8,14},{9,15},{10,... | collective-permute-start | bytes 98312 | tf_op jit(solution)/shard_map/ppermute | solution.py:267
  19.7 1.4 %collective-permute-start.6 = (bf16[144,256]{1,0:T(8,128)(2,1)S(1)}, bf16[144,256]{1,0:T(8,128)(2,1)S(1)}, u32[]{:S(2)}, u32[]{:S(2)}) collective-permute-start(bf16[144,256]{1,0:T(8,128)(2,1)S(1)} %get-tuple-element.43), channel_id=1, source_target_pairs={{0,1},{1,0},{2,3},{3,2},{4,5},{5,4},{6,7},{7,6},{8,9},{9,8},{10,11... | collective-permute-start | bytes 221192 | tf_op jit(solution)/shard_map/ppermute | solution.py:267
  21.1 4.4 %collective-permute-start.9 = (bf16[144,256]{1,0:T(8,128)(2,1)S(1)}, bf16[144,256]{1,0:T(8,128)(2,1)S(1)}, u32[]{:S(2)}, u32[]{:S(2)}) collective-permute-start(bf16[144,256]{1,0:T(8,128)(2,1)S(1)} %get-tuple-element.46), channel_id=1, source_target_pairs={{0,2},{1,3},{2,0},{3,1},{4,6},{5,7},{6,4},{7,5},{8,10},{9,11},{10,... | collective-permute-start | bytes 221192 | tf_op jit(solution)/shard_map/ppermute | solution.py:267
  21.6 4.4 %collective-permute-start.8 = (bf16[144,256]{1,0:T(8,128)(2,1)S(1)}, bf16[144,256]{1,0:T(8,128)(2,1)S(1)}, u32[]{:S(2)}, u32[]{:S(2)}) collective-permute-start(bf16[144,256]{1,0:T(8,128)(2,1)S(1)} %get-tuple-element.46), channel_id=1, source_target_pairs={{0,64},{64,0},{128,192},{192,128},{1,65},{65,1},{129,193},{193,129... | collective-permute-start | bytes 221192 | tf_op jit(solution)/shard_map/ppermute | solution.py:265
  23.0 5.5 %collective-permute-start.7 = (bf16[144,256]{1,0:T(8,128)(2,1)S(1)}, bf16[144,256]{1,0:T(8,128)(2,1)S(1)}, u32[]{:S(2)}, u32[]{:S(2)}) collective-permute-start(bf16[144,256]{1,0:T(8,128)(2,1)S(1)} %get-tuple-element.46), channel_id=1, source_target_pairs={{0,66},{1,67},{2,64},{3,65},{4,70},{5,71},{6,68},{7,69},{64,2},{65... | collective-permute-start | bytes 221192 | tf_op jit(solution)/shard_map/ppermute | solution.py:276
  28.5 6.3 %collective-permute-start.11 = (bf16[144,256]{1,0:T(8,128)(2,1)S(1)}, bf16[144,256]{1,0:T(8,128)(2,1)S(1)}, u32[]{:S(2)}, u32[]{:S(2)}) collective-permute-start(bf16[144,256]{1,0:T(8,128)(2,1)S(1)} %get-tuple-element.49), channel_id=1, source_target_pairs={{0,6},{1,135},{2,4},{3,133},{4,2},{5,131},{6,0},{7,129},{64,70},{6... | collective-permute-start | bytes 221192 | tf_op jit(solution)/shard_map/ppermute | solution.py:276
  31.6 5.6 %collective-permute-start.10 = (bf16[144,256]{1,0:T(8,128)(2,1)S(1)}, bf16[144,256]{1,0:T(8,128)(2,1)S(1)}, u32[]{:S(2)}, u32[]{:S(2)}) collective-permute-start(bf16[144,256]{1,0:T(8,128)(2,1)S(1)} %get-tuple-element.49), channel_id=1, source_target_pairs={{0,6},{1,129},{2,4},{3,131},{4,2},{5,133},{6,0},{7,135},{64,70},{6... | collective-permute-start | bytes 221192 | tf_op jit(solution)/shard_map/ppermute | solution.py:276
  37.2 1.4 %collective-permute-start.12 = (bf16[144,256]{1,0:T(8,128)(2,1)S(1)}, bf16[144,256]{1,0:T(8,128)(2,1)S(1)}, u32[]{:S(2)}, u32[]{:S(2)}) collective-permute-start(bf16[144,256]{1,0:T(8,128)(2,1)S(1)} %get-tuple-element.52), channel_id=1, source_target_pairs={{0,1},{1,0},{2,3},{3,2},{4,5},{5,4},{6,7},{7,6},{8,9},{9,8},{10,11... | collective-permute-start | bytes 221192 | tf_op jit(solution)/shard_map/ppermute | solution.py:267

commit v6 on v5

--- a/solution.py
+++ b/solution.py
@@ -133,34 +133,19 @@
     live_ref[...] = live.astype(F32)
 
 
-def pair_up(mine, other, mine_is_first):
-    rows = mine.shape[0]
-    place = lax.broadcasted_iota(jnp.int32, (2 * rows, rows), 0)
-    row = lax.broadcasted_iota(jnp.int32, (2 * rows, rows), 1)
-    lower, upper = (place == row).astype(F32), (place == row + rows).astype(F32)
-    first = mine_is_first.astype(F32)
-    mine_place = (lower * first + upper * (1.0 - first)).astype(BF)
-    other_place = (upper * first + lower * (1.0 - first)).astype(BF)
-    both = dot(mine_place, mine, ((1,), (0,))) + dot(other_place, other, ((1,), (0,)))
-    return both.astype(BF)
-
-
-def core_pair_kernel(mine_ref, other_ref, out_ref):
+def place_kernel(mine_ref, other_ref, out_ref):
     req_id = lax.axis_index("req")
-    out_ref[...] = pair_up(mine_ref[...], other_ref[...], req_id % 2 == 0)
-
-
-def y_pair_kernel(mine_ref, other_ref, out_ref):
-    req_id = lax.axis_index("req")
-    out_ref[...] = pair_up(mine_ref[...], other_ref[...], req_id // 2 % 2 == 0)
-
-
-def prompt_kernel(
-    mine_ref, other_ref, live_ref, kv_ref, cw_ref, cs_ref, kw_ref, ks_ref, send_ref
-):
+    place = lax.broadcasted_iota(jnp.int32, (NREQ, 2), 0)
+    row = lax.broadcasted_iota(jnp.int32, (NREQ, 2), 1)
+    mine = (place == req_id * 2 + row).astype(BF)
+    other = (place == (req_id ^ 1) * 2 + row).astype(BF)
+    placed = dot(mine, mine_ref[...], ((1,), (0,))) + dot(other, other_ref[...], ((1,), (0,)))
+    out_ref[...] = placed.astype(BF)
+
+
+def prompt_kernel(q_ref, live_ref, kv_ref, cw_ref, cs_ref, kw_ref, ks_ref, send_ref):
     new_kv = kv_ref[...]
-    req_id = lax.axis_index("req")
-    queries = rows_of(pair_up(mine_ref[...], other_ref[...], req_id < lax.axis_size("req") // 2))
+    queries = rows_of(q_ref[...])
     live = live_ref[...] > 0.5
     scores = dot(new_kv[:, 0:HD], queries, ((1,), (1,))) * FACTOR
     scores = jnp.where(live, scores, LOW)
@@ -293,18 +278,15 @@
     )
     chunks, other_queries = lax.optimization_barrier((chunks, other_queries))
 
-    def paired(kernel, mine, other, name):
-        return call(
-            kernel,
-            [(vmem(), mine), (vmem(), other)],
-            shape((2 * mine.shape[0], mine.shape[1]), BF),
-            name,
-        )
-
-    of_chip = paired(core_pair_kernel, queries, other_queries, "core_pair")
+    gathered = call(
+        place_kernel,
+        [(vmem(), queries), (vmem(), other_queries)],
+        shape((NREQ, queries.shape[1]), BF),
+        "place",
+    )
+    gathered = gathered + over(gathered, 0, 2)
     arrived = [over(chunks[flip], flip, 0) for flip in (3, 2, 1)]
-    of_half = paired(y_pair_kernel, of_chip, over(of_chip, 0, 2), "y_pair")
-    of_other_half = over(of_half, 0, 6)
+    gathered = gathered + over(gathered, 0, 6)
     cached_weighted, cached_stats, live = call(
         cached_kernel,
         [
@@ -326,7 +308,7 @@
         prompt_kernel,
         [
             (vmem(), value)
-            for value in (of_half, of_other_half, live, new_kv, cached_weighted, cached_stats)
+            for value in (gathered, live, new_kv, cached_weighted, cached_stats)
         ],
         STATE,
         "prompt",

time: 59.3 us -> 56.3 us (0.949)
  waiting for transfers between devices: 14.3 us -> 12.8 us
  starting transfers between devices: 17.6 us -> 16.5 us
    ppermute x6, waiting for transfers between devices: 6.09 us -> 3.66 us  [over(): lax.ppermute(value, 'req', [(i, i ^ req_flip) for i in range(req_count)])]
    ppermute x4, waiting for transfers between devices: 0.37 us -> 1.69 us  [over(): lax.ppermute(value, 'sec', [(i, i ^ sec_flip) for i in range(sec_count)])]
    ppermute x6, starting transfers between devices: 5.78 us -> 4.51 us  [over(): lax.ppermute(value, 'req', [(i, i ^ req_flip) for i in range(req_count)])]
    pallas_call x10 -> x9, Pallas kernels: 6.94 us -> 6.6 us  [call(): pl.pallas_call(kernel, out_shape=outs, in_specs=[spec for spec, _ in ins]...]
  transfers between devices with their start and end apart: 13 -> 13, of which waited for: 9 -> 10; matrix products, arithmetic and copies ran while one was open for 0% -> 0% of each run, Pallas kernels for 10% -> 10%
where the time goes in v6:
time: 56.3 us; the launch traced here: 55.5 us
  blocking collectives  18.8 us (33%)
  starting transfers between devices  16.5 us (29%)
  waiting for transfers between devices  12.8 us (23%)
  Pallas kernels  6.6 us (12%)
  other arithmetic  0.64 us (1%)
    all_to_all x1, blocking collectives, on_device(): pieces = lax.all_to_all(pieces, 'head', 0, 0, tiled=True)  18.8 us
    ppermute x3, waiting for transfers between devices, over_cores(): return lax.ppermute(value, ('sec', 'req'), pairs)  7.45 us
    ppermute x4, starting transfers between devices, over(): lax.ppermute(value, 'sec', [(i, i ^ sec_flip) for i in range(sec_count)])  6.74 us
    pallas_call x9, Pallas kernels, call(): pl.pallas_call(kernel, out_shape=outs, in_specs=[spec for spec, _ in ins]...  6.6 us
    ppermute x3, starting transfers between devices, over_cores(): return lax.ppermute(value, ('sec', 'req'), pairs)  5.25 us
    ppermute x6, starting transfers between devices, over(): lax.ppermute(value, 'req', [(i, i ^ req_flip) for i in range(req_count)])  4.51 us
    ppermute x6, waiting for transfers between devices, over(): lax.ppermute(value, 'req', [(i, i ^ req_flip) for i in range(req_count)])  3.66 us
    ppermute x4, waiting for transfers between devices, over(): lax.ppermute(value, 'sec', [(i, i ^ sec_flip) for i in range(sec_count)])  1.69 us
  transfers between devices with their start and end apart: 13, of which 10 were waited for; matrix products, arithmetic and copies ran while one was open for 0% of the time, Pallas kernels for 10%

profile of v6, /device:TPU:2, one launch (start us, length us, event | category | flops | bytes accessed | tf_op | source)
XLA Modules:
  0.0 55.5 jit_solution(6994205603500492682)
XLA Ops:
  0.0 0.0 copy-start.2
  0.0 0.0 copy-start.6
  0.0 0.0 copy-start.5
  0.0 0.0 copy-start.4
  0.0 0.0 copy-start.3
  0.0 0.0 copy-start.1
  0.0 0.1 collective-permute-start
  0.1 4.2 %new_kv.1 = (bf16[128,256]{1,0:T(8,128)(2,1)S(1)}, bf16[128,256]{1,0:T(8,128)(2,1)S(1)}, bf16[128,256]{1,0:T(8,128)(2,1)S(1)}, bf16[128,256]{1,0:T(8,128)(2,1)S(1)}) custom-call(bf16[512,4096]{1,0:T(8,128)(2,1)} %x_ref.1, bf16[4096,256]{1,0:T(8,128)(2,1)} %w_ref.1), custom_call_target="tpu_custom_call" | custom-call | flops 1073741824 | bytes 6291456 | tf_op jit(solution)/shard_map/new_kv/pallas_call | solution.py:226
  4.4 0.0 copy-start
  4.4 0.0 collective-permute-done.other_ref
  4.4 0.0 copy-done.2
  4.4 0.2 place.1
  4.6 1.7 %collective-permute-start.1 = (bf16[16,2048]{1,0:T(8,128)(2,1)S(1)}, bf16[16,2048]{1,0:T(8,128)(2,1)S(1)}, u32[]{:S(2)}, u32[]{:S(2)}) collective-permute-start(bf16[16,2048]{1,0:T(8,128)(2,1)S(1)} %place.1), channel_id=1, source_target_pairs={{0,2},{1,3},{2,0},{3,1},{4,6},{5,7},{6,4},{7,5},{8,10},{9,11},{10,... | collective-permute-start | bytes 196616 | tf_op jit(solution)/shard_map/ppermute | solution.py:252
  6.2 4.6 %collective-permute-start.3 = (bf16[128,256]{1,0:T(8,128)(2,1)S(1)}, bf16[128,256]{1,0:T(8,128)(2,1)S(1)}, u32[]{:S(2)}, u32[]{:S(2)}) collective-permute-start(bf16[128,256]{1,0:T(8,128)(2,1)S(1)} %get-tuple-element.36), channel_id=1, source_target_pairs={{0,192},{64,128},{128,64},{192,0},{1,193},{65,129},{129,65},{193,1... | collective-permute-start | bytes 196616 | tf_op jit(solution)/shard_map/ppermute | solution.py:250
  10.9 0.0 collective-permute-start.4
  10.9 0.6 %collective-permute-start.5 = (bf16[128,256]{1,0:T(8,128)(2,1)S(1)}, bf16[128,256]{1,0:T(8,128)(2,1)S(1)}, u32[]{:S(2)}, u32[]{:S(2)}) collective-permute-start(bf16[128,256]{1,0:T(8,128)(2,1)S(1)} %get-tuple-element.38), channel_id=1, source_target_pairs={{0,64},{64,0},{128,192},{192,128},{1,65},{65,1},{129,193},{193,129... | collective-permute-start | bytes 196616 | tf_op jit(solution)/shard_map/ppermute | solution.py:250
  11.4 0.0 collective-permute-done.1
  11.5 2.3 %collective-permute-start.2 = (bf16[16,2048]{1,0:T(8,128)(2,1)S(1)}, bf16[16,2048]{1,0:T(8,128)(2,1)S(1)}, u32[]{:S(2)}, u32[]{:S(2)}) collective-permute-start(bf16[16,2048]{1,0:T(8,128)(2,1)S(1)} %add.6), channel_id=1, source_target_pairs={{0,6},{1,7},{2,4},{3,5},{4,2},{5,3},{6,0},{7,1},{8,14},{9,15},{10,... | collective-permute-start | bytes 196616 | tf_op jit(solution)/shard_map/ppermute | solution.py:252
  13.7 0.0 copy-done.6
  13.7 0.0 copy-done.5
  13.7 0.0 copy-done.4
  13.7 0.0 copy-done.3
  13.8 0.0 copy-done.1
  13.8 1.2 %cached.1 = (f32[128,256]{1,0:T(8,128)S(1)}, f32[8,256]{1,0:T(8,128)S(1)}, f32[128,256]{1,0:T(8,128)S(1)}) custom-call(s32[1,256]{1,0:T(1,128)S(1)} %bitcast.6, s32[1,256]{1,0:T(1,128)S(1)} %bitcast.7, s32[1,256]{1,0:T(1,128)S(1)} %bitcast.8, s32[1,2]{1,0:T(1,128)S(1)} %bitcast.9, bf16[2,2048]{1,0:T(2,128)(2,1)S(1)} %copy-done.2, ...), custom_call_target="tpu_custom_call" | custom-call | flops 268435456 | bytes 1059848 | tf_op jit(solution)/shard_map/cached/pallas_call | solution.py:226
  14.9 0.0 collective-permute-done.3.a_ref
  14.9 1.3 %collective-permute-done.4.b_ref = bf16[128,256]{1,0:T(8,128)(2,1)S(1)} collective-permute-done((bf16[128,256]{1,0:T(8,128)(2,1)S(1)}, bf16[128,256]{1,0:T(8,128)(2,1)S(1)}, u32[]{:S(2)}, u32[]{:S(2)}) %collective-permute-start.4) | collective-permute-done | bytes 65568 | tf_op jit(solution)/shard_map/ppermute | solution.py:250
  16.2 0.3 collective-permute-done.5.c_ref
  16.6 0.5 collective-permute-done.2
  17.1 0.4 prompt.1
  17.4 0.1 collective-permute-start.6
  17.5 1.3 %collective-permute-done.6.refs_0_ = bf16[144,256]{1,0:T(8,128)(2,1)S(1)} collective-permute-done((bf16[144,256]{1,0:T(8,128)(2,1)S(1)}, bf16[144,256]{1,0:T(8,128)(2,1)S(1)}, u32[]{:S(2)}, u32[]{:S(2)}) %collective-permute-start.6) | collective-permute-done | bytes 73760 | tf_op jit(solution)/shard_map/ppermute | solution.py:252
  18.8 0.1 join_core.1
  18.9 0.1 collective-permute-start.9
  19.0 1.5 %collective-permute-start.8 = (bf16[144,256]{1,0:T(8,128)(2,1)S(1)}, bf16[144,256]{1,0:T(8,128)(2,1)S(1)}, u32[]{:S(2)}, u32[]{:S(2)}) collective-permute-start(bf16[144,256]{1,0:T(8,128)(2,1)S(1)} %get-tuple-element.46), channel_id=1, source_target_pairs={{0,64},{64,0},{128,192},{192,128},{1,65},{65,1},{129,193},{193,129... | collective-permute-start | bytes 221192 | tf_op jit(solution)/shard_map/ppermute | solution.py:250
  20.5 1.9 %collective-permute-start.7 = (bf16[144,256]{1,0:T(8,128)(2,1)S(1)}, bf16[144,256]{1,0:T(8,128)(2,1)S(1)}, u32[]{:S(2)}, u32[]{:S(2)}) collective-permute-start(bf16[144,256]{1,0:T(8,128)(2,1)S(1)} %get-tuple-element.46), channel_id=1, source_target_pairs={{0,66},{1,67},{2,64},{3,65},{4,70},{5,71},{6,68},{7,69},{64,2},{65... | collective-permute-start | bytes 221192 | tf_op jit(solution)/shard_map/ppermute | solution.py:261
  22.4 0.9 %collective-permute-done.9.refs_2_ = bf16[144,256]{1,0:T(8,128)(2,1)S(1)} collective-permute-done((bf16[144,256]{1,0:T(8,128)(2,1)S(1)}, bf16[144,256]{1,0:T(8,128)(2,1)S(1)}, u32[]{:S(2)}, u32[]{:S(2)}) %collective-permute-start.9) | collective-permute-done | bytes 73760 | tf_op jit(solution)/shard_map/ppermute | solution.py:252
  23.3 0.1 collective-permute-done.8.refs_1_
  23.4 2.8 %collective-permute-done.7.refs_0_ = bf16[144,256]{1,0:T(8,128)(2,1)S(1)} collective-permute-done((bf16[144,256]{1,0:T(8,128)(2,1)S(1)}, bf16[144,256]{1,0:T(8,128)(2,1)S(1)}, u32[]{:S(2)}, u32[]{:S(2)}) %collective-permute-start.7) | collective-permute-done | bytes 73760 | tf_op jit(solution)/shard_map/ppermute | solution.py:261
  26.2 0.1 join_near.1
  26.3 2.4 %collective-permute-start.11 = (bf16[144,256]{1,0:T(8,128)(2,1)S(1)}, bf16[144,256]{1,0:T(8,128)(2,1)S(1)}, u32[]{:S(2)}, u32[]{:S(2)}) collective-permute-start(bf16[144,256]{1,0:T(8,128)(2,1)S(1)} %get-tuple-element.49), channel_id=1, source_target_pairs={{0,6},{1,135},{2,4},{3,133},{4,2},{5,131},{6,0},{7,129},{64,70},{6... | collective-permute-start | bytes 221192 | tf_op jit(solution)/shard_map/ppermute | solution.py:261
  28.7 1.0 %collective-permute-start.10 = (bf16[144,256]{1,0:T(8,128)(2,1)S(1)}, bf16[144,256]{1,0:T(8,128)(2,1)S(1)}, u32[]{:S(2)}, u32[]{:S(2)}) collective-permute-start(bf16[144,256]{1,0:T(8,128)(2,1)S(1)} %get-tuple-element.49), channel_id=1, source_target_pairs={{0,6},{1,129},{2,4},{3,131},{4,2},{5,133},{6,0},{7,135},{64,70},{6... | collective-permute-start | bytes 221192 | tf_op jit(solution)/shard_map/ppermute | solution.py:261
  29.7 2.7 %collective-permute-done.11.second_ref = bf16[144,256]{1,0:T(8,128)(2,1)S(1)} collective-permute-done((bf16[144,256]{1,0:T(8,128)(2,1)S(1)}, bf16[144,256]{1,0:T(8,128)(2,1)S(1)}, u32[]{:S(2)}, u32[]{:S(2)}) %collective-permute-start.11) | collective-permute-done | bytes 73760 | tf_op jit(solution)/shard_map/ppermute | solution.py:261
  32.3 1.9 %collective-permute-done.10.first_ref = bf16[144,256]{1,0:T(8,128)(2,1)S(1)} collective-permute-done((bf16[144,256]{1,0:T(8,128)(2,1)S(1)}, bf16[144,256]{1,0:T(8,128)(2,1)S(1)}, u32[]{:S(2)}, u32[]{:S(2)}) %collective-permute-start.10) | collective-permute-done | bytes 73760 | tf_op jit(solution)/shard_map/ppermute | solution.py:261
  34.3 0.3 collective-permute-start.12
  34.6 1.1 %collective-permute-done.12.got_ref = bf16[144,256]{1,0:T(8,128)(2,1)S(1)} collective-permute-done((bf16[144,256]{1,0:T(8,128)(2,1)S(1)}, bf16[144,256]{1,0:T(8,128)(2,1)S(1)}, u32[]{:S(2)}, u32[]{:S(2)}) %collective-permute-start.12) | collective-permute-done | bytes 73760 | tf_op jit(solution)/shard_map/ppermute | solution.py:252
  35.7 0.0 copy-done
  35.7 0.5 project.1
  36.2 18.8 %all_to_all.5 = bf16[8,2,512]{2,1,0:T(2,128)(2,1)S(1)} all-to-all(bf16[8,2,512]{2,1,0:T(2,128)(2,1)S(1)} %reshape.19), channel_id=1, replica_groups=mesh['sec'=4,'head'=8,'req'=8] {'head'}, dimensions={0} | all-to-all | bytes 32768 | tf_op jit(solution)/shard_map/all_to_all | solution.py:342
  54.9 0.6 %reduce_sum.12 = bf16[2,512]{1,0:T(2,128)(2,1)} reduce(bf16[8,2,512]{2,1,0:T(2,128)(2,1)S(1)} %all_to_all.5, bf16[]{:T(256)} %constant.2.clone.1), dimensions={0}, to_apply=%region_0.0 | reduce | flops 7168 | bytes 18434 | tf_op jit(solution)/shard_map/reduce_sum | solution.py:343
  (5 shorter events, 0.1 us)
Async XLA Ops:
  0.0 4.4 %copy-start.2 = (bf16[2,2048]{1,0:T(2,128)(2,1)S(1)}, bf16[2,2048]{1,0:T(2,128)(2,1)}, u32[]{:S(2)}) copy-start(bf16[2,2048]{1,0:T(2,128)(2,1)} %q_ref.1) | copy-start | bytes 24580
  0.0 13.7 %copy-start.6 = (s32[2]{0:T(128)S(1)}, s32[2]{0:T(128)}, u32[]{:S(2)}) copy-start(s32[2]{0:T(128)} %param.17) | copy-start | bytes 28
  0.0 13.7 %copy-start.5 = (s32[256]{0:T(256)S(1)}, s32[256]{0:T(256)}, u32[]{:S(2)}) copy-start(s32[256]{0:T(256)} %param.16) | copy-start | bytes 3076
  0.0 13.7 %copy-start.4 = (s32[256]{0:T(256)S(1)}, s32[256]{0:T(256)}, u32[]{:S(2)}) copy-start(s32[256]{0:T(256)} %param.15) | copy-start | bytes 3076
  0.0 13.7 %copy-start.3 = (s32[256,1]{0,1:T(1,128)S(1)}, s32[256,1]{0,1:T(1,128)}, u32[]{:S(2)}) copy-start(s32[256,1]{0,1:T(1,128)} %param.14) | copy-start | bytes 3076
  0.0 13.7 %copy-start.1 = (bf16[2,1024,1,256]{3,1,2,0:T(8,128)(2,1)S(1)}, bf16[2,1024,1,256]{3,1,2,0:T(8,128)(2,1)}, u32[]{:S(2)}) copy-start(bf16[2,1024,1,256]{3,1,2,0:T(8,128)(2,1)} %param.12) | copy-start | bytes 3145732
  0.0 4.3 %collective-permute-start = (bf16[2,2048]{1,0:T(2,128)(2,1)}, bf16[2,2048]{1,0:T(2,128)(2,1)S(1)}, u32[]{:S(2)}, u32[]{:S(2)}) collective-permute-start(bf16[2,2048]{1,0:T(2,128)(2,1)} %q_ref.1), channel_id=1, source_target_pairs={{0,1},{1,0},{2,3},{3,2},{4,5},{5,4},{6,7},{7,6},{8,9},{9,8},{10,11... | collective-permute-start | bytes 24584 | tf_op jit(solution)/shard_map/ppermute | solution.py:252
  4.4 31.3 %copy-start = (bf16[2048,512]{1,0:T(8,128)(2,1)S(1)}, bf16[2048,512]{1,0:T(8,128)(2,1)}, u32[]{:S(2)}) copy-start(bf16[2048,512]{1,0:T(8,128)(2,1)} %out_w_ref.1) | copy-start | bytes 6291460
  4.6 6.9 %collective-permute-start.1 = (bf16[16,2048]{1,0:T(8,128)(2,1)S(1)}, bf16[16,2048]{1,0:T(8,128)(2,1)S(1)}, u32[]{:S(2)}, u32[]{:S(2)}) collective-permute-start(bf16[16,2048]{1,0:T(8,128)(2,1)S(1)} %place.1), channel_id=1, source_target_pairs={{0,2},{1,3},{2,0},{3,1},{4,6},{5,7},{6,4},{7,5},{8,10},{9,11},{10,... | collective-permute-start | bytes 196616 | tf_op jit(solution)/shard_map/ppermute | solution.py:252
  6.2 8.7 %collective-permute-start.3 = (bf16[128,256]{1,0:T(8,128)(2,1)S(1)}, bf16[128,256]{1,0:T(8,128)(2,1)S(1)}, u32[]{:S(2)}, u32[]{:S(2)}) collective-permute-start(bf16[128,256]{1,0:T(8,128)(2,1)S(1)} %get-tuple-element.36), channel_id=1, source_target_pairs={{0,192},{64,128},{128,64},{192,0},{1,193},{65,129},{129,65},{193,1... | collective-permute-start | bytes 196616 | tf_op jit(solution)/shard_map/ppermute | solution.py:250
  10.9 5.3 %collective-permute-start.4 = (bf16[128,256]{1,0:T(8,128)(2,1)S(1)}, bf16[128,256]{1,0:T(8,128)(2,1)S(1)}, u32[]{:S(2)}, u32[]{:S(2)}) collective-permute-start(bf16[128,256]{1,0:T(8,128)(2,1)S(1)} %get-tuple-element.37), channel_id=1, source_target_pairs={{0,128},{64,192},{128,0},{192,64},{1,129},{65,193},{129,1},{193,65... | collective-permute-start | bytes 196616 | tf_op jit(solution)/shard_map/ppermute | solution.py:250
  10.9 5.7 %collective-permute-start.5 = (bf16[128,256]{1,0:T(8,128)(2,1)S(1)}, bf16[128,256]{1,0:T(8,128)(2,1)S(1)}, u32[]{:S(2)}, u32[]{:S(2)}) collective-permute-start(bf16[128,256]{1,0:T(8,128)(2,1)S(1)} %get-tuple-element.38), channel_id=1, source_target_pairs={{0,64},{64,0},{128,192},{192,128},{1,65},{65,1},{129,193},{193,129... | collective-permute-start | bytes 196616 | tf_op jit(solution)/shard_map/ppermute | solution.py:250
  11.5 5.6 %collective-permute-start.2 = (bf16[16,2048]{1,0:T(8,128)(2,1)S(1)}, bf16[16,2048]{1,0:T(8,128)(2,1)S(1)}, u32[]{:S(2)}, u32[]{:S(2)}) collective-permute-start(bf16[16,2048]{1,0:T(8,128)(2,1)S(1)} %add.6), channel_id=1, source_target_pairs={{0,6},{1,7},{2,4},{3,5},{4,2},{5,3},{6,0},{7,1},{8,14},{9,15},{10,... | collective-permute-start | bytes 196616 | tf_op jit(solution)/shard_map/ppermute | solution.py:252
  17.4 1.4 %collective-permute-start.6 = (bf16[144,256]{1,0:T(8,128)(2,1)S(1)}, bf16[144,256]{1,0:T(8,128)(2,1)S(1)}, u32[]{:S(2)}, u32[]{:S(2)}) collective-permute-start(bf16[144,256]{1,0:T(8,128)(2,1)S(1)} %get-tuple-element.43), channel_id=1, source_target_pairs={{0,1},{1,0},{2,3},{3,2},{4,5},{5,4},{6,7},{7,6},{8,9},{9,8},{10,11... | collective-permute-start | bytes 221192 | tf_op jit(solution)/shard_map/ppermute | solution.py:252
  18.9 4.4 %collective-permute-start.9 = (bf16[144,256]{1,0:T(8,128)(2,1)S(1)}, bf16[144,256]{1,0:T(8,128)(2,1)S(1)}, u32[]{:S(2)}, u32[]{:S(2)}) collective-permute-start(bf16[144,256]{1,0:T(8,128)(2,1)S(1)} %get-tuple-element.46), channel_id=1, source_target_pairs={{0,2},{1,3},{2,0},{3,1},{4,6},{5,7},{6,4},{7,5},{8,10},{9,11},{10,... | collective-permute-start | bytes 221192 | tf_op jit(solution)/shard_map/ppermute | solution.py:252
  19.0 4.4 %collective-permute-start.8 = (bf16[144,256]{1,0:T(8,128)(2,1)S(1)}, bf16[144,256]{1,0:T(8,128)(2,1)S(1)}, u32[]{:S(2)}, u32[]{:S(2)}) collective-permute-start(bf16[144,256]{1,0:T(8,128)(2,1)S(1)} %get-tuple-element.46), channel_id=1, source_target_pairs={{0,64},{64,0},{128,192},{192,128},{1,65},{65,1},{129,193},{193,129... | collective-permute-start | bytes 221192 | tf_op jit(solution)/shard_map/ppermute | solution.py:250
  20.5 5.7 %collective-permute-start.7 = (bf16[144,256]{1,0:T(8,128)(2,1)S(1)}, bf16[144,256]{1,0:T(8,128)(2,1)S(1)}, u32[]{:S(2)}, u32[]{:S(2)}) collective-permute-start(bf16[144,256]{1,0:T(8,128)(2,1)S(1)} %get-tuple-element.46), channel_id=1, source_target_pairs={{0,66},{1,67},{2,64},{3,65},{4,70},{5,71},{6,68},{7,69},{64,2},{65... | collective-permute-start | bytes 221192 | tf_op jit(solution)/shard_map/ppermute | solution.py:261
  26.3 6.0 %collective-permute-start.11 = (bf16[144,256]{1,0:T(8,128)(2,1)S(1)}, bf16[144,256]{1,0:T(8,128)(2,1)S(1)}, u32[]{:S(2)}, u32[]{:S(2)}) collective-permute-start(bf16[144,256]{1,0:T(8,128)(2,1)S(1)} %get-tuple-element.49), channel_id=1, source_target_pairs={{0,6},{1,135},{2,4},{3,133},{4,2},{5,131},{6,0},{7,129},{64,70},{6... | collective-permute-start | bytes 221192 | tf_op jit(solution)/shard_map/ppermute | solution.py:261
  28.7 5.6 %collective-permute-start.10 = (bf16[144,256]{1,0:T(8,128)(2,1)S(1)}, bf16[144,256]{1,0:T(8,128)(2,1)S(1)}, u32[]{:S(2)}, u32[]{:S(2)}) collective-permute-start(bf16[144,256]{1,0:T(8,128)(2,1)S(1)} %get-tuple-element.49), channel_id=1, source_target_pairs={{0,6},{1,129},{2,4},{3,131},{4,2},{5,133},{6,0},{7,135},{64,70},{6... | collective-permute-start | bytes 221192 | tf_op jit(solution)/shard_map/ppermute | solution.py:261
  34.3 1.4 %collective-permute-start.12 = (bf16[144,256]{1,0:T(8,128)(2,1)S(1)}, bf16[144,256]{1,0:T(8,128)(2,1)S(1)}, u32[]{:S(2)}, u32[]{:S(2)}) collective-permute-start(bf16[144,256]{1,0:T(8,128)(2,1)S(1)} %get-tuple-element.52), channel_id=1, source_target_pairs={{0,1},{1,0},{2,3},{3,2},{4,5},{5,4},{6,7},{7,6},{8,9},{9,8},{10,11... | collective-permute-start | bytes 221192 | tf_op jit(solution)/shard_map/ppermute | solution.py:252

commit v7 on v6

--- a/solution.py
+++ b/solution.py
@@ -62,20 +62,12 @@
     ref[HD : HD + STAT, :] = packed_stats(peak, total)
 
 
-def kv_kernel(x_ref, w_ref, out0, out1, out2, out3, x_buf, w_buf, sems):
+def kv_kernel(x_ref, w_ref, out0, out1, out2, out3):
     sec_id = lax.axis_index("sec")
     rows = out0.shape[0]
-    copies = (
-        pltpu.make_async_copy(w_ref, w_buf, sems.at[0]),
-        pltpu.make_async_copy(x_ref, x_buf, sems.at[1]),
-    )
-    for copy in copies:
-        copy.start()
-    for copy in copies:
-        copy.wait()
     for flip, out in enumerate((out0, out1, out2, out3)):
         start = pl.multiple_of((sec_id ^ flip) * rows, rows)
-        out[...] = dot(x_buf[pl.ds(start, rows), :], w_buf[...], ((1,), (0,))).astype(BF)
+        out[...] = dot(x_ref[pl.ds(start, rows), :], w_ref[...], ((1,), (0,))).astype(BF)
 
 
 def sum_kernel(own_ref, a_ref, b_ref, c_ref, out_ref):
@@ -133,14 +125,11 @@
     live_ref[...] = live.astype(F32)
 
 
-def place_kernel(mine_ref, other_ref, out_ref):
-    req_id = lax.axis_index("req")
+def place_kernel(mine_ref, out_ref):
     place = lax.broadcasted_iota(jnp.int32, (NREQ, 2), 0)
     row = lax.broadcasted_iota(jnp.int32, (NREQ, 2), 1)
-    mine = (place == req_id * 2 + row).astype(BF)
-    other = (place == (req_id ^ 1) * 2 + row).astype(BF)
-    placed = dot(mine, mine_ref[...], ((1,), (0,))) + dot(other, other_ref[...], ((1,), (0,)))
-    out_ref[...] = placed.astype(BF)
+    mine = (place == lax.axis_index("req") * 2 + row).astype(BF)
+    out_ref[...] = dot(mine, mine_ref[...], ((1,), (0,))).astype(BF)
 
 
 def prompt_kernel(q_ref, live_ref, kv_ref, cw_ref, cs_ref, kw_ref, ks_ref, send_ref):
@@ -261,30 +250,22 @@
         return lax.ppermute(value, ("sec", "req"), pairs)
 
     chunk = shape((rows, width), BF)
-    hbm = pl.BlockSpec(memory_space=pltpu.HBM)
-    other_queries = over(queries, 0, 1)
+    gathered = call(
+        place_kernel,
+        [(vmem(), queries)],
+        shape((NREQ, queries.shape[1]), BF),
+        "place",
+        flops=2_000_000_000,
+    )
+    gathered = gathered + over(gathered, 0, 1)
+    gathered = gathered + over(gathered, 0, 2)
     chunks = call(
         kv_kernel,
-        [(hbm, prompt_x), (hbm, w_kv)],
+        [(vmem(), prompt_x), (vmem(), w_kv)],
         (chunk, chunk, chunk, chunk),
         "new_kv",
         flops=2 * prompt_x.size * width,
-        scratch=(
-            pltpu.VMEM(prompt_x.shape, BF),
-            pltpu.VMEM(w_kv.shape, BF),
-            pltpu.SemaphoreType.DMA((2,)),
-        ),
-        grant=52,
-    )
-    chunks, other_queries = lax.optimization_barrier((chunks, other_queries))
-
-    gathered = call(
-        place_kernel,
-        [(vmem(), queries), (vmem(), other_queries)],
-        shape((NREQ, queries.shape[1]), BF),
-        "place",
-    )
-    gathered = gathered + over(gathered, 0, 2)
+    )
     arrived = [over(chunks[flip], flip, 0) for flip in (3, 2, 1)]
     gathered = gathered + over(gathered, 0, 6)
     cached_weighted, cached_stats, live = call(
@@ -316,7 +297,7 @@
     )
     for name, moves in (
         ("join_core", ((0, 1),)),
-        ("join_near", ((1, 2), (1, 0), (0, 2))),
+        ("join_near", ((1, 0), (0, 2), (1, 2))),
     ):
         got = [over(kept[2], *flips) for flips in moves]
         kept = call(

time: 56.3 us -> 54.8 us (0.973)
  Pallas kernels: 6.6 us -> 3.72 us
  waiting for transfers between devices: 12.8 us -> 13.9 us
  blocking collectives: 18.8 us -> 17.9 us
  local copies, waits for them, and re-layouts: 0.06 us -> 0.92 us
    pallas_call x9, Pallas kernels: 6.6 us -> 3.72 us  [call(): pl.pallas_call(kernel, out_shape=outs, in_specs=[spec for spec, _ in ins]...]
    ppermute x6, starting transfers between devices: 4.51 us -> 6.73 us  [over(): lax.ppermute(value, 'req', [(i, i ^ req_flip) for i in range(req_count)])]
    ppermute x6, waiting for transfers between devices: 3.66 us -> 5.1 us  [over(): lax.ppermute(value, 'req', [(i, i ^ req_flip) for i in range(req_count)])]
    ppermute x3, starting transfers between devices: 5.25 us -> 3.83 us  [over_cores(): return lax.ppermute(value, ('sec', 'req'), pairs)]
    all_to_all x1, blocking collectives: 18.8 us -> 17.9 us  [on_device(): pieces = lax.all_to_all(pieces, 'head', 0, 0, tiled=True)]
    unnamed x14 -> x18, local copies, waits for them, and re-layouts: 0.03 us -> 0.89 us
    ppermute x4, starting transfers between devices: 6.74 us -> 6.03 us  [over(): lax.ppermute(value, 'sec', [(i, i ^ sec_flip) for i in range(sec_count)])]
    ppermute x3, waiting for transfers between devices: 7.45 us -> 6.82 us  [over_cores(): return lax.ppermute(value, ('sec', 'req'), pairs)]
  transfers between devices with their start and end apart: 13 -> 13, of which waited for: 10 -> 11; matrix products, arithmetic and copies ran while one was open for 0% -> 0% of each run, Pallas kernels for 10% -> 5%
where the time goes in v7:
time: 54.8 us; the launch traced here: 53.8 us
  blocking collectives  17.9 us (33%)
  starting transfers between devices  16.6 us (30%)
  waiting for transfers between devices  13.9 us (25%)
  Pallas kernels  3.72 us (7%)
  local copies, waits for them, and re-layouts  0.92 us (2%)
  other arithmetic  0.66 us (1%)
    all_to_all x1, blocking collectives, on_device(): pieces = lax.all_to_all(pieces, 'head', 0, 0, tiled=True)  17.9 us
    ppermute x3, waiting for transfers between devices, over_cores(): return lax.ppermute(value, ('sec', 'req'), pairs)  6.82 us
    ppermute x6, starting transfers between devices, over(): lax.ppermute(value, 'req', [(i, i ^ req_flip) for i in range(req_count)])  6.73 us
    ppermute x4, starting transfers between devices, over(): lax.ppermute(value, 'sec', [(i, i ^ sec_flip) for i in range(sec_count)])  6.03 us
    ppermute x6, waiting for transfers between devices, over(): lax.ppermute(value, 'req', [(i, i ^ req_flip) for i in range(req_count)])  5.1 us
    ppermute x3, starting transfers between devices, over_cores(): return lax.ppermute(value, ('sec', 'req'), pairs)  3.83 us
    pallas_call x9, Pallas kernels, call(): pl.pallas_call(kernel, out_shape=outs, in_specs=[spec for spec, _ in ins]...  3.72 us
    ppermute x4, waiting for transfers between devices, over(): lax.ppermute(value, 'sec', [(i, i ^ sec_flip) for i in range(sec_count)])  1.97 us
  transfers between devices with their start and end apart: 13, of which 11 were waited for; matrix products, arithmetic and copies ran while one was open for 0% of the time, Pallas kernels for 5%

profile of v7, /device:TPU:2, one launch (start us, length us, event | category | flops | bytes accessed | tf_op | source)
XLA Modules:
  0.0 53.8 jit_solution(5183424477424119501)
XLA Ops:
  0.0 0.0 copy-start.1
  0.0 0.0 copy-start
  0.0 0.0 copy-start.4
  0.0 0.8 %copy-done.4 = bf16[2,2048]{1,0:T(2,128)(2,1)S(1)} copy-done((bf16[2,2048]{1,0:T(2,128)(2,1)S(1)}, bf16[2,2048]{1,0:T(2,128)(2,1)}, u32[]{:S(2)}) %copy-start.4) | copy-done | bytes 8216
  0.9 0.1 place.1
  1.0 0.1 collective-permute-start
  1.1 1.2 %collective-permute-done = bf16[16,2048]{1,0:T(8,128)(2,1)S(1)} collective-permute-done((bf16[16,2048]{1,0:T(8,128)(2,1)S(1)}, bf16[16,2048]{1,0:T(8,128)(2,1)S(1)}, u32[]{:S(2)}, u32[]{:S(2)}) %collective-permute-start) | collective-permute-done | bytes 65568 | tf_op jit(solution)/shard_map/ppermute | solution.py:241
  2.4 0.0 copy-start.3
  2.4 0.0 copy-start.5
  2.4 0.0 copy-start.6
  2.4 0.0 copy-start.7
  2.4 0.0 copy-start.8
  2.4 1.7 %collective-permute-start.1 = (bf16[16,2048]{1,0:T(8,128)(2,1)S(1)}, bf16[16,2048]{1,0:T(8,128)(2,1)S(1)}, u32[]{:S(2)}, u32[]{:S(2)}) collective-permute-start(bf16[16,2048]{1,0:T(8,128)(2,1)S(1)} %add.9), channel_id=1, source_target_pairs={{0,2},{1,3},{2,0},{3,1},{4,6},{5,7},{6,4},{7,5},{8,10},{9,11},{10,... | collective-permute-start | bytes 196616 | tf_op jit(solution)/shard_map/ppermute | solution.py:241
  4.1 0.0 copy-done.1
  4.1 0.0 copy-done
  4.1 1.4 %new_kv.1 = (bf16[128,256]{1,0:T(8,128)(2,1)S(1)}, bf16[128,256]{1,0:T(8,128)(2,1)S(1)}, bf16[128,256]{1,0:T(8,128)(2,1)S(1)}, bf16[128,256]{1,0:T(8,128)(2,1)S(1)}) custom-call(bf16[512,4096]{1,0:T(8,128)(2,1)S(1)} %copy-done, bf16[4096,256]{1,0:T(8,128)(2,1)S(1)} %copy-done.1), custom_call_target="tpu_custom_call" | custom-call | flops 1073741824 | bytes 6291456 | tf_op jit(solution)/shard_map/new_kv/pallas_call | solution.py:215
  5.5 0.0 copy-start.2
  5.5 4.7 %collective-permute-start.3 = (bf16[128,256]{1,0:T(8,128)(2,1)S(1)}, bf16[128,256]{1,0:T(8,128)(2,1)S(1)}, u32[]{:S(2)}, u32[]{:S(2)}) collective-permute-start(bf16[128,256]{1,0:T(8,128)(2,1)S(1)} %get-tuple-element.26), channel_id=1, source_target_pairs={{0,192},{64,128},{128,64},{192,0},{1,193},{65,129},{129,65},{193,1... | collective-permute-start | bytes 196616 | tf_op jit(solution)/shard_map/ppermute | solution.py:239
  10.2 0.0 collective-permute-start.4
  10.2 0.7 %collective-permute-start.5 = (bf16[128,256]{1,0:T(8,128)(2,1)S(1)}, bf16[128,256]{1,0:T(8,128)(2,1)S(1)}, u32[]{:S(2)}, u32[]{:S(2)}) collective-permute-start(bf16[128,256]{1,0:T(8,128)(2,1)S(1)} %get-tuple-element.28), channel_id=1, source_target_pairs={{0,64},{64,0},{128,192},{192,128},{1,65},{65,1},{129,193},{193,129... | collective-permute-start | bytes 196616 | tf_op jit(solution)/shard_map/ppermute | solution.py:239
  10.8 0.0 collective-permute-done.1
  10.9 2.3 %collective-permute-start.2 = (bf16[16,2048]{1,0:T(8,128)(2,1)S(1)}, bf16[16,2048]{1,0:T(8,128)(2,1)S(1)}, u32[]{:S(2)}, u32[]{:S(2)}) collective-permute-start(bf16[16,2048]{1,0:T(8,128)(2,1)S(1)} %add.10), channel_id=1, source_target_pairs={{0,6},{1,7},{2,4},{3,5},{4,2},{5,3},{6,0},{7,1},{8,14},{9,15},{10,... | collective-permute-start | bytes 196616 | tf_op jit(solution)/shard_map/ppermute | solution.py:241
  13.1 0.0 copy-done.3
  13.1 0.0 copy-done.5
  13.1 0.0 copy-done.6
  13.1 0.0 copy-done.7
  13.1 0.0 copy-done.8
  13.2 1.2 %cached.1 = (f32[128,256]{1,0:T(8,128)S(1)}, f32[8,256]{1,0:T(8,128)S(1)}, f32[128,256]{1,0:T(8,128)S(1)}) custom-call(s32[1,256]{1,0:T(1,128)S(1)} %bitcast.6, s32[1,256]{1,0:T(1,128)S(1)} %bitcast.7, s32[1,256]{1,0:T(1,128)S(1)} %bitcast.8, s32[1,2]{1,0:T(1,128)S(1)} %bitcast.9, bf16[2,2048]{1,0:T(2,128)(2,1)S(1)} %copy-done.4, ...), custom_call_target="tpu_custom_call" | custom-call | flops 268435456 | bytes 1059848 | tf_op jit(solution)/shard_map/cached/pallas_call | solution.py:215
  14.3 0.0 collective-permute-done.3.a_ref
  14.3 1.1 %collective-permute-done.4.b_ref = bf16[128,256]{1,0:T(8,128)(2,1)S(1)} collective-permute-done((bf16[128,256]{1,0:T(8,128)(2,1)S(1)}, bf16[128,256]{1,0:T(8,128)(2,1)S(1)}, u32[]{:S(2)}, u32[]{:S(2)}) %collective-permute-start.4) | collective-permute-done | bytes 65568 | tf_op jit(solution)/shard_map/ppermute | solution.py:239
  15.5 0.4 collective-permute-done.5.c_ref
  15.9 0.5 %collective-permute-done.2 = bf16[16,2048]{1,0:T(8,128)(2,1)S(1)} collective-permute-done((bf16[16,2048]{1,0:T(8,128)(2,1)S(1)}, bf16[16,2048]{1,0:T(8,128)(2,1)S(1)}, u32[]{:S(2)}, u32[]{:S(2)}) %collective-permute-start.2) | collective-permute-done | bytes 65568 | tf_op jit(solution)/shard_map/ppermute | solution.py:241
  16.5 0.4 prompt.1
  16.8 0.1 collective-permute-start.6
  16.9 1.3 %collective-permute-done.6.refs_0_ = bf16[144,256]{1,0:T(8,128)(2,1)S(1)} collective-permute-done((bf16[144,256]{1,0:T(8,128)(2,1)S(1)}, bf16[144,256]{1,0:T(8,128)(2,1)S(1)}, u32[]{:S(2)}, u32[]{:S(2)}) %collective-permute-start.6) | collective-permute-done | bytes 73760 | tf_op jit(solution)/shard_map/ppermute | solution.py:241
  18.2 0.1 join_core.1
  18.2 0.5 collective-permute-start.9
  18.8 2.4 %collective-permute-start.8 = (bf16[144,256]{1,0:T(8,128)(2,1)S(1)}, bf16[144,256]{1,0:T(8,128)(2,1)S(1)}, u32[]{:S(2)}, u32[]{:S(2)}) collective-permute-start(bf16[144,256]{1,0:T(8,128)(2,1)S(1)} %get-tuple-element.36), channel_id=1, source_target_pairs={{0,2},{1,3},{2,0},{3,1},{4,6},{5,7},{6,4},{7,5},{8,10},{9,11},{10,... | collective-permute-start | bytes 221192 | tf_op jit(solution)/shard_map/ppermute | solution.py:241
  21.2 0.7 %collective-permute-start.7 = (bf16[144,256]{1,0:T(8,128)(2,1)S(1)}, bf16[144,256]{1,0:T(8,128)(2,1)S(1)}, u32[]{:S(2)}, u32[]{:S(2)}) collective-permute-start(bf16[144,256]{1,0:T(8,128)(2,1)S(1)} %get-tuple-element.36), channel_id=1, source_target_pairs={{0,64},{64,0},{128,192},{192,128},{1,65},{65,1},{129,193},{193,129... | collective-permute-start | bytes 221192 | tf_op jit(solution)/shard_map/ppermute | solution.py:239
  21.8 2.3 %collective-permute-done.9.refs_2_ = bf16[144,256]{1,0:T(8,128)(2,1)S(1)} collective-permute-done((bf16[144,256]{1,0:T(8,128)(2,1)S(1)}, bf16[144,256]{1,0:T(8,128)(2,1)S(1)}, u32[]{:S(2)}, u32[]{:S(2)}) %collective-permute-start.9) | collective-permute-done | bytes 73760 | tf_op jit(solution)/shard_map/ppermute | solution.py:250
  24.1 0.9 %collective-permute-done.8.refs_1_ = bf16[144,256]{1,0:T(8,128)(2,1)S(1)} collective-permute-done((bf16[144,256]{1,0:T(8,128)(2,1)S(1)}, bf16[144,256]{1,0:T(8,128)(2,1)S(1)}, u32[]{:S(2)}, u32[]{:S(2)}) %collective-permute-start.8) | collective-permute-done | bytes 73760 | tf_op jit(solution)/shard_map/ppermute | solution.py:241
  25.1 0.5 collective-permute-done.7.refs_0_
  25.5 0.1 join_near.1
  25.6 2.3 %collective-permute-start.11 = (bf16[144,256]{1,0:T(8,128)(2,1)S(1)}, bf16[144,256]{1,0:T(8,128)(2,1)S(1)}, u32[]{:S(2)}, u32[]{:S(2)}) collective-permute-start(bf16[144,256]{1,0:T(8,128)(2,1)S(1)} %get-tuple-element.39), channel_id=1, source_target_pairs={{0,6},{1,135},{2,4},{3,133},{4,2},{5,131},{6,0},{7,129},{64,70},{6... | collective-permute-start | bytes 221192 | tf_op jit(solution)/shard_map/ppermute | solution.py:250
  27.9 1.1 %collective-permute-start.10 = (bf16[144,256]{1,0:T(8,128)(2,1)S(1)}, bf16[144,256]{1,0:T(8,128)(2,1)S(1)}, u32[]{:S(2)}, u32[]{:S(2)}) collective-permute-start(bf16[144,256]{1,0:T(8,128)(2,1)S(1)} %get-tuple-element.39), channel_id=1, source_target_pairs={{0,6},{1,129},{2,4},{3,131},{4,2},{5,133},{6,0},{7,135},{64,70},{6... | collective-permute-start | bytes 221192 | tf_op jit(solution)/shard_map/ppermute | solution.py:250
  28.9 3.1 %collective-permute-done.11.second_ref = bf16[144,256]{1,0:T(8,128)(2,1)S(1)} collective-permute-done((bf16[144,256]{1,0:T(8,128)(2,1)S(1)}, bf16[144,256]{1,0:T(8,128)(2,1)S(1)}, u32[]{:S(2)}, u32[]{:S(2)}) %collective-permute-start.11) | collective-permute-done | bytes 73760 | tf_op jit(solution)/shard_map/ppermute | solution.py:250
  32.0 1.4 %collective-permute-done.10.first_ref = bf16[144,256]{1,0:T(8,128)(2,1)S(1)} collective-permute-done((bf16[144,256]{1,0:T(8,128)(2,1)S(1)}, bf16[144,256]{1,0:T(8,128)(2,1)S(1)}, u32[]{:S(2)}, u32[]{:S(2)}) %collective-permute-start.10) | collective-permute-done | bytes 73760 | tf_op jit(solution)/shard_map/ppermute | solution.py:250
  33.5 0.2 collective-permute-start.12
  33.7 1.2 %collective-permute-done.12.got_ref = bf16[144,256]{1,0:T(8,128)(2,1)S(1)} collective-permute-done((bf16[144,256]{1,0:T(8,128)(2,1)S(1)}, bf16[144,256]{1,0:T(8,128)(2,1)S(1)}, u32[]{:S(2)}, u32[]{:S(2)}) %collective-permute-start.12) | collective-permute-done | bytes 73760 | tf_op jit(solution)/shard_map/ppermute | solution.py:241
  34.8 0.0 copy-done.2
  34.8 0.5 project.1
  35.3 17.9 %all_to_all.5 = bf16[8,2,512]{2,1,0:T(2,128)(2,1)S(1)} all-to-all(bf16[8,2,512]{2,1,0:T(2,128)(2,1)S(1)} %reshape.19), channel_id=1, replica_groups=mesh['sec'=4,'head'=8,'req'=8] {'head'}, dimensions={0} | all-to-all | bytes 32768 | tf_op jit(solution)/shard_map/all_to_all | solution.py:323
  53.2 0.6 %reduce_sum.12 = bf16[2,512]{1,0:T(2,128)(2,1)} reduce(bf16[8,2,512]{2,1,0:T(2,128)(2,1)S(1)} %all_to_all.5, bf16[]{:T(256)} %constant.2.clone.1), dimensions={0}, to_apply=%region_0.0 | reduce | flops 7168 | bytes 18434 | tf_op jit(solution)/shard_map/reduce_sum | solution.py:324
  (6 shorter events, 0.2 us)
Async XLA Ops:
  0.0 4.1 %copy-start.1 = (bf16[4096,256]{1,0:T(8,128)(2,1)S(1)}, bf16[4096,256]{1,0:T(8,128)(2,1)}, u32[]{:S(2)}) copy-start(bf16[4096,256]{1,0:T(8,128)(2,1)} %w_ref.1) | copy-start | bytes 6291460
  0.0 4.1 %copy-start = (bf16[512,4096]{1,0:T(8,128)(2,1)S(1)}, bf16[512,4096]{1,0:T(8,128)(2,1)}, u32[]{:S(2)}) copy-start(bf16[512,4096]{1,0:T(8,128)(2,1)} %x_ref.1) | copy-start | bytes 12582916
  0.0 0.8 %copy-start.4 = (bf16[2,2048]{1,0:T(2,128)(2,1)S(1)}, bf16[2,2048]{1,0:T(2,128)(2,1)}, u32[]{:S(2)}) copy-start(bf16[2,2048]{1,0:T(2,128)(2,1)} %q_ref.1) | copy-start | bytes 24580
  1.0 1.3 %collective-permute-start = (bf16[16,2048]{1,0:T(8,128)(2,1)S(1)}, bf16[16,2048]{1,0:T(8,128)(2,1)S(1)}, u32[]{:S(2)}, u32[]{:S(2)}) collective-permute-start(bf16[16,2048]{1,0:T(8,128)(2,1)S(1)} %place.1), channel_id=1, source_target_pairs={{0,1},{1,0},{2,3},{3,2},{4,5},{5,4},{6,7},{7,6},{8,9},{9,8},{10,11... | collective-permute-start | bytes 196616 | tf_op jit(solution)/shard_map/ppermute | solution.py:241
  2.4 10.8 %copy-start.3 = (bf16[2,1024,1,256]{3,1,2,0:T(8,128)(2,1)S(1)}, bf16[2,1024,1,256]{3,1,2,0:T(8,128)(2,1)}, u32[]{:S(2)}) copy-start(bf16[2,1024,1,256]{3,1,2,0:T(8,128)(2,1)} %param.12) | copy-start | bytes 3145732
  2.4 10.8 %copy-start.5 = (s32[256,1]{0,1:T(1,128)S(1)}, s32[256,1]{0,1:T(1,128)}, u32[]{:S(2)}) copy-start(s32[256,1]{0,1:T(1,128)} %param.14) | copy-start | bytes 3076
  2.4 10.8 %copy-start.6 = (s32[256]{0:T(256)S(1)}, s32[256]{0:T(256)}, u32[]{:S(2)}) copy-start(s32[256]{0:T(256)} %param.15) | copy-start | bytes 3076
  2.4 10.8 %copy-start.7 = (s32[256]{0:T(256)S(1)}, s32[256]{0:T(256)}, u32[]{:S(2)}) copy-start(s32[256]{0:T(256)} %param.16) | copy-start | bytes 3076
  2.4 10.7 %copy-start.8 = (s32[2]{0:T(128)S(1)}, s32[2]{0:T(128)}, u32[]{:S(2)}) copy-start(s32[2]{0:T(128)} %param.17) | copy-start | bytes 28
  2.4 8.4 %collective-permute-start.1 = (bf16[16,2048]{1,0:T(8,128)(2,1)S(1)}, bf16[16,2048]{1,0:T(8,128)(2,1)S(1)}, u32[]{:S(2)}, u32[]{:S(2)}) collective-permute-start(bf16[16,2048]{1,0:T(8,128)(2,1)S(1)} %add.9), channel_id=1, source_target_pairs={{0,2},{1,3},{2,0},{3,1},{4,6},{5,7},{6,4},{7,5},{8,10},{9,11},{10,... | collective-permute-start | bytes 196616 | tf_op jit(solution)/shard_map/ppermute | solution.py:241
  5.5 29.4 %copy-start.2 = (bf16[2048,512]{1,0:T(8,128)(2,1)S(1)}, bf16[2048,512]{1,0:T(8,128)(2,1)}, u32[]{:S(2)}) copy-start(bf16[2048,512]{1,0:T(8,128)(2,1)} %out_w_ref.1) | copy-start | bytes 6291460
  5.5 8.9 %collective-permute-start.3 = (bf16[128,256]{1,0:T(8,128)(2,1)S(1)}, bf16[128,256]{1,0:T(8,128)(2,1)S(1)}, u32[]{:S(2)}, u32[]{:S(2)}) collective-permute-start(bf16[128,256]{1,0:T(8,128)(2,1)S(1)} %get-tuple-element.26), channel_id=1, source_target_pairs={{0,192},{64,128},{128,64},{192,0},{1,193},{65,129},{129,65},{193,1... | collective-permute-start | bytes 196616 | tf_op jit(solution)/shard_map/ppermute | solution.py:239
  10.2 5.3 %collective-permute-start.4 = (bf16[128,256]{1,0:T(8,128)(2,1)S(1)}, bf16[128,256]{1,0:T(8,128)(2,1)S(1)}, u32[]{:S(2)}, u32[]{:S(2)}) collective-permute-start(bf16[128,256]{1,0:T(8,128)(2,1)S(1)} %get-tuple-element.27), channel_id=1, source_target_pairs={{0,128},{64,192},{128,0},{192,64},{1,129},{65,193},{129,1},{193,65... | collective-permute-start | bytes 196616 | tf_op jit(solution)/shard_map/ppermute | solution.py:239
  10.2 5.7 %collective-permute-start.5 = (bf16[128,256]{1,0:T(8,128)(2,1)S(1)}, bf16[128,256]{1,0:T(8,128)(2,1)S(1)}, u32[]{:S(2)}, u32[]{:S(2)}) collective-permute-start(bf16[128,256]{1,0:T(8,128)(2,1)S(1)} %get-tuple-element.28), channel_id=1, source_target_pairs={{0,64},{64,0},{128,192},{192,128},{1,65},{65,1},{129,193},{193,129... | collective-permute-start | bytes 196616 | tf_op jit(solution)/shard_map/ppermute | solution.py:239
  10.9 5.6 %collective-permute-start.2 = (bf16[16,2048]{1,0:T(8,128)(2,1)S(1)}, bf16[16,2048]{1,0:T(8,128)(2,1)S(1)}, u32[]{:S(2)}, u32[]{:S(2)}) collective-permute-start(bf16[16,2048]{1,0:T(8,128)(2,1)S(1)} %add.10), channel_id=1, source_target_pairs={{0,6},{1,7},{2,4},{3,5},{4,2},{5,3},{6,0},{7,1},{8,14},{9,15},{10,... | collective-permute-start | bytes 196616 | tf_op jit(solution)/shard_map/ppermute | solution.py:241
  16.8 1.4 %collective-permute-start.6 = (bf16[144,256]{1,0:T(8,128)(2,1)S(1)}, bf16[144,256]{1,0:T(8,128)(2,1)S(1)}, u32[]{:S(2)}, u32[]{:S(2)}) collective-permute-start(bf16[144,256]{1,0:T(8,128)(2,1)S(1)} %get-tuple-element.33), channel_id=1, source_target_pairs={{0,1},{1,0},{2,3},{3,2},{4,5},{5,4},{6,7},{7,6},{8,9},{9,8},{10,11... | collective-permute-start | bytes 221192 | tf_op jit(solution)/shard_map/ppermute | solution.py:241
  18.2 5.9 %collective-permute-start.9 = (bf16[144,256]{1,0:T(8,128)(2,1)S(1)}, bf16[144,256]{1,0:T(8,128)(2,1)S(1)}, u32[]{:S(2)}, u32[]{:S(2)}) collective-permute-start(bf16[144,256]{1,0:T(8,128)(2,1)S(1)} %get-tuple-element.36), channel_id=1, source_target_pairs={{0,66},{1,67},{2,64},{3,65},{4,70},{5,71},{6,68},{7,69},{64,2},{65... | collective-permute-start | bytes 221192 | tf_op jit(solution)/shard_map/ppermute | solution.py:250
  18.8 6.3 %collective-permute-start.8 = (bf16[144,256]{1,0:T(8,128)(2,1)S(1)}, bf16[144,256]{1,0:T(8,128)(2,1)S(1)}, u32[]{:S(2)}, u32[]{:S(2)}) collective-permute-start(bf16[144,256]{1,0:T(8,128)(2,1)S(1)} %get-tuple-element.36), channel_id=1, source_target_pairs={{0,2},{1,3},{2,0},{3,1},{4,6},{5,7},{6,4},{7,5},{8,10},{9,11},{10,... | collective-permute-start | bytes 221192 | tf_op jit(solution)/shard_map/ppermute | solution.py:241
  21.2 4.4 %collective-permute-start.7 = (bf16[144,256]{1,0:T(8,128)(2,1)S(1)}, bf16[144,256]{1,0:T(8,128)(2,1)S(1)}, u32[]{:S(2)}, u32[]{:S(2)}) collective-permute-start(bf16[144,256]{1,0:T(8,128)(2,1)S(1)} %get-tuple-element.36), channel_id=1, source_target_pairs={{0,64},{64,0},{128,192},{192,128},{1,65},{65,1},{129,193},{193,129... | collective-permute-start | bytes 221192 | tf_op jit(solution)/shard_map/ppermute | solution.py:239
  25.6 6.4 %collective-permute-start.11 = (bf16[144,256]{1,0:T(8,128)(2,1)S(1)}, bf16[144,256]{1,0:T(8,128)(2,1)S(1)}, u32[]{:S(2)}, u32[]{:S(2)}) collective-permute-start(bf16[144,256]{1,0:T(8,128)(2,1)S(1)} %get-tuple-element.39), channel_id=1, source_target_pairs={{0,6},{1,135},{2,4},{3,133},{4,2},{5,131},{6,0},{7,129},{64,70},{6... | collective-permute-start | bytes 221192 | tf_op jit(solution)/shard_map/ppermute | solution.py:250
  27.9 5.6 %collective-permute-start.10 = (bf16[144,256]{1,0:T(8,128)(2,1)S(1)}, bf16[144,256]{1,0:T(8,128)(2,1)S(1)}, u32[]{:S(2)}, u32[]{:S(2)}) collective-permute-start(bf16[144,256]{1,0:T(8,128)(2,1)S(1)} %get-tuple-element.39), channel_id=1, source_target_pairs={{0,6},{1,129},{2,4},{3,131},{4,2},{5,133},{6,0},{7,135},{64,70},{6... | collective-permute-start | bytes 221192 | tf_op jit(solution)/shard_map/ppermute | solution.py:250
  33.5 1.4 %collective-permute-start.12 = (bf16[144,256]{1,0:T(8,128)(2,1)S(1)}, bf16[144,256]{1,0:T(8,128)(2,1)S(1)}, u32[]{:S(2)}, u32[]{:S(2)}) collective-permute-start(bf16[144,256]{1,0:T(8,128)(2,1)S(1)} %get-tuple-element.42), channel_id=1, source_target_pairs={{0,1},{1,0},{2,3},{3,2},{4,5},{5,4},{6,7},{7,6},{8,9},{9,8},{10,11... | collective-permute-start | bytes 221192 | tf_op jit(solution)/shard_map/ppermute | solution.py:241

commit v8 on v7

--- a/solution.py
+++ b/solution.py
@@ -125,11 +125,19 @@
     live_ref[...] = live.astype(F32)
 
 
-def place_kernel(mine_ref, out_ref):
+def placed(rows, holder):
     place = lax.broadcasted_iota(jnp.int32, (NREQ, 2), 0)
     row = lax.broadcasted_iota(jnp.int32, (NREQ, 2), 1)
-    mine = (place == lax.axis_index("req") * 2 + row).astype(BF)
-    out_ref[...] = dot(mine, mine_ref[...], ((1,), (0,))).astype(BF)
+    return dot((place == holder * 2 + row).astype(BF), rows, ((1,), (0,)))
+
+
+def place_mine_kernel(mine_ref, out_ref):
+    out_ref[...] = placed(mine_ref[...], lax.axis_index("req")).astype(BF)
+
+
+def place_other_kernel(so_far_ref, other_ref, out_ref):
+    other = placed(other_ref[...], lax.axis_index("req") ^ 1)
+    out_ref[...] = (so_far_ref[...].astype(F32) + other).astype(BF)
 
 
 def prompt_kernel(q_ref, live_ref, kv_ref, cw_ref, cs_ref, kw_ref, ks_ref, send_ref):
@@ -250,14 +258,14 @@
         return lax.ppermute(value, ("sec", "req"), pairs)
 
     chunk = shape((rows, width), BF)
+    everyone = shape((NREQ, queries.shape[1]), BF)
+    other_queries = over(queries, 0, 1)
     gathered = call(
-        place_kernel,
-        [(vmem(), queries)],
-        shape((NREQ, queries.shape[1]), BF),
-        "place",
-        flops=2_000_000_000,
-    )
-    gathered = gathered + over(gathered, 0, 1)
+        place_mine_kernel, [(vmem(), queries)], everyone, "place_mine", flops=2_000_000_000
+    )
+    gathered = call(
+        place_other_kernel, [(vmem(), gathered), (vmem(), other_queries)], everyone, "place_other"
+    )
     gathered = gathered + over(gathered, 0, 2)
     chunks = call(
         kv_kernel,
@@ -297,14 +305,14 @@
     )
     for name, moves in (
         ("join_core", ((0, 1),)),
-        ("join_near", ((1, 0), (0, 2), (1, 2))),
+        ("join_near", ((0, 2), (0, 6), (0, 4))),
     ):
         got = [over(kept[2], *flips) for flips in moves]
         kept = call(
             join_kernel, [(vmem(), value) for value in (kept[0], kept[1], *got)], STATE, name
         )
     got = [
-        over_cores(kept[2], (0, 6), flips) for flips in ((2, 0), (2, 6))
+        over_cores(kept[2], (1, 0), flips) for flips in ((3, 0), (2, 0))
     ]
     far = call(far_kernel, [(vmem(), value) for value in got], STATE, "join_far")
     columns = w_out.shape[1]

time: 54.8 us -> 54 us (0.985)
  waiting for transfers between devices: 13.9 us -> 12.4 us
  blocking collectives: 17.9 us -> 19.2 us
    ppermute x3 -> x2, waiting for transfers between devices: 6.82 us -> 3.71 us  [over_cores(): return lax.ppermute(value, ('sec', 'req'), pairs)]
    ppermute x6 -> x8, waiting for transfers between devices: 5.1 us -> 7.54 us  [over(): lax.ppermute(value, 'req', [(i, i ^ req_flip) for i in range(req_count)])]
    ppermute x6 -> x8, starting transfers between devices: 6.73 us -> 8.57 us  [over(): lax.ppermute(value, 'req', [(i, i ^ req_flip) for i in range(req_count)])]
    ppermute x3 -> x2, starting transfers between devices: 3.83 us -> 2.11 us  [over_cores(): return lax.ppermute(value, ('sec', 'req'), pairs)]
    all_to_all x1, blocking collectives: 17.9 us -> 19.2 us  [on_device(): pieces = lax.all_to_all(pieces, 'head', 0, 0, tiled=True)]
    ppermute x4 -> x3, waiting for transfers between devices: 1.97 us -> 1.11 us  [over(): lax.ppermute(value, 'sec', [(i, i ^ sec_flip) for i in range(sec_count)])]
    ppermute x4 -> x3, starting transfers between devices: 6.03 us -> 5.37 us  [over(): lax.ppermute(value, 'sec', [(i, i ^ sec_flip) for i in range(sec_count)])]
    pallas_call x9 -> x10, Pallas kernels: 3.72 us -> 3.86 us  [call(): pl.pallas_call(kernel, out_shape=outs, in_specs=[spec for spec, _ in ins]...]
  transfers between devices with their start and end apart: 13 -> 13, of which waited for: 11 -> 10; matrix products, arithmetic and copies ran while one was open for 0% -> 0% of each run, Pallas kernels for 5% -> 5%
where the time goes in v8:
time: 54 us; the launch traced here: 53.1 us
  blocking collectives  19.2 us (36%)
  starting transfers between devices  16.1 us (30%)
  waiting for transfers between devices  12.4 us (23%)
  Pallas kernels  3.86 us (7%)
  local copies, waits for them, and re-layouts  0.91 us (2%)
  other arithmetic  0.64 us (1%)
    all_to_all x1, blocking collectives, on_device(): pieces = lax.all_to_all(pieces, 'head', 0, 0, tiled=True)  19.2 us
    ppermute x8, starting transfers between devices, over(): lax.ppermute(value, 'req', [(i, i ^ req_flip) for i in range(req_count)])  8.57 us
    ppermute x8, waiting for transfers between devices, over(): lax.ppermute(value, 'req', [(i, i ^ req_flip) for i in range(req_count)])  7.54 us
    ppermute x3, starting transfers between devices, over(): lax.ppermute(value, 'sec', [(i, i ^ sec_flip) for i in range(sec_count)])  5.37 us
    pallas_call x10, Pallas kernels, call(): pl.pallas_call(kernel, out_shape=outs, in_specs=[spec for spec, _ in ins]...  3.86 us
    ppermute x2, waiting for transfers between devices, over_cores(): return lax.ppermute(value, ('sec', 'req'), pairs)  3.71 us
    ppermute x2, starting transfers between devices, over_cores(): return lax.ppermute(value, ('sec', 'req'), pairs)  2.11 us
    ppermute x3, waiting for transfers between devices, over(): lax.ppermute(value, 'sec', [(i, i ^ sec_flip) for i in range(sec_count)])  1.11 us
  transfers between devices with their start and end apart: 13, of which 10 were waited for; matrix products, arithmetic and copies ran while one was open for 0% of the time, Pallas kernels for 5%

profile of v8, /device:TPU:2, one launch (start us, length us, event | category | flops | bytes accessed | tf_op | source)
XLA Modules:
  0.0 53.1 jit_solution(16303532764947833436)
XLA Ops:
  0.0 0.0 copy-start.1
  0.0 0.0 copy-start
  0.0 0.0 collective-permute-start
  0.0 0.0 copy-start.4
  0.0 0.8 %copy-done.4 = bf16[2,2048]{1,0:T(2,128)(2,1)S(1)} copy-done((bf16[2,2048]{1,0:T(2,128)(2,1)S(1)}, bf16[2,2048]{1,0:T(2,128)(2,1)}, u32[]{:S(2)}) %copy-start.4) | copy-done | bytes 8216
  0.9 0.1 place_mine.1.so_far_ref
  1.0 0.4 collective-permute-done.other_ref
  1.4 0.1 place_other.1
  1.5 0.0 copy-start.3
  1.5 0.0 copy-start.5
  1.6 0.0 copy-start.6
  1.6 0.0 copy-start.7
  1.6 0.0 copy-start.8
  1.6 1.7 %collective-permute-start.1 = (bf16[16,2048]{1,0:T(8,128)(2,1)S(1)}, bf16[16,2048]{1,0:T(8,128)(2,1)S(1)}, u32[]{:S(2)}, u32[]{:S(2)}) collective-permute-start(bf16[16,2048]{1,0:T(8,128)(2,1)S(1)} %place_other.1), channel_id=1, source_target_pairs={{0,2},{1,3},{2,0},{3,1},{4,6},{5,7},{6,4},{7,5},{8,10},{9,11},{10,... | collective-permute-start | bytes 196616 | tf_op jit(solution)/shard_map/ppermute | solution.py:249
  3.3 0.0 copy-done.1
  3.3 0.0 copy-done
  3.3 1.4 %new_kv.1 = (bf16[128,256]{1,0:T(8,128)(2,1)S(1)}, bf16[128,256]{1,0:T(8,128)(2,1)S(1)}, bf16[128,256]{1,0:T(8,128)(2,1)S(1)}, bf16[128,256]{1,0:T(8,128)(2,1)S(1)}) custom-call(bf16[512,4096]{1,0:T(8,128)(2,1)S(1)} %copy-done, bf16[4096,256]{1,0:T(8,128)(2,1)S(1)} %copy-done.1), custom_call_target="tpu_custom_call" | custom-call | flops 1073741824 | bytes 6291456 | tf_op jit(solution)/shard_map/new_kv/pallas_call | solution.py:223
  4.6 0.0 copy-start.2
  4.6 4.7 %collective-permute-start.3 = (bf16[128,256]{1,0:T(8,128)(2,1)S(1)}, bf16[128,256]{1,0:T(8,128)(2,1)S(1)}, u32[]{:S(2)}, u32[]{:S(2)}) collective-permute-start(bf16[128,256]{1,0:T(8,128)(2,1)S(1)} %get-tuple-element.26), channel_id=1, source_target_pairs={{0,192},{64,128},{128,64},{192,0},{1,193},{65,129},{129,65},{193,1... | collective-permute-start | bytes 196616 | tf_op jit(solution)/shard_map/ppermute | solution.py:247
  9.3 0.0 collective-permute-start.4
  9.4 0.7 %collective-permute-start.5 = (bf16[128,256]{1,0:T(8,128)(2,1)S(1)}, bf16[128,256]{1,0:T(8,128)(2,1)S(1)}, u32[]{:S(2)}, u32[]{:S(2)}) collective-permute-start(bf16[128,256]{1,0:T(8,128)(2,1)S(1)} %get-tuple-element.28), channel_id=1, source_target_pairs={{0,64},{64,0},{128,192},{192,128},{1,65},{65,1},{129,193},{193,129... | collective-permute-start | bytes 196616 | tf_op jit(solution)/shard_map/ppermute | solution.py:247
  10.0 0.0 collective-permute-done.1
  10.0 2.7 %collective-permute-start.2 = (bf16[16,2048]{1,0:T(8,128)(2,1)S(1)}, bf16[16,2048]{1,0:T(8,128)(2,1)S(1)}, u32[]{:S(2)}, u32[]{:S(2)}) collective-permute-start(bf16[16,2048]{1,0:T(8,128)(2,1)S(1)} %add.6), channel_id=1, source_target_pairs={{0,6},{1,7},{2,4},{3,5},{4,2},{5,3},{6,0},{7,1},{8,14},{9,15},{10,... | collective-permute-start | bytes 196616 | tf_op jit(solution)/shard_map/ppermute | solution.py:249
  12.7 0.0 copy-done.3
  12.7 0.0 copy-done.5
  12.7 0.0 copy-done.6
  12.7 0.0 copy-done.7
  12.7 0.0 copy-done.8
  12.7 1.2 %cached.1 = (f32[128,256]{1,0:T(8,128)S(1)}, f32[8,256]{1,0:T(8,128)S(1)}, f32[128,256]{1,0:T(8,128)S(1)}) custom-call(s32[1,256]{1,0:T(1,128)S(1)} %bitcast.6, s32[1,256]{1,0:T(1,128)S(1)} %bitcast.7, s32[1,256]{1,0:T(1,128)S(1)} %bitcast.8, s32[1,2]{1,0:T(1,128)S(1)} %bitcast.9, bf16[2,2048]{1,0:T(2,128)(2,1)S(1)} %copy-done.4, ...), custom_call_target="tpu_custom_call" | custom-call | flops 268435456 | bytes 1059848 | tf_op jit(solution)/shard_map/cached/pallas_call | solution.py:223
  13.9 0.0 collective-permute-done.3.a_ref
  13.9 0.8 %collective-permute-done.4.b_ref = bf16[128,256]{1,0:T(8,128)(2,1)S(1)} collective-permute-done((bf16[128,256]{1,0:T(8,128)(2,1)S(1)}, bf16[128,256]{1,0:T(8,128)(2,1)S(1)}, u32[]{:S(2)}, u32[]{:S(2)}) %collective-permute-start.4) | collective-permute-done | bytes 65568 | tf_op jit(solution)/shard_map/ppermute | solution.py:247
  14.7 0.4 collective-permute-done.5.c_ref
  15.1 0.5 %collective-permute-done.2 = bf16[16,2048]{1,0:T(8,128)(2,1)S(1)} collective-permute-done((bf16[16,2048]{1,0:T(8,128)(2,1)S(1)}, bf16[16,2048]{1,0:T(8,128)(2,1)S(1)}, u32[]{:S(2)}, u32[]{:S(2)}) %collective-permute-start.2) | collective-permute-done | bytes 65568 | tf_op jit(solution)/shard_map/ppermute | solution.py:249
  15.6 0.4 prompt.1
  16.0 0.1 collective-permute-start.6
  16.1 1.3 %collective-permute-done.6.refs_0_ = bf16[144,256]{1,0:T(8,128)(2,1)S(1)} collective-permute-done((bf16[144,256]{1,0:T(8,128)(2,1)S(1)}, bf16[144,256]{1,0:T(8,128)(2,1)S(1)}, u32[]{:S(2)}, u32[]{:S(2)}) %collective-permute-start.6) | collective-permute-done | bytes 73760 | tf_op jit(solution)/shard_map/ppermute | solution.py:249
  17.4 0.1 join_core.1
  17.4 2.5 %collective-permute-start.9 = (bf16[144,256]{1,0:T(8,128)(2,1)S(1)}, bf16[144,256]{1,0:T(8,128)(2,1)S(1)}, u32[]{:S(2)}, u32[]{:S(2)}) collective-permute-start(bf16[144,256]{1,0:T(8,128)(2,1)S(1)} %get-tuple-element.36), channel_id=1, source_target_pairs={{0,4},{1,5},{2,6},{3,7},{4,0},{5,1},{6,2},{7,3},{8,12},{9,13},{10,... | collective-permute-start | bytes 221192 | tf_op jit(solution)/shard_map/ppermute | solution.py:249
  19.9 0.9 %collective-permute-start.8 = (bf16[144,256]{1,0:T(8,128)(2,1)S(1)}, bf16[144,256]{1,0:T(8,128)(2,1)S(1)}, u32[]{:S(2)}, u32[]{:S(2)}) collective-permute-start(bf16[144,256]{1,0:T(8,128)(2,1)S(1)} %get-tuple-element.36), channel_id=1, source_target_pairs={{0,6},{1,7},{2,4},{3,5},{4,2},{5,3},{6,0},{7,1},{8,14},{9,15},{10,... | collective-permute-start | bytes 221192 | tf_op jit(solution)/shard_map/ppermute | solution.py:249
  20.8 0.2 collective-permute-start.7
  21.0 2.4 %collective-permute-done.9.refs_2_ = bf16[144,256]{1,0:T(8,128)(2,1)S(1)} collective-permute-done((bf16[144,256]{1,0:T(8,128)(2,1)S(1)}, bf16[144,256]{1,0:T(8,128)(2,1)S(1)}, u32[]{:S(2)}, u32[]{:S(2)}) %collective-permute-start.9) | collective-permute-done | bytes 73760 | tf_op jit(solution)/shard_map/ppermute | solution.py:249
  23.4 2.1 %collective-permute-done.8.refs_1_ = bf16[144,256]{1,0:T(8,128)(2,1)S(1)} collective-permute-done((bf16[144,256]{1,0:T(8,128)(2,1)S(1)}, bf16[144,256]{1,0:T(8,128)(2,1)S(1)}, u32[]{:S(2)}, u32[]{:S(2)}) %collective-permute-start.8) | collective-permute-done | bytes 73760 | tf_op jit(solution)/shard_map/ppermute | solution.py:249
  25.4 0.0 collective-permute-done.7.refs_0_
  25.4 0.1 join_near.1
  25.5 1.3 %collective-permute-start.11 = (bf16[144,256]{1,0:T(8,128)(2,1)S(1)}, bf16[144,256]{1,0:T(8,128)(2,1)S(1)}, u32[]{:S(2)}, u32[]{:S(2)}) collective-permute-start(bf16[144,256]{1,0:T(8,128)(2,1)S(1)} %get-tuple-element.39), channel_id=1, source_target_pairs={{0,64},{1,129},{2,66},{3,131},{4,68},{5,133},{6,70},{7,135},{64,0}... | collective-permute-start | bytes 221192 | tf_op jit(solution)/shard_map/ppermute | solution.py:258
  26.8 0.8 %collective-permute-start.10 = (bf16[144,256]{1,0:T(8,128)(2,1)S(1)}, bf16[144,256]{1,0:T(8,128)(2,1)S(1)}, u32[]{:S(2)}, u32[]{:S(2)}) collective-permute-start(bf16[144,256]{1,0:T(8,128)(2,1)S(1)} %get-tuple-element.39), channel_id=1, source_target_pairs={{0,64},{1,193},{2,66},{3,195},{4,68},{5,197},{6,70},{7,199},{64,0}... | collective-permute-start | bytes 221192 | tf_op jit(solution)/shard_map/ppermute | solution.py:258
  27.7 2.3 %collective-permute-done.11.second_ref = bf16[144,256]{1,0:T(8,128)(2,1)S(1)} collective-permute-done((bf16[144,256]{1,0:T(8,128)(2,1)S(1)}, bf16[144,256]{1,0:T(8,128)(2,1)S(1)}, u32[]{:S(2)}, u32[]{:S(2)}) %collective-permute-start.11) | collective-permute-done | bytes 73760 | tf_op jit(solution)/shard_map/ppermute | solution.py:258
  30.0 1.4 %collective-permute-done.10.first_ref = bf16[144,256]{1,0:T(8,128)(2,1)S(1)} collective-permute-done((bf16[144,256]{1,0:T(8,128)(2,1)S(1)}, bf16[144,256]{1,0:T(8,128)(2,1)S(1)}, u32[]{:S(2)}, u32[]{:S(2)}) %collective-permute-start.10) | collective-permute-done | bytes 73760 | tf_op jit(solution)/shard_map/ppermute | solution.py:258
  31.4 0.6 %collective-permute-start.12 = (bf16[144,256]{1,0:T(8,128)(2,1)S(1)}, bf16[144,256]{1,0:T(8,128)(2,1)S(1)}, u32[]{:S(2)}, u32[]{:S(2)}) collective-permute-start(bf16[144,256]{1,0:T(8,128)(2,1)S(1)} %get-tuple-element.42), channel_id=1, source_target_pairs={{0,1},{1,0},{2,3},{3,2},{4,5},{5,4},{6,7},{7,6},{8,9},{9,8},{10,11... | collective-permute-start | bytes 221192 | tf_op jit(solution)/shard_map/ppermute | solution.py:249
  32.0 0.9 %collective-permute-done.12.got_ref = bf16[144,256]{1,0:T(8,128)(2,1)S(1)} collective-permute-done((bf16[144,256]{1,0:T(8,128)(2,1)S(1)}, bf16[144,256]{1,0:T(8,128)(2,1)S(1)}, u32[]{:S(2)}, u32[]{:S(2)}) %collective-permute-start.12) | collective-permute-done | bytes 73760 | tf_op jit(solution)/shard_map/ppermute | solution.py:249
  32.9 0.0 copy-done.2
  32.9 0.5 project.1
  33.4 19.2 %all_to_all.5 = bf16[8,2,512]{2,1,0:T(2,128)(2,1)S(1)} all-to-all(bf16[8,2,512]{2,1,0:T(2,128)(2,1)S(1)} %reshape.19), channel_id=1, replica_groups=mesh['sec'=4,'head'=8,'req'=8] {'head'}, dimensions={0} | all-to-all | bytes 32768 | tf_op jit(solution)/shard_map/all_to_all | solution.py:331
  52.5 0.6 %reduce_sum.12 = bf16[2,512]{1,0:T(2,128)(2,1)} reduce(bf16[8,2,512]{2,1,0:T(2,128)(2,1)S(1)} %all_to_all.5, bf16[]{:T(256)} %constant.2.clone.1), dimensions={0}, to_apply=%region_0.0 | reduce | flops 7168 | bytes 18434 | tf_op jit(solution)/shard_map/reduce_sum | solution.py:332
  (5 shorter events, 0.1 us)
Async XLA Ops:
  0.0 3.3 %copy-start.1 = (bf16[4096,256]{1,0:T(8,128)(2,1)S(1)}, bf16[4096,256]{1,0:T(8,128)(2,1)}, u32[]{:S(2)}) copy-start(bf16[4096,256]{1,0:T(8,128)(2,1)} %w_ref.1) | copy-start | bytes 6291460
  0.0 3.3 %copy-start = (bf16[512,4096]{1,0:T(8,128)(2,1)S(1)}, bf16[512,4096]{1,0:T(8,128)(2,1)}, u32[]{:S(2)}) copy-start(bf16[512,4096]{1,0:T(8,128)(2,1)} %x_ref.1) | copy-start | bytes 12582916
  0.0 1.4 %collective-permute-start = (bf16[2,2048]{1,0:T(2,128)(2,1)}, bf16[2,2048]{1,0:T(2,128)(2,1)S(1)}, u32[]{:S(2)}, u32[]{:S(2)}) collective-permute-start(bf16[2,2048]{1,0:T(2,128)(2,1)} %q_ref.1), channel_id=1, source_target_pairs={{0,1},{1,0},{2,3},{3,2},{4,5},{5,4},{6,7},{7,6},{8,9},{9,8},{10,11... | collective-permute-start | bytes 24584 | tf_op jit(solution)/shard_map/ppermute | solution.py:249
  0.0 0.8 %copy-start.4 = (bf16[2,2048]{1,0:T(2,128)(2,1)S(1)}, bf16[2,2048]{1,0:T(2,128)(2,1)}, u32[]{:S(2)}) copy-start(bf16[2,2048]{1,0:T(2,128)(2,1)} %q_ref.1) | copy-start | bytes 24580
  1.5 11.2 %copy-start.3 = (bf16[2,1024,1,256]{3,1,2,0:T(8,128)(2,1)S(1)}, bf16[2,1024,1,256]{3,1,2,0:T(8,128)(2,1)}, u32[]{:S(2)}) copy-start(bf16[2,1024,1,256]{3,1,2,0:T(8,128)(2,1)} %param.12) | copy-start | bytes 3145732
  1.5 11.2 %copy-start.5 = (s32[256,1]{0,1:T(1,128)S(1)}, s32[256,1]{0,1:T(1,128)}, u32[]{:S(2)}) copy-start(s32[256,1]{0,1:T(1,128)} %param.14) | copy-start | bytes 3076
  1.6 11.2 %copy-start.6 = (s32[256]{0:T(256)S(1)}, s32[256]{0:T(256)}, u32[]{:S(2)}) copy-start(s32[256]{0:T(256)} %param.15) | copy-start | bytes 3076
  1.6 11.1 %copy-start.7 = (s32[256]{0:T(256)S(1)}, s32[256]{0:T(256)}, u32[]{:S(2)}) copy-start(s32[256]{0:T(256)} %param.16) | copy-start | bytes 3076
  1.6 11.1 %copy-start.8 = (s32[2]{0:T(128)S(1)}, s32[2]{0:T(128)}, u32[]{:S(2)}) copy-start(s32[2]{0:T(128)} %param.17) | copy-start | bytes 28
  1.6 8.4 %collective-permute-start.1 = (bf16[16,2048]{1,0:T(8,128)(2,1)S(1)}, bf16[16,2048]{1,0:T(8,128)(2,1)S(1)}, u32[]{:S(2)}, u32[]{:S(2)}) collective-permute-start(bf16[16,2048]{1,0:T(8,128)(2,1)S(1)} %place_other.1), channel_id=1, source_target_pairs={{0,2},{1,3},{2,0},{3,1},{4,6},{5,7},{6,4},{7,5},{8,10},{9,11},{10,... | collective-permute-start | bytes 196616 | tf_op jit(solution)/shard_map/ppermute | solution.py:249
  4.6 28.3 %copy-start.2 = (bf16[2048,512]{1,0:T(8,128)(2,1)S(1)}, bf16[2048,512]{1,0:T(8,128)(2,1)}, u32[]{:S(2)}) copy-start(bf16[2048,512]{1,0:T(8,128)(2,1)} %out_w_ref.1) | copy-start | bytes 6291460
  4.6 9.3 %collective-permute-start.3 = (bf16[128,256]{1,0:T(8,128)(2,1)S(1)}, bf16[128,256]{1,0:T(8,128)(2,1)S(1)}, u32[]{:S(2)}, u32[]{:S(2)}) collective-permute-start(bf16[128,256]{1,0:T(8,128)(2,1)S(1)} %get-tuple-element.26), channel_id=1, source_target_pairs={{0,192},{64,128},{128,64},{192,0},{1,193},{65,129},{129,65},{193,1... | collective-permute-start | bytes 196616 | tf_op jit(solution)/shard_map/ppermute | solution.py:247
  9.3 5.3 %collective-permute-start.4 = (bf16[128,256]{1,0:T(8,128)(2,1)S(1)}, bf16[128,256]{1,0:T(8,128)(2,1)S(1)}, u32[]{:S(2)}, u32[]{:S(2)}) collective-permute-start(bf16[128,256]{1,0:T(8,128)(2,1)S(1)} %get-tuple-element.27), channel_id=1, source_target_pairs={{0,128},{64,192},{128,0},{192,64},{1,129},{65,193},{129,1},{193,65... | collective-permute-start | bytes 196616 | tf_op jit(solution)/shard_map/ppermute | solution.py:247
  9.4 5.7 %collective-permute-start.5 = (bf16[128,256]{1,0:T(8,128)(2,1)S(1)}, bf16[128,256]{1,0:T(8,128)(2,1)S(1)}, u32[]{:S(2)}, u32[]{:S(2)}) collective-permute-start(bf16[128,256]{1,0:T(8,128)(2,1)S(1)} %get-tuple-element.28), channel_id=1, source_target_pairs={{0,64},{64,0},{128,192},{192,128},{1,65},{65,1},{129,193},{193,129... | collective-permute-start | bytes 196616 | tf_op jit(solution)/shard_map/ppermute | solution.py:247
  10.0 5.6 %collective-permute-start.2 = (bf16[16,2048]{1,0:T(8,128)(2,1)S(1)}, bf16[16,2048]{1,0:T(8,128)(2,1)S(1)}, u32[]{:S(2)}, u32[]{:S(2)}) collective-permute-start(bf16[16,2048]{1,0:T(8,128)(2,1)S(1)} %add.6), channel_id=1, source_target_pairs={{0,6},{1,7},{2,4},{3,5},{4,2},{5,3},{6,0},{7,1},{8,14},{9,15},{10,... | collective-permute-start | bytes 196616 | tf_op jit(solution)/shard_map/ppermute | solution.py:249
  16.0 1.4 %collective-permute-start.6 = (bf16[144,256]{1,0:T(8,128)(2,1)S(1)}, bf16[144,256]{1,0:T(8,128)(2,1)S(1)}, u32[]{:S(2)}, u32[]{:S(2)}) collective-permute-start(bf16[144,256]{1,0:T(8,128)(2,1)S(1)} %get-tuple-element.33), channel_id=1, source_target_pairs={{0,1},{1,0},{2,3},{3,2},{4,5},{5,4},{6,7},{7,6},{8,9},{9,8},{10,11... | collective-permute-start | bytes 221192 | tf_op jit(solution)/shard_map/ppermute | solution.py:249
  17.4 5.9 %collective-permute-start.9 = (bf16[144,256]{1,0:T(8,128)(2,1)S(1)}, bf16[144,256]{1,0:T(8,128)(2,1)S(1)}, u32[]{:S(2)}, u32[]{:S(2)}) collective-permute-start(bf16[144,256]{1,0:T(8,128)(2,1)S(1)} %get-tuple-element.36), channel_id=1, source_target_pairs={{0,4},{1,5},{2,6},{3,7},{4,0},{5,1},{6,2},{7,3},{8,12},{9,13},{10,... | collective-permute-start | bytes 221192 | tf_op jit(solution)/shard_map/ppermute | solution.py:249
  19.9 5.6 %collective-permute-start.8 = (bf16[144,256]{1,0:T(8,128)(2,1)S(1)}, bf16[144,256]{1,0:T(8,128)(2,1)S(1)}, u32[]{:S(2)}, u32[]{:S(2)}) collective-permute-start(bf16[144,256]{1,0:T(8,128)(2,1)S(1)} %get-tuple-element.36), channel_id=1, source_target_pairs={{0,6},{1,7},{2,4},{3,5},{4,2},{5,3},{6,0},{7,1},{8,14},{9,15},{10,... | collective-permute-start | bytes 221192 | tf_op jit(solution)/shard_map/ppermute | solution.py:249
  20.8 4.6 %collective-permute-start.7 = (bf16[144,256]{1,0:T(8,128)(2,1)S(1)}, bf16[144,256]{1,0:T(8,128)(2,1)S(1)}, u32[]{:S(2)}, u32[]{:S(2)}) collective-permute-start(bf16[144,256]{1,0:T(8,128)(2,1)S(1)} %get-tuple-element.36), channel_id=1, source_target_pairs={{0,2},{1,3},{2,0},{3,1},{4,6},{5,7},{6,4},{7,5},{8,10},{9,11},{10,... | collective-permute-start | bytes 221192 | tf_op jit(solution)/shard_map/ppermute | solution.py:249
  25.5 4.4 %collective-permute-start.11 = (bf16[144,256]{1,0:T(8,128)(2,1)S(1)}, bf16[144,256]{1,0:T(8,128)(2,1)S(1)}, u32[]{:S(2)}, u32[]{:S(2)}) collective-permute-start(bf16[144,256]{1,0:T(8,128)(2,1)S(1)} %get-tuple-element.39), channel_id=1, source_target_pairs={{0,64},{1,129},{2,66},{3,131},{4,68},{5,133},{6,70},{7,135},{64,0}... | collective-permute-start | bytes 221192 | tf_op jit(solution)/shard_map/ppermute | solution.py:258
  26.8 4.6 %collective-permute-start.10 = (bf16[144,256]{1,0:T(8,128)(2,1)S(1)}, bf16[144,256]{1,0:T(8,128)(2,1)S(1)}, u32[]{:S(2)}, u32[]{:S(2)}) collective-permute-start(bf16[144,256]{1,0:T(8,128)(2,1)S(1)} %get-tuple-element.39), channel_id=1, source_target_pairs={{0,64},{1,193},{2,66},{3,195},{4,68},{5,197},{6,70},{7,199},{64,0}... | collective-permute-start | bytes 221192 | tf_op jit(solution)/shard_map/ppermute | solution.py:258
  31.4 1.5 %collective-permute-start.12 = (bf16[144,256]{1,0:T(8,128)(2,1)S(1)}, bf16[144,256]{1,0:T(8,128)(2,1)S(1)}, u32[]{:S(2)}, u32[]{:S(2)}) collective-permute-start(bf16[144,256]{1,0:T(8,128)(2,1)S(1)} %get-tuple-element.42), channel_id=1, source_target_pairs={{0,1},{1,0},{2,3},{3,2},{4,5},{5,4},{6,7},{7,6},{8,9},{9,8},{10,11... | collective-permute-start | bytes 221192 | tf_op jit(solution)/shard_map/ppermute | solution.py:249

commit v9 on v8

--- a/solution.py
+++ b/solution.py
@@ -312,7 +312,7 @@
             join_kernel, [(vmem(), value) for value in (kept[0], kept[1], *got)], STATE, name
         )
     got = [
-        over_cores(kept[2], (1, 0), flips) for flips in ((3, 0), (2, 0))
+        over_cores(kept[2], own, flips) for own, flips in (((1, 0), (3, 0)), ((0, 2), (2, 0)))
     ]
     far = call(far_kernel, [(vmem(), value) for value in got], STATE, "join_far")
     columns = w_out.shape[1]

time: 54 us -> 53.2 us (0.985)
  blocking collectives: 19.2 us -> 18 us
  starting transfers between devices: 16.1 us -> 17 us
  waiting for transfers between devices: 12.4 us -> 11.8 us
    ppermute x8, starting transfers between devices: 8.57 us -> 9.95 us  [over(): lax.ppermute(value, 'req', [(i, i ^ req_flip) for i in range(req_count)])]
    all_to_all x1, blocking collectives: 19.2 us -> 18 us  [on_device(): pieces = lax.all_to_all(pieces, 'head', 0, 0, tiled=True)]
    ppermute x2, waiting for transfers between devices: 3.71 us -> 3.14 us  [over_cores(): return lax.ppermute(value, ('sec', 'req'), pairs)]
where the time goes in v9:
time: 53.2 us; the launch traced here: 52.4 us
  blocking collectives  18 us (34%)
  starting transfers between devices  17 us (32%)
  waiting for transfers between devices  11.8 us (22%)
  Pallas kernels  3.86 us (7%)
  local copies, waits for them, and re-layouts  0.91 us (2%)
  other arithmetic  0.64 us (1%)
    all_to_all x1, blocking collectives, on_device(): pieces = lax.all_to_all(pieces, 'head', 0, 0, tiled=True)  18 us
    ppermute x8, starting transfers between devices, over(): lax.ppermute(value, 'req', [(i, i ^ req_flip) for i in range(req_count)])  9.95 us
    ppermute x8, waiting for transfers between devices, over(): lax.ppermute(value, 'req', [(i, i ^ req_flip) for i in range(req_count)])  7.54 us
    ppermute x3, starting transfers between devices, over(): lax.ppermute(value, 'sec', [(i, i ^ sec_flip) for i in range(sec_count)])  5.37 us
    pallas_call x10, Pallas kernels, call(): pl.pallas_call(kernel, out_shape=outs, in_specs=[spec for spec, _ in ins]...  3.86 us
    ppermute x2, waiting for transfers between devices, over_cores(): return lax.ppermute(value, ('sec', 'req'), pairs)  3.14 us
    ppermute x2, starting transfers between devices, over_cores(): return lax.ppermute(value, ('sec', 'req'), pairs)  1.64 us
    ppermute x3, waiting for transfers between devices, over(): lax.ppermute(value, 'sec', [(i, i ^ sec_flip) for i in range(sec_count)])  1.11 us
  transfers between devices with their start and end apart: 13, of which 10 were waited for; matrix products, arithmetic and copies ran while one was open for 0% of the time, Pallas kernels for 5%

profile of v9, /device:TPU:2, one launch (start us, length us, event | category | flops | bytes accessed | tf_op | source)
XLA Modules:
  0.0 52.4 jit_solution(10689194876603773828)
XLA Ops:
  0.0 0.0 copy-start.1
  0.0 0.0 copy-start
  0.0 0.0 collective-permute-start
  0.0 0.0 copy-start.4
  0.0 0.8 %copy-done.4 = bf16[2,2048]{1,0:T(2,128)(2,1)S(1)} copy-done((bf16[2,2048]{1,0:T(2,128)(2,1)S(1)}, bf16[2,2048]{1,0:T(2,128)(2,1)}, u32[]{:S(2)}) %copy-start.4) | copy-done | bytes 8216
  0.9 0.1 place_mine.1.so_far_ref
  1.0 0.4 collective-permute-done.other_ref
  1.4 0.1 place_other.1
  1.5 0.0 copy-start.3
  1.5 0.0 copy-start.5
  1.6 0.0 copy-start.6
  1.6 0.0 copy-start.7
  1.6 0.0 copy-start.8
  1.6 1.7 %collective-permute-start.1 = (bf16[16,2048]{1,0:T(8,128)(2,1)S(1)}, bf16[16,2048]{1,0:T(8,128)(2,1)S(1)}, u32[]{:S(2)}, u32[]{:S(2)}) collective-permute-start(bf16[16,2048]{1,0:T(8,128)(2,1)S(1)} %place_other.1), channel_id=1, source_target_pairs={{0,2},{1,3},{2,0},{3,1},{4,6},{5,7},{6,4},{7,5},{8,10},{9,11},{10,... | collective-permute-start | bytes 196616 | tf_op jit(solution)/shard_map/ppermute | solution.py:249
  3.3 0.0 copy-done.1
  3.3 0.0 copy-done
  3.3 1.4 %new_kv.1 = (bf16[128,256]{1,0:T(8,128)(2,1)S(1)}, bf16[128,256]{1,0:T(8,128)(2,1)S(1)}, bf16[128,256]{1,0:T(8,128)(2,1)S(1)}, bf16[128,256]{1,0:T(8,128)(2,1)S(1)}) custom-call(bf16[512,4096]{1,0:T(8,128)(2,1)S(1)} %copy-done, bf16[4096,256]{1,0:T(8,128)(2,1)S(1)} %copy-done.1), custom_call_target="tpu_custom_call" | custom-call | flops 1073741824 | bytes 6291456 | tf_op jit(solution)/shard_map/new_kv/pallas_call | solution.py:223
  4.6 0.0 copy-start.2
  4.6 4.7 %collective-permute-start.3 = (bf16[128,256]{1,0:T(8,128)(2,1)S(1)}, bf16[128,256]{1,0:T(8,128)(2,1)S(1)}, u32[]{:S(2)}, u32[]{:S(2)}) collective-permute-start(bf16[128,256]{1,0:T(8,128)(2,1)S(1)} %get-tuple-element.26), channel_id=1, source_target_pairs={{0,192},{64,128},{128,64},{192,0},{1,193},{65,129},{129,65},{193,1... | collective-permute-start | bytes 196616 | tf_op jit(solution)/shard_map/ppermute | solution.py:247
  9.3 0.0 collective-permute-start.4
  9.4 0.7 %collective-permute-start.5 = (bf16[128,256]{1,0:T(8,128)(2,1)S(1)}, bf16[128,256]{1,0:T(8,128)(2,1)S(1)}, u32[]{:S(2)}, u32[]{:S(2)}) collective-permute-start(bf16[128,256]{1,0:T(8,128)(2,1)S(1)} %get-tuple-element.28), channel_id=1, source_target_pairs={{0,64},{64,0},{128,192},{192,128},{1,65},{65,1},{129,193},{193,129... | collective-permute-start | bytes 196616 | tf_op jit(solution)/shard_map/ppermute | solution.py:247
  10.0 0.0 collective-permute-done.1
  10.0 2.7 %collective-permute-start.2 = (bf16[16,2048]{1,0:T(8,128)(2,1)S(1)}, bf16[16,2048]{1,0:T(8,128)(2,1)S(1)}, u32[]{:S(2)}, u32[]{:S(2)}) collective-permute-start(bf16[16,2048]{1,0:T(8,128)(2,1)S(1)} %add.6), channel_id=1, source_target_pairs={{0,6},{1,7},{2,4},{3,5},{4,2},{5,3},{6,0},{7,1},{8,14},{9,15},{10,... | collective-permute-start | bytes 196616 | tf_op jit(solution)/shard_map/ppermute | solution.py:249
  12.7 0.0 copy-done.3
  12.7 0.0 copy-done.5
  12.7 0.0 copy-done.6
  12.7 0.0 copy-done.7
  12.7 0.0 copy-done.8
  12.7 1.2 %cached.1 = (f32[128,256]{1,0:T(8,128)S(1)}, f32[8,256]{1,0:T(8,128)S(1)}, f32[128,256]{1,0:T(8,128)S(1)}) custom-call(s32[1,256]{1,0:T(1,128)S(1)} %bitcast.6, s32[1,256]{1,0:T(1,128)S(1)} %bitcast.7, s32[1,256]{1,0:T(1,128)S(1)} %bitcast.8, s32[1,2]{1,0:T(1,128)S(1)} %bitcast.9, bf16[2,2048]{1,0:T(2,128)(2,1)S(1)} %copy-done.4, ...), custom_call_target="tpu_custom_call" | custom-call | flops 268435456 | bytes 1059848 | tf_op jit(solution)/shard_map/cached/pallas_call | solution.py:223
  13.9 0.0 collective-permute-done.3.a_ref
  13.9 0.8 %collective-permute-done.4.b_ref = bf16[128,256]{1,0:T(8,128)(2,1)S(1)} collective-permute-done((bf16[128,256]{1,0:T(8,128)(2,1)S(1)}, bf16[128,256]{1,0:T(8,128)(2,1)S(1)}, u32[]{:S(2)}, u32[]{:S(2)}) %collective-permute-start.4) | collective-permute-done | bytes 65568 | tf_op jit(solution)/shard_map/ppermute | solution.py:247
  14.7 0.4 collective-permute-done.5.c_ref
  15.1 0.5 %collective-permute-done.2 = bf16[16,2048]{1,0:T(8,128)(2,1)S(1)} collective-permute-done((bf16[16,2048]{1,0:T(8,128)(2,1)S(1)}, bf16[16,2048]{1,0:T(8,128)(2,1)S(1)}, u32[]{:S(2)}, u32[]{:S(2)}) %collective-permute-start.2) | collective-permute-done | bytes 65568 | tf_op jit(solution)/shard_map/ppermute | solution.py:249
  15.6 0.4 prompt.1
  16.0 0.1 collective-permute-start.6
  16.1 1.3 %collective-permute-done.6.refs_0_ = bf16[144,256]{1,0:T(8,128)(2,1)S(1)} collective-permute-done((bf16[144,256]{1,0:T(8,128)(2,1)S(1)}, bf16[144,256]{1,0:T(8,128)(2,1)S(1)}, u32[]{:S(2)}, u32[]{:S(2)}) %collective-permute-start.6) | collective-permute-done | bytes 73760 | tf_op jit(solution)/shard_map/ppermute | solution.py:249
  17.4 0.1 join_core.1
  17.4 2.5 %collective-permute-start.9 = (bf16[144,256]{1,0:T(8,128)(2,1)S(1)}, bf16[144,256]{1,0:T(8,128)(2,1)S(1)}, u32[]{:S(2)}, u32[]{:S(2)}) collective-permute-start(bf16[144,256]{1,0:T(8,128)(2,1)S(1)} %get-tuple-element.36), channel_id=1, source_target_pairs={{0,4},{1,5},{2,6},{3,7},{4,0},{5,1},{6,2},{7,3},{8,12},{9,13},{10,... | collective-permute-start | bytes 221192 | tf_op jit(solution)/shard_map/ppermute | solution.py:249
  19.9 0.9 %collective-permute-start.8 = (bf16[144,256]{1,0:T(8,128)(2,1)S(1)}, bf16[144,256]{1,0:T(8,128)(2,1)S(1)}, u32[]{:S(2)}, u32[]{:S(2)}) collective-permute-start(bf16[144,256]{1,0:T(8,128)(2,1)S(1)} %get-tuple-element.36), channel_id=1, source_target_pairs={{0,6},{1,7},{2,4},{3,5},{4,2},{5,3},{6,0},{7,1},{8,14},{9,15},{10,... | collective-permute-start | bytes 221192 | tf_op jit(solution)/shard_map/ppermute | solution.py:249
  20.8 0.2 collective-permute-start.7
  21.0 2.4 %collective-permute-done.9.refs_2_ = bf16[144,256]{1,0:T(8,128)(2,1)S(1)} collective-permute-done((bf16[144,256]{1,0:T(8,128)(2,1)S(1)}, bf16[144,256]{1,0:T(8,128)(2,1)S(1)}, u32[]{:S(2)}, u32[]{:S(2)}) %collective-permute-start.9) | collective-permute-done | bytes 73760 | tf_op jit(solution)/shard_map/ppermute | solution.py:249
  23.4 2.1 %collective-permute-done.8.refs_1_ = bf16[144,256]{1,0:T(8,128)(2,1)S(1)} collective-permute-done((bf16[144,256]{1,0:T(8,128)(2,1)S(1)}, bf16[144,256]{1,0:T(8,128)(2,1)S(1)}, u32[]{:S(2)}, u32[]{:S(2)}) %collective-permute-start.8) | collective-permute-done | bytes 73760 | tf_op jit(solution)/shard_map/ppermute | solution.py:249
  25.4 0.0 collective-permute-done.7.refs_0_
  25.4 0.1 join_near.1
  25.5 0.4 collective-permute-start.11
  26.0 1.2 %collective-permute-start.10 = (bf16[144,256]{1,0:T(8,128)(2,1)S(1)}, bf16[144,256]{1,0:T(8,128)(2,1)S(1)}, u32[]{:S(2)}, u32[]{:S(2)}) collective-permute-start(bf16[144,256]{1,0:T(8,128)(2,1)S(1)} %get-tuple-element.39), channel_id=1, source_target_pairs={{0,64},{1,193},{2,66},{3,195},{4,68},{5,197},{6,70},{7,199},{64,0}... | collective-permute-start | bytes 221192 | tf_op jit(solution)/shard_map/ppermute | solution.py:258
  27.2 2.8 %collective-permute-done.11.second_ref = bf16[144,256]{1,0:T(8,128)(2,1)S(1)} collective-permute-done((bf16[144,256]{1,0:T(8,128)(2,1)S(1)}, bf16[144,256]{1,0:T(8,128)(2,1)S(1)}, u32[]{:S(2)}, u32[]{:S(2)}) %collective-permute-start.11) | collective-permute-done | bytes 73760 | tf_op jit(solution)/shard_map/ppermute | solution.py:258
  30.0 0.3 collective-permute-done.10.first_ref
  30.4 2.0 %collective-permute-start.12 = (bf16[144,256]{1,0:T(8,128)(2,1)S(1)}, bf16[144,256]{1,0:T(8,128)(2,1)S(1)}, u32[]{:S(2)}, u32[]{:S(2)}) collective-permute-start(bf16[144,256]{1,0:T(8,128)(2,1)S(1)} %get-tuple-element.42), channel_id=1, source_target_pairs={{0,1},{1,0},{2,3},{3,2},{4,5},{5,4},{6,7},{7,6},{8,9},{9,8},{10,11... | collective-permute-start | bytes 221192 | tf_op jit(solution)/shard_map/ppermute | solution.py:249
  32.3 0.9 %collective-permute-done.12.got_ref = bf16[144,256]{1,0:T(8,128)(2,1)S(1)} collective-permute-done((bf16[144,256]{1,0:T(8,128)(2,1)S(1)}, bf16[144,256]{1,0:T(8,128)(2,1)S(1)}, u32[]{:S(2)}, u32[]{:S(2)}) %collective-permute-start.12) | collective-permute-done | bytes 73760 | tf_op jit(solution)/shard_map/ppermute | solution.py:249
  33.2 0.0 copy-done.2
  33.2 0.5 project.1
  33.7 18.0 %all_to_all.5 = bf16[8,2,512]{2,1,0:T(2,128)(2,1)S(1)} all-to-all(bf16[8,2,512]{2,1,0:T(2,128)(2,1)S(1)} %reshape.19), channel_id=1, replica_groups=mesh['sec'=4,'head'=8,'req'=8] {'head'}, dimensions={0} | all-to-all | bytes 32768 | tf_op jit(solution)/shard_map/all_to_all | solution.py:331
  51.8 0.6 %reduce_sum.12 = bf16[2,512]{1,0:T(2,128)(2,1)} reduce(bf16[8,2,512]{2,1,0:T(2,128)(2,1)S(1)} %all_to_all.5, bf16[]{:T(256)} %constant.2.clone.1), dimensions={0}, to_apply=%region_0.0 | reduce | flops 7168 | bytes 18434 | tf_op jit(solution)/shard_map/reduce_sum | solution.py:332
  (5 shorter events, 0.1 us)
Async XLA Ops:
  0.0 3.3 %copy-start.1 = (bf16[4096,256]{1,0:T(8,128)(2,1)S(1)}, bf16[4096,256]{1,0:T(8,128)(2,1)}, u32[]{:S(2)}) copy-start(bf16[4096,256]{1,0:T(8,128)(2,1)} %w_ref.1) | copy-start | bytes 6291460
  0.0 3.3 %copy-start = (bf16[512,4096]{1,0:T(8,128)(2,1)S(1)}, bf16[512,4096]{1,0:T(8,128)(2,1)}, u32[]{:S(2)}) copy-start(bf16[512,4096]{1,0:T(8,128)(2,1)} %x_ref.1) | copy-start | bytes 12582916
  0.0 1.4 %collective-permute-start = (bf16[2,2048]{1,0:T(2,128)(2,1)}, bf16[2,2048]{1,0:T(2,128)(2,1)S(1)}, u32[]{:S(2)}, u32[]{:S(2)}) collective-permute-start(bf16[2,2048]{1,0:T(2,128)(2,1)} %q_ref.1), channel_id=1, source_target_pairs={{0,1},{1,0},{2,3},{3,2},{4,5},{5,4},{6,7},{7,6},{8,9},{9,8},{10,11... | collective-permute-start | bytes 24584 | tf_op jit(solution)/shard_map/ppermute | solution.py:249
  0.0 0.8 %copy-start.4 = (bf16[2,2048]{1,0:T(2,128)(2,1)S(1)}, bf16[2,2048]{1,0:T(2,128)(2,1)}, u32[]{:S(2)}) copy-start(bf16[2,2048]{1,0:T(2,128)(2,1)} %q_ref.1) | copy-start | bytes 24580
  1.5 11.2 %copy-start.3 = (bf16[2,1024,1,256]{3,1,2,0:T(8,128)(2,1)S(1)}, bf16[2,1024,1,256]{3,1,2,0:T(8,128)(2,1)}, u32[]{:S(2)}) copy-start(bf16[2,1024,1,256]{3,1,2,0:T(8,128)(2,1)} %param.12) | copy-start | bytes 3145732
  1.5 11.2 %copy-start.5 = (s32[256,1]{0,1:T(1,128)S(1)}, s32[256,1]{0,1:T(1,128)}, u32[]{:S(2)}) copy-start(s32[256,1]{0,1:T(1,128)} %param.14) | copy-start | bytes 3076
  1.6 11.2 %copy-start.6 = (s32[256]{0:T(256)S(1)}, s32[256]{0:T(256)}, u32[]{:S(2)}) copy-start(s32[256]{0:T(256)} %param.15) | copy-start | bytes 3076
  1.6 11.1 %copy-start.7 = (s32[256]{0:T(256)S(1)}, s32[256]{0:T(256)}, u32[]{:S(2)}) copy-start(s32[256]{0:T(256)} %param.16) | copy-start | bytes 3076
  1.6 11.1 %copy-start.8 = (s32[2]{0:T(128)S(1)}, s32[2]{0:T(128)}, u32[]{:S(2)}) copy-start(s32[2]{0:T(128)} %param.17) | copy-start | bytes 28
  1.6 8.4 %collective-permute-start.1 = (bf16[16,2048]{1,0:T(8,128)(2,1)S(1)}, bf16[16,2048]{1,0:T(8,128)(2,1)S(1)}, u32[]{:S(2)}, u32[]{:S(2)}) collective-permute-start(bf16[16,2048]{1,0:T(8,128)(2,1)S(1)} %place_other.1), channel_id=1, source_target_pairs={{0,2},{1,3},{2,0},{3,1},{4,6},{5,7},{6,4},{7,5},{8,10},{9,11},{10,... | collective-permute-start | bytes 196616 | tf_op jit(solution)/shard_map/ppermute | solution.py:249
  4.6 28.6 %copy-start.2 = (bf16[2048,512]{1,0:T(8,128)(2,1)S(1)}, bf16[2048,512]{1,0:T(8,128)(2,1)}, u32[]{:S(2)}) copy-start(bf16[2048,512]{1,0:T(8,128)(2,1)} %out_w_ref.1) | copy-start | bytes 6291460
  4.6 9.3 %collective-permute-start.3 = (bf16[128,256]{1,0:T(8,128)(2,1)S(1)}, bf16[128,256]{1,0:T(8,128)(2,1)S(1)}, u32[]{:S(2)}, u32[]{:S(2)}) collective-permute-start(bf16[128,256]{1,0:T(8,128)(2,1)S(1)} %get-tuple-element.26), channel_id=1, source_target_pairs={{0,192},{64,128},{128,64},{192,0},{1,193},{65,129},{129,65},{193,1... | collective-permute-start | bytes 196616 | tf_op jit(solution)/shard_map/ppermute | solution.py:247
  9.3 5.3 %collective-permute-start.4 = (bf16[128,256]{1,0:T(8,128)(2,1)S(1)}, bf16[128,256]{1,0:T(8,128)(2,1)S(1)}, u32[]{:S(2)}, u32[]{:S(2)}) collective-permute-start(bf16[128,256]{1,0:T(8,128)(2,1)S(1)} %get-tuple-element.27), channel_id=1, source_target_pairs={{0,128},{64,192},{128,0},{192,64},{1,129},{65,193},{129,1},{193,65... | collective-permute-start | bytes 196616 | tf_op jit(solution)/shard_map/ppermute | solution.py:247
  9.4 5.7 %collective-permute-start.5 = (bf16[128,256]{1,0:T(8,128)(2,1)S(1)}, bf16[128,256]{1,0:T(8,128)(2,1)S(1)}, u32[]{:S(2)}, u32[]{:S(2)}) collective-permute-start(bf16[128,256]{1,0:T(8,128)(2,1)S(1)} %get-tuple-element.28), channel_id=1, source_target_pairs={{0,64},{64,0},{128,192},{192,128},{1,65},{65,1},{129,193},{193,129... | collective-permute-start | bytes 196616 | tf_op jit(solution)/shard_map/ppermute | solution.py:247
  10.0 5.6 %collective-permute-start.2 = (bf16[16,2048]{1,0:T(8,128)(2,1)S(1)}, bf16[16,2048]{1,0:T(8,128)(2,1)S(1)}, u32[]{:S(2)}, u32[]{:S(2)}) collective-permute-start(bf16[16,2048]{1,0:T(8,128)(2,1)S(1)} %add.6), channel_id=1, source_target_pairs={{0,6},{1,7},{2,4},{3,5},{4,2},{5,3},{6,0},{7,1},{8,14},{9,15},{10,... | collective-permute-start | bytes 196616 | tf_op jit(solution)/shard_map/ppermute | solution.py:249
  16.0 1.4 %collective-permute-start.6 = (bf16[144,256]{1,0:T(8,128)(2,1)S(1)}, bf16[144,256]{1,0:T(8,128)(2,1)S(1)}, u32[]{:S(2)}, u32[]{:S(2)}) collective-permute-start(bf16[144,256]{1,0:T(8,128)(2,1)S(1)} %get-tuple-element.33), channel_id=1, source_target_pairs={{0,1},{1,0},{2,3},{3,2},{4,5},{5,4},{6,7},{7,6},{8,9},{9,8},{10,11... | collective-permute-start | bytes 221192 | tf_op jit(solution)/shard_map/ppermute | solution.py:249
  17.4 5.9 %collective-permute-start.9 = (bf16[144,256]{1,0:T(8,128)(2,1)S(1)}, bf16[144,256]{1,0:T(8,128)(2,1)S(1)}, u32[]{:S(2)}, u32[]{:S(2)}) collective-permute-start(bf16[144,256]{1,0:T(8,128)(2,1)S(1)} %get-tuple-element.36), channel_id=1, source_target_pairs={{0,4},{1,5},{2,6},{3,7},{4,0},{5,1},{6,2},{7,3},{8,12},{9,13},{10,... | collective-permute-start | bytes 221192 | tf_op jit(solution)/shard_map/ppermute | solution.py:249
  19.9 5.6 %collective-permute-start.8 = (bf16[144,256]{1,0:T(8,128)(2,1)S(1)}, bf16[144,256]{1,0:T(8,128)(2,1)S(1)}, u32[]{:S(2)}, u32[]{:S(2)}) collective-permute-start(bf16[144,256]{1,0:T(8,128)(2,1)S(1)} %get-tuple-element.36), channel_id=1, source_target_pairs={{0,6},{1,7},{2,4},{3,5},{4,2},{5,3},{6,0},{7,1},{8,14},{9,15},{10,... | collective-permute-start | bytes 221192 | tf_op jit(solution)/shard_map/ppermute | solution.py:249
  20.8 4.6 %collective-permute-start.7 = (bf16[144,256]{1,0:T(8,128)(2,1)S(1)}, bf16[144,256]{1,0:T(8,128)(2,1)S(1)}, u32[]{:S(2)}, u32[]{:S(2)}) collective-permute-start(bf16[144,256]{1,0:T(8,128)(2,1)S(1)} %get-tuple-element.36), channel_id=1, source_target_pairs={{0,2},{1,3},{2,0},{3,1},{4,6},{5,7},{6,4},{7,5},{8,10},{9,11},{10,... | collective-permute-start | bytes 221192 | tf_op jit(solution)/shard_map/ppermute | solution.py:249
  25.5 4.4 %collective-permute-start.11 = (bf16[144,256]{1,0:T(8,128)(2,1)S(1)}, bf16[144,256]{1,0:T(8,128)(2,1)S(1)}, u32[]{:S(2)}, u32[]{:S(2)}) collective-permute-start(bf16[144,256]{1,0:T(8,128)(2,1)S(1)} %get-tuple-element.39), channel_id=1, source_target_pairs={{0,2},{1,129},{2,0},{3,131},{4,6},{5,133},{6,4},{7,135},{64,66},{6... | collective-permute-start | bytes 221192 | tf_op jit(solution)/shard_map/ppermute | solution.py:258
  26.0 4.4 %collective-permute-start.10 = (bf16[144,256]{1,0:T(8,128)(2,1)S(1)}, bf16[144,256]{1,0:T(8,128)(2,1)S(1)}, u32[]{:S(2)}, u32[]{:S(2)}) collective-permute-start(bf16[144,256]{1,0:T(8,128)(2,1)S(1)} %get-tuple-element.39), channel_id=1, source_target_pairs={{0,64},{1,193},{2,66},{3,195},{4,68},{5,197},{6,70},{7,199},{64,0}... | collective-permute-start | bytes 221192 | tf_op jit(solution)/shard_map/ppermute | solution.py:258
  30.4 2.9 %collective-permute-start.12 = (bf16[144,256]{1,0:T(8,128)(2,1)S(1)}, bf16[144,256]{1,0:T(8,128)(2,1)S(1)}, u32[]{:S(2)}, u32[]{:S(2)}) collective-permute-start(bf16[144,256]{1,0:T(8,128)(2,1)S(1)} %get-tuple-element.42), channel_id=1, source_target_pairs={{0,1},{1,0},{2,3},{3,2},{4,5},{5,4},{6,7},{7,6},{8,9},{9,8},{10,11... | collective-permute-start | bytes 221192 | tf_op jit(solution)/shard_map/ppermute | solution.py:249

commit v10 on v9

--- a/solution.py
+++ b/solution.py
@@ -274,7 +274,7 @@
         "new_kv",
         flops=2 * prompt_x.size * width,
     )
-    arrived = [over(chunks[flip], flip, 0) for flip in (3, 2, 1)]
+    arrived = [over(chunks[flip], flip, 0) for flip in (3, 1, 2)]
     gathered = gathered + over(gathered, 0, 6)
     cached_weighted, cached_stats, live = call(
         cached_kernel,

time: 53.2 us -> 53.1 us (level)
  no operation moved by 1% of the time
where the time goes in v10:
time: 53.1 us; the launch traced here: 52.2 us
  blocking collectives  18.2 us (34%)
  starting transfers between devices  16.7 us (31%)
  waiting for transfers between devices  11.7 us (22%)
  Pallas kernels  3.86 us (7%)
  local copies, waits for them, and re-layouts  0.91 us (2%)
  other arithmetic  0.64 us (1%)
    all_to_all x1, blocking collectives, on_device(): pieces = lax.all_to_all(pieces, 'head', 0, 0, tiled=True)  18.2 us
    ppermute x8, starting transfers between devices, over(): lax.ppermute(value, 'req', [(i, i ^ req_flip) for i in range(req_count)])  9.52 us
    ppermute x8, waiting for transfers between devices, over(): lax.ppermute(value, 'req', [(i, i ^ req_flip) for i in range(req_count)])  7.53 us
    ppermute x3, starting transfers between devices, over(): lax.ppermute(value, 'sec', [(i, i ^ sec_flip) for i in range(sec_count)])  5.37 us
    pallas_call x10, Pallas kernels, call(): pl.pallas_call(kernel, out_shape=outs, in_specs=[spec for spec, _ in ins]...  3.86 us
    ppermute x2, waiting for transfers between devices, over_cores(): return lax.ppermute(value, ('sec', 'req'), pairs)  2.96 us
    ppermute x2, starting transfers between devices, over_cores(): return lax.ppermute(value, ('sec', 'req'), pairs)  1.82 us
    ppermute x3, waiting for transfers between devices, over(): lax.ppermute(value, 'sec', [(i, i ^ sec_flip) for i in range(sec_count)])  1.25 us
  transfers between devices with their start and end apart: 13, of which 10 were waited for; matrix products, arithmetic and copies ran while one was open for 0% of the time, Pallas kernels for 5%

profile of v10, /device:TPU:2, one launch (start us, length us, event | category | flops | bytes accessed | tf_op | source)
XLA Modules:
  0.0 52.2 jit_solution(10764023524915875720)
XLA Ops:
  0.0 0.0 copy-start.1
  0.0 0.0 copy-start
  0.0 0.0 collective-permute-start
  0.0 0.0 copy-start.4
  0.0 0.8 %copy-done.4 = bf16[2,2048]{1,0:T(2,128)(2,1)S(1)} copy-done((bf16[2,2048]{1,0:T(2,128)(2,1)S(1)}, bf16[2,2048]{1,0:T(2,128)(2,1)}, u32[]{:S(2)}) %copy-start.4) | copy-done | bytes 8216
  0.9 0.1 place_mine.1.so_far_ref
  1.0 0.4 collective-permute-done.other_ref
  1.4 0.1 place_other.1
  1.5 0.0 copy-start.3
  1.5 0.0 copy-start.5
  1.6 0.0 copy-start.6
  1.6 0.0 copy-start.7
  1.6 0.0 copy-start.8
  1.6 1.7 %collective-permute-start.1 = (bf16[16,2048]{1,0:T(8,128)(2,1)S(1)}, bf16[16,2048]{1,0:T(8,128)(2,1)S(1)}, u32[]{:S(2)}, u32[]{:S(2)}) collective-permute-start(bf16[16,2048]{1,0:T(8,128)(2,1)S(1)} %place_other.1), channel_id=1, source_target_pairs={{0,2},{1,3},{2,0},{3,1},{4,6},{5,7},{6,4},{7,5},{8,10},{9,11},{10,... | collective-permute-start | bytes 196616 | tf_op jit(solution)/shard_map/ppermute | solution.py:249
  3.3 0.0 copy-done.1
  3.3 0.0 copy-done
  3.3 1.4 %new_kv.1 = (bf16[128,256]{1,0:T(8,128)(2,1)S(1)}, bf16[128,256]{1,0:T(8,128)(2,1)S(1)}, bf16[128,256]{1,0:T(8,128)(2,1)S(1)}, bf16[128,256]{1,0:T(8,128)(2,1)S(1)}) custom-call(bf16[512,4096]{1,0:T(8,128)(2,1)S(1)} %copy-done, bf16[4096,256]{1,0:T(8,128)(2,1)S(1)} %copy-done.1), custom_call_target="tpu_custom_call" | custom-call | flops 1073741824 | bytes 6291456 | tf_op jit(solution)/shard_map/new_kv/pallas_call | solution.py:223
  4.6 0.0 copy-start.2
  4.6 4.7 %collective-permute-start.3 = (bf16[128,256]{1,0:T(8,128)(2,1)S(1)}, bf16[128,256]{1,0:T(8,128)(2,1)S(1)}, u32[]{:S(2)}, u32[]{:S(2)}) collective-permute-start(bf16[128,256]{1,0:T(8,128)(2,1)S(1)} %get-tuple-element.26), channel_id=1, source_target_pairs={{0,192},{64,128},{128,64},{192,0},{1,193},{65,129},{129,65},{193,1... | collective-permute-start | bytes 196616 | tf_op jit(solution)/shard_map/ppermute | solution.py:247
  9.3 0.0 collective-permute-start.4
  9.4 0.7 %collective-permute-start.5 = (bf16[128,256]{1,0:T(8,128)(2,1)S(1)}, bf16[128,256]{1,0:T(8,128)(2,1)S(1)}, u32[]{:S(2)}, u32[]{:S(2)}) collective-permute-start(bf16[128,256]{1,0:T(8,128)(2,1)S(1)} %get-tuple-element.28), channel_id=1, source_target_pairs={{0,128},{64,192},{128,0},{192,64},{1,129},{65,193},{129,1},{193,65... | collective-permute-start | bytes 196616 | tf_op jit(solution)/shard_map/ppermute | solution.py:247
  10.0 0.0 collective-permute-done.1
  10.0 2.7 %collective-permute-start.2 = (bf16[16,2048]{1,0:T(8,128)(2,1)S(1)}, bf16[16,2048]{1,0:T(8,128)(2,1)S(1)}, u32[]{:S(2)}, u32[]{:S(2)}) collective-permute-start(bf16[16,2048]{1,0:T(8,128)(2,1)S(1)} %add.6), channel_id=1, source_target_pairs={{0,6},{1,7},{2,4},{3,5},{4,2},{5,3},{6,0},{7,1},{8,14},{9,15},{10,... | collective-permute-start | bytes 196616 | tf_op jit(solution)/shard_map/ppermute | solution.py:249
  12.7 0.0 copy-done.3
  12.7 0.0 copy-done.5
  12.7 0.0 copy-done.6
  12.7 0.0 copy-done.7
  12.7 0.0 copy-done.8
  12.7 1.2 %cached.1 = (f32[128,256]{1,0:T(8,128)S(1)}, f32[8,256]{1,0:T(8,128)S(1)}, f32[128,256]{1,0:T(8,128)S(1)}) custom-call(s32[1,256]{1,0:T(1,128)S(1)} %bitcast.6, s32[1,256]{1,0:T(1,128)S(1)} %bitcast.7, s32[1,256]{1,0:T(1,128)S(1)} %bitcast.8, s32[1,2]{1,0:T(1,128)S(1)} %bitcast.9, bf16[2,2048]{1,0:T(2,128)(2,1)S(1)} %copy-done.4, ...), custom_call_target="tpu_custom_call" | custom-call | flops 268435456 | bytes 1059848 | tf_op jit(solution)/shard_map/cached/pallas_call | solution.py:223
  13.9 0.0 collective-permute-done.3.a_ref
  13.9 0.2 collective-permute-done.4.b_ref
  14.1 1.1 %collective-permute-done.5.c_ref = bf16[128,256]{1,0:T(8,128)(2,1)S(1)} collective-permute-done((bf16[128,256]{1,0:T(8,128)(2,1)S(1)}, bf16[128,256]{1,0:T(8,128)(2,1)S(1)}, u32[]{:S(2)}, u32[]{:S(2)}) %collective-permute-start.5) | collective-permute-done | bytes 65568 | tf_op jit(solution)/shard_map/ppermute | solution.py:247
  15.2 0.4 collective-permute-done.2
  15.6 0.4 prompt.1
  16.0 0.1 collective-permute-start.6
  16.1 1.3 %collective-permute-done.6.refs_0_ = bf16[144,256]{1,0:T(8,128)(2,1)S(1)} collective-permute-done((bf16[144,256]{1,0:T(8,128)(2,1)S(1)}, bf16[144,256]{1,0:T(8,128)(2,1)S(1)}, u32[]{:S(2)}, u32[]{:S(2)}) %collective-permute-start.6) | collective-permute-done | bytes 73760 | tf_op jit(solution)/shard_map/ppermute | solution.py:249
  17.4 0.1 join_core.1
  17.4 2.6 %collective-permute-start.9 = (bf16[144,256]{1,0:T(8,128)(2,1)S(1)}, bf16[144,256]{1,0:T(8,128)(2,1)S(1)}, u32[]{:S(2)}, u32[]{:S(2)}) collective-permute-start(bf16[144,256]{1,0:T(8,128)(2,1)S(1)} %get-tuple-element.36), channel_id=1, source_target_pairs={{0,4},{1,5},{2,6},{3,7},{4,0},{5,1},{6,2},{7,3},{8,12},{9,13},{10,... | collective-permute-start | bytes 221192 | tf_op jit(solution)/shard_map/ppermute | solution.py:249
  20.0 0.8 %collective-permute-start.8 = (bf16[144,256]{1,0:T(8,128)(2,1)S(1)}, bf16[144,256]{1,0:T(8,128)(2,1)S(1)}, u32[]{:S(2)}, u32[]{:S(2)}) collective-permute-start(bf16[144,256]{1,0:T(8,128)(2,1)S(1)} %get-tuple-element.36), channel_id=1, source_target_pairs={{0,6},{1,7},{2,4},{3,5},{4,2},{5,3},{6,0},{7,1},{8,14},{9,15},{10,... | collective-permute-start | bytes 221192 | tf_op jit(solution)/shard_map/ppermute | solution.py:249
  20.8 0.2 collective-permute-start.7
  21.0 2.4 %collective-permute-done.9.refs_2_ = bf16[144,256]{1,0:T(8,128)(2,1)S(1)} collective-permute-done((bf16[144,256]{1,0:T(8,128)(2,1)S(1)}, bf16[144,256]{1,0:T(8,128)(2,1)S(1)}, u32[]{:S(2)}, u32[]{:S(2)}) %collective-permute-start.9) | collective-permute-done | bytes 73760 | tf_op jit(solution)/shard_map/ppermute | solution.py:249
  23.4 2.2 %collective-permute-done.8.refs_1_ = bf16[144,256]{1,0:T(8,128)(2,1)S(1)} collective-permute-done((bf16[144,256]{1,0:T(8,128)(2,1)S(1)}, bf16[144,256]{1,0:T(8,128)(2,1)S(1)}, u32[]{:S(2)}, u32[]{:S(2)}) %collective-permute-start.8) | collective-permute-done | bytes 73760 | tf_op jit(solution)/shard_map/ppermute | solution.py:249
  25.6 0.0 collective-permute-done.7.refs_0_
  25.6 0.1 join_near.1
  25.7 0.4 collective-permute-start.11
  26.1 1.4 %collective-permute-start.10 = (bf16[144,256]{1,0:T(8,128)(2,1)S(1)}, bf16[144,256]{1,0:T(8,128)(2,1)S(1)}, u32[]{:S(2)}, u32[]{:S(2)}) collective-permute-start(bf16[144,256]{1,0:T(8,128)(2,1)S(1)} %get-tuple-element.39), channel_id=1, source_target_pairs={{0,64},{1,193},{2,66},{3,195},{4,68},{5,197},{6,70},{7,199},{64,0}... | collective-permute-start | bytes 221192 | tf_op jit(solution)/shard_map/ppermute | solution.py:258
  27.5 2.6 %collective-permute-done.11.second_ref = bf16[144,256]{1,0:T(8,128)(2,1)S(1)} collective-permute-done((bf16[144,256]{1,0:T(8,128)(2,1)S(1)}, bf16[144,256]{1,0:T(8,128)(2,1)S(1)}, u32[]{:S(2)}, u32[]{:S(2)}) %collective-permute-start.11) | collective-permute-done | bytes 73760 | tf_op jit(solution)/shard_map/ppermute | solution.py:258
  30.1 0.3 collective-permute-done.10.first_ref
  30.5 1.5 %collective-permute-start.12 = (bf16[144,256]{1,0:T(8,128)(2,1)S(1)}, bf16[144,256]{1,0:T(8,128)(2,1)S(1)}, u32[]{:S(2)}, u32[]{:S(2)}) collective-permute-start(bf16[144,256]{1,0:T(8,128)(2,1)S(1)} %get-tuple-element.42), channel_id=1, source_target_pairs={{0,1},{1,0},{2,3},{3,2},{4,5},{5,4},{6,7},{7,6},{8,9},{9,8},{10,11... | collective-permute-start | bytes 221192 | tf_op jit(solution)/shard_map/ppermute | solution.py:249
  32.0 0.9 %collective-permute-done.12.got_ref = bf16[144,256]{1,0:T(8,128)(2,1)S(1)} collective-permute-done((bf16[144,256]{1,0:T(8,128)(2,1)S(1)}, bf16[144,256]{1,0:T(8,128)(2,1)S(1)}, u32[]{:S(2)}, u32[]{:S(2)}) %collective-permute-start.12) | collective-permute-done | bytes 73760 | tf_op jit(solution)/shard_map/ppermute | solution.py:249
  32.9 0.0 copy-done.2
  32.9 0.5 project.1
  33.4 18.2 %all_to_all.5 = bf16[8,2,512]{2,1,0:T(2,128)(2,1)S(1)} all-to-all(bf16[8,2,512]{2,1,0:T(2,128)(2,1)S(1)} %reshape.19), channel_id=1, replica_groups=mesh['sec'=4,'head'=8,'req'=8] {'head'}, dimensions={0} | all-to-all | bytes 32768 | tf_op jit(solution)/shard_map/all_to_all | solution.py:331
  51.6 0.6 %reduce_sum.12 = bf16[2,512]{1,0:T(2,128)(2,1)} reduce(bf16[8,2,512]{2,1,0:T(2,128)(2,1)S(1)} %all_to_all.5, bf16[]{:T(256)} %constant.2.clone.1), dimensions={0}, to_apply=%region_0.0 | reduce | flops 7168 | bytes 18434 | tf_op jit(solution)/shard_map/reduce_sum | solution.py:332
  (5 shorter events, 0.1 us)
Async XLA Ops:
  0.0 3.3 %copy-start.1 = (bf16[4096,256]{1,0:T(8,128)(2,1)S(1)}, bf16[4096,256]{1,0:T(8,128)(2,1)}, u32[]{:S(2)}) copy-start(bf16[4096,256]{1,0:T(8,128)(2,1)} %w_ref.1) | copy-start | bytes 6291460
  0.0 3.3 %copy-start = (bf16[512,4096]{1,0:T(8,128)(2,1)S(1)}, bf16[512,4096]{1,0:T(8,128)(2,1)}, u32[]{:S(2)}) copy-start(bf16[512,4096]{1,0:T(8,128)(2,1)} %x_ref.1) | copy-start | bytes 12582916
  0.0 1.4 %collective-permute-start = (bf16[2,2048]{1,0:T(2,128)(2,1)}, bf16[2,2048]{1,0:T(2,128)(2,1)S(1)}, u32[]{:S(2)}, u32[]{:S(2)}) collective-permute-start(bf16[2,2048]{1,0:T(2,128)(2,1)} %q_ref.1), channel_id=1, source_target_pairs={{0,1},{1,0},{2,3},{3,2},{4,5},{5,4},{6,7},{7,6},{8,9},{9,8},{10,11... | collective-permute-start | bytes 24584 | tf_op jit(solution)/shard_map/ppermute | solution.py:249
  0.0 0.8 %copy-start.4 = (bf16[2,2048]{1,0:T(2,128)(2,1)S(1)}, bf16[2,2048]{1,0:T(2,128)(2,1)}, u32[]{:S(2)}) copy-start(bf16[2,2048]{1,0:T(2,128)(2,1)} %q_ref.1) | copy-start | bytes 24580
  1.5 11.2 %copy-start.3 = (bf16[2,1024,1,256]{3,1,2,0:T(8,128)(2,1)S(1)}, bf16[2,1024,1,256]{3,1,2,0:T(8,128)(2,1)}, u32[]{:S(2)}) copy-start(bf16[2,1024,1,256]{3,1,2,0:T(8,128)(2,1)} %param.12) | copy-start | bytes 3145732
  1.5 11.2 %copy-start.5 = (s32[256,1]{0,1:T(1,128)S(1)}, s32[256,1]{0,1:T(1,128)}, u32[]{:S(2)}) copy-start(s32[256,1]{0,1:T(1,128)} %param.14) | copy-start | bytes 3076
  1.6 11.2 %copy-start.6 = (s32[256]{0:T(256)S(1)}, s32[256]{0:T(256)}, u32[]{:S(2)}) copy-start(s32[256]{0:T(256)} %param.15) | copy-start | bytes 3076
  1.6 11.1 %copy-start.7 = (s32[256]{0:T(256)S(1)}, s32[256]{0:T(256)}, u32[]{:S(2)}) copy-start(s32[256]{0:T(256)} %param.16) | copy-start | bytes 3076
  1.6 11.1 %copy-start.8 = (s32[2]{0:T(128)S(1)}, s32[2]{0:T(128)}, u32[]{:S(2)}) copy-start(s32[2]{0:T(128)} %param.17) | copy-start | bytes 28
  1.6 8.4 %collective-permute-start.1 = (bf16[16,2048]{1,0:T(8,128)(2,1)S(1)}, bf16[16,2048]{1,0:T(8,128)(2,1)S(1)}, u32[]{:S(2)}, u32[]{:S(2)}) collective-permute-start(bf16[16,2048]{1,0:T(8,128)(2,1)S(1)} %place_other.1), channel_id=1, source_target_pairs={{0,2},{1,3},{2,0},{3,1},{4,6},{5,7},{6,4},{7,5},{8,10},{9,11},{10,... | collective-permute-start | bytes 196616 | tf_op jit(solution)/shard_map/ppermute | solution.py:249
  4.6 28.3 %copy-start.2 = (bf16[2048,512]{1,0:T(8,128)(2,1)S(1)}, bf16[2048,512]{1,0:T(8,128)(2,1)}, u32[]{:S(2)}) copy-start(bf16[2048,512]{1,0:T(8,128)(2,1)} %out_w_ref.1) | copy-start | bytes 6291460
  4.6 9.3 %collective-permute-start.3 = (bf16[128,256]{1,0:T(8,128)(2,1)S(1)}, bf16[128,256]{1,0:T(8,128)(2,1)S(1)}, u32[]{:S(2)}, u32[]{:S(2)}) collective-permute-start(bf16[128,256]{1,0:T(8,128)(2,1)S(1)} %get-tuple-element.26), channel_id=1, source_target_pairs={{0,192},{64,128},{128,64},{192,0},{1,193},{65,129},{129,65},{193,1... | collective-permute-start | bytes 196616 | tf_op jit(solution)/shard_map/ppermute | solution.py:247
  9.3 4.7 %collective-permute-start.4 = (bf16[128,256]{1,0:T(8,128)(2,1)S(1)}, bf16[128,256]{1,0:T(8,128)(2,1)S(1)}, u32[]{:S(2)}, u32[]{:S(2)}) collective-permute-start(bf16[128,256]{1,0:T(8,128)(2,1)S(1)} %get-tuple-element.27), channel_id=1, source_target_pairs={{0,64},{64,0},{128,192},{192,128},{1,65},{65,1},{129,193},{193,129... | collective-permute-start | bytes 196616 | tf_op jit(solution)/shard_map/ppermute | solution.py:247
  9.4 5.8 %collective-permute-start.5 = (bf16[128,256]{1,0:T(8,128)(2,1)S(1)}, bf16[128,256]{1,0:T(8,128)(2,1)S(1)}, u32[]{:S(2)}, u32[]{:S(2)}) collective-permute-start(bf16[128,256]{1,0:T(8,128)(2,1)S(1)} %get-tuple-element.28), channel_id=1, source_target_pairs={{0,128},{64,192},{128,0},{192,64},{1,129},{65,193},{129,1},{193,65... | collective-permute-start | bytes 196616 | tf_op jit(solution)/shard_map/ppermute | solution.py:247
  10.0 5.6 %collective-permute-start.2 = (bf16[16,2048]{1,0:T(8,128)(2,1)S(1)}, bf16[16,2048]{1,0:T(8,128)(2,1)S(1)}, u32[]{:S(2)}, u32[]{:S(2)}) collective-permute-start(bf16[16,2048]{1,0:T(8,128)(2,1)S(1)} %add.6), channel_id=1, source_target_pairs={{0,6},{1,7},{2,4},{3,5},{4,2},{5,3},{6,0},{7,1},{8,14},{9,15},{10,... | collective-permute-start | bytes 196616 | tf_op jit(solution)/shard_map/ppermute | solution.py:249
  16.0 1.4 %collective-permute-start.6 = (bf16[144,256]{1,0:T(8,128)(2,1)S(1)}, bf16[144,256]{1,0:T(8,128)(2,1)S(1)}, u32[]{:S(2)}, u32[]{:S(2)}) collective-permute-start(bf16[144,256]{1,0:T(8,128)(2,1)S(1)} %get-tuple-element.33), channel_id=1, source_target_pairs={{0,1},{1,0},{2,3},{3,2},{4,5},{5,4},{6,7},{7,6},{8,9},{9,8},{10,11... | collective-permute-start | bytes 221192 | tf_op jit(solution)/shard_map/ppermute | solution.py:249
  17.4 5.9 %collective-permute-start.9 = (bf16[144,256]{1,0:T(8,128)(2,1)S(1)}, bf16[144,256]{1,0:T(8,128)(2,1)S(1)}, u32[]{:S(2)}, u32[]{:S(2)}) collective-permute-start(bf16[144,256]{1,0:T(8,128)(2,1)S(1)} %get-tuple-element.36), channel_id=1, source_target_pairs={{0,4},{1,5},{2,6},{3,7},{4,0},{5,1},{6,2},{7,3},{8,12},{9,13},{10,... | collective-permute-start | bytes 221192 | tf_op jit(solution)/shard_map/ppermute | solution.py:249
  20.0 5.6 %collective-permute-start.8 = (bf16[144,256]{1,0:T(8,128)(2,1)S(1)}, bf16[144,256]{1,0:T(8,128)(2,1)S(1)}, u32[]{:S(2)}, u32[]{:S(2)}) collective-permute-start(bf16[144,256]{1,0:T(8,128)(2,1)S(1)} %get-tuple-element.36), channel_id=1, source_target_pairs={{0,6},{1,7},{2,4},{3,5},{4,2},{5,3},{6,0},{7,1},{8,14},{9,15},{10,... | collective-permute-start | bytes 221192 | tf_op jit(solution)/shard_map/ppermute | solution.py:249
  20.8 4.8 %collective-permute-start.7 = (bf16[144,256]{1,0:T(8,128)(2,1)S(1)}, bf16[144,256]{1,0:T(8,128)(2,1)S(1)}, u32[]{:S(2)}, u32[]{:S(2)}) collective-permute-start(bf16[144,256]{1,0:T(8,128)(2,1)S(1)} %get-tuple-element.36), channel_id=1, source_target_pairs={{0,2},{1,3},{2,0},{3,1},{4,6},{5,7},{6,4},{7,5},{8,10},{9,11},{10,... | collective-permute-start | bytes 221192 | tf_op jit(solution)/shard_map/ppermute | solution.py:249
  25.7 4.4 %collective-permute-start.11 = (bf16[144,256]{1,0:T(8,128)(2,1)S(1)}, bf16[144,256]{1,0:T(8,128)(2,1)S(1)}, u32[]{:S(2)}, u32[]{:S(2)}) collective-permute-start(bf16[144,256]{1,0:T(8,128)(2,1)S(1)} %get-tuple-element.39), channel_id=1, source_target_pairs={{0,2},{1,129},{2,0},{3,131},{4,6},{5,133},{6,4},{7,135},{64,66},{6... | collective-permute-start | bytes 221192 | tf_op jit(solution)/shard_map/ppermute | solution.py:258
  26.1 4.4 %collective-permute-start.10 = (bf16[144,256]{1,0:T(8,128)(2,1)S(1)}, bf16[144,256]{1,0:T(8,128)(2,1)S(1)}, u32[]{:S(2)}, u32[]{:S(2)}) collective-permute-start(bf16[144,256]{1,0:T(8,128)(2,1)S(1)} %get-tuple-element.39), channel_id=1, source_target_pairs={{0,64},{1,193},{2,66},{3,195},{4,68},{5,197},{6,70},{7,199},{64,0}... | collective-permute-start | bytes 221192 | tf_op jit(solution)/shard_map/ppermute | solution.py:258
  30.5 2.4 %collective-permute-start.12 = (bf16[144,256]{1,0:T(8,128)(2,1)S(1)}, bf16[144,256]{1,0:T(8,128)(2,1)S(1)}, u32[]{:S(2)}, u32[]{:S(2)}) collective-permute-start(bf16[144,256]{1,0:T(8,128)(2,1)S(1)} %get-tuple-element.42), channel_id=1, source_target_pairs={{0,1},{1,0},{2,3},{3,2},{4,5},{5,4},{6,7},{7,6},{8,9},{9,8},{10,11... | collective-permute-start | bytes 221192 | tf_op jit(solution)/shard_map/ppermute | solution.py:249
